TPU v7x, 32 devices: a whole 2x2x4 slice. The times are simulated.
32 devices in a mesh: dp: 32 (over z, y, x, core).
Axes of the slice: x: 2, y: 2, z: 4, core: 2. Of those that a mesh axis runs over, the one named last changes fastest.
Arguments:
- tokens: bfloat16 [64, 320, 768], P('dp'), may hold values from -6 to 6
- lengths: int32 [64], P('dp'), may hold values from 157 to 314, as said below
- source: int32 [64], P('dp'), may hold values from 0 to 1, as said below
- cotangent: bfloat16 [64, 320, 768], P('dp'), may hold values from -6 to 6
- w_qkv: bfloat16 [768, 2304], P('dp'), may hold values from -0.21875 to 0.21875
- w_out: bfloat16 [768, 768], P(None, 'dp'), may hold values from -0.875 to 0.875
- w_up: bfloat16 [768, 3072], P('dp'), may hold values from -0.21875 to 0.21875
- w_down: bfloat16 [3072, 768], P(None, 'dp'), may hold values from -0.109375 to 0.109375
- gain_one: bfloat16 [768], P('dp'), may hold values from 0.25 to 1.75
- shift_one: bfloat16 [768], P('dp'), may hold values from -3 to 3
- bias_query: bfloat16 [768], P('dp'), may hold values from -2 to 2
- bias_value: bfloat16 [768], P('dp'), may hold values from -2 to 2
- bias_out: bfloat16 [768], P('dp'), may hold values from -2 to 2
- gain_two: bfloat16 [768], P('dp'), may hold values from 0.25 to 1.75
- shift_two: bfloat16 [768], P('dp'), may hold values from -3 to 3
- bias_up: bfloat16 [3072], P('dp'), may hold values from -2 to 2
- bias_down: bfloat16 [768], P('dp'), may hold values from -2 to 2
Outputs:
- mixed: bfloat16 [64, 320, 768], P('dp')
- grad_tokens: bfloat16 [64, 320, 768], P('dp')
- grad_qkv: float32 [768, 2304], P('dp')
- grad_out: float32 [768, 768], P(None, 'dp')
- grad_up: float32 [768, 3072], P('dp')
- grad_down: float32 [3072, 768], P(None, 'dp')
- grad_gain_one: float32 [768], P('dp')
- grad_shift_one: float32 [768], P('dp')
- grad_bias_query: float32 [768], P('dp')
- grad_bias_value: float32 [768], P('dp')
- grad_bias_out: float32 [768], P('dp')
- grad_gain_two: float32 [768], P('dp')
- grad_shift_two: float32 [768], P('dp')
- grad_bias_up: float32 [3072], P('dp')
- grad_bias_down: float32 [768], P('dp')
Inputs may be any that keep to these rules, and one draw needn't show every extreme that they name: `lengths`: visible tokens of a video sequence; some video sequence has exactly 314. Grouped by source: images come first, then videos, each a quarter of the sequences or more.
All inputs are finite; a program needn't handle non-finite values.
Results may differ from a plain program's by a relative error of at most 0.012.
Values may be sent and summed in bfloat16 or wider, within the bound.
No kernel may reach another device: no remote copies, remote signals or barrier semaphores. Data moves between devices by JAX's collectives and lax.ppermute only.
A program may use at most 192 MiB of HBM per device.

v0:
```python
import jax
import jax.numpy as jnp
from jax import lax
from jax.sharding import PartitionSpec as P

HEADS = 12
HEAD_DIM = 64
IMG_LEN = 196
MICRO = 2


epsilon = 1e-06


def layer_norm(values, gain_vec, shift_vec):
    center = values - jnp.mean(values, -1, keepdims=True)
    spread = jnp.mean(center * center, -1, keepdims=True)
    return center * lax.rsqrt(spread + epsilon) * gain_vec + shift_vec


def smooth_gate(values):
    return jax.nn.gelu(values, approximate=True)


def widen(vector):
    return vector.astype(jnp.float32)


def project(group_rows, matrix):
    return jnp.einsum("spd,de->spe", group_rows, matrix, preferred_element_type=jnp.float32)


def project_back(grad_rows, matrix):
    return jnp.einsum("spe,de->spd", grad_rows, matrix, preferred_element_type=jnp.float32)


def outer_sum(group_rows, grad_rows):
    return jnp.einsum("spd,spe->de", group_rows, grad_rows, preferred_element_type=jnp.float32)


def masked_scores(query_rows, key_rows, key_keep):
    scores = jnp.einsum(
        "sqhe,skhe->shqk", query_rows, key_rows, preferred_element_type=jnp.float32
    ) * HEAD_DIM ** (-0.5)
    return jnp.where(key_keep[:, None, None, :], scores, -1e30)


def attend_forward(query_rows, key_rows, value_rows, key_keep):
    masked = masked_scores(query_rows, key_rows, key_keep)
    top_score = jnp.max(masked, -1, keepdims=True)
    log_total = top_score + jnp.log(jnp.sum(jnp.exp(masked - top_score), -1, keepdims=True))
    soft_low = jnp.exp(masked - log_total).astype(jnp.bfloat16)
    mixed_rows = jnp.einsum(
        "shqk,skhe->sqhe", soft_low, value_rows, preferred_element_type=jnp.float32
    )
    return (mixed_rows, log_total)


def attend_backward(query_rows, key_rows, value_rows, key_keep, log_total, grad_mixed):
    masked = masked_scores(query_rows, key_rows, key_keep)
    soft_full = jnp.exp(masked - log_total)
    soft_low = soft_full.astype(jnp.bfloat16)
    grad_soft = jnp.einsum(
        "sqhe,skhe->shqk", grad_mixed, value_rows, preferred_element_type=jnp.float32
    )
    grad_values = jnp.einsum(
        "shqk,sqhe->skhe", soft_low, grad_mixed, preferred_element_type=jnp.float32
    )
    inner = jnp.sum(soft_full * grad_soft, -1, keepdims=True)
    grad_scores = (soft_full * (grad_soft - inner)).astype(jnp.bfloat16)
    grad_queries = jnp.einsum(
        "shqk,skhe->sqhe", grad_scores, key_rows, preferred_element_type=jnp.float32
    ) * HEAD_DIM ** (-0.5)
    grad_keys = jnp.einsum(
        "shqk,sqhe->skhe", grad_scores, query_rows, preferred_element_type=jnp.float32
    ) * HEAD_DIM ** (-0.5)
    return (grad_queries, grad_keys, grad_values)


def forward_pass(tokens_part, key_keep, weights):
    (
        w_qkv,
        w_out,
        w_up,
        w_down,
        gain_one,
        shift_one,
        bias_query,
        bias_value,
        bias_out,
        gain_two,
        shift_two,
        bias_up,
        bias_down,
    ) = weights
    seq_count, slot_count, model_width = tokens_part.shape
    inputs = tokens_part.astype(jnp.float32)
    normed_one = layer_norm(inputs, widen(gain_one), widen(shift_one)).astype(jnp.bfloat16)
    bias_all = jnp.concatenate(
        [widen(bias_query), jnp.zeros((model_width,), jnp.float32), widen(bias_value)]
    )
    triple = (project(normed_one, w_qkv) + bias_all).astype(jnp.bfloat16)
    head_shape = (seq_count, slot_count, HEADS, HEAD_DIM)
    query_rows = triple[:, :, :model_width].reshape(head_shape)
    key_rows = triple[:, :, model_width : 2 * model_width].reshape(head_shape)
    value_rows = triple[:, :, 2 * model_width :].reshape(head_shape)
    mixed_rows, log_total = attend_forward(query_rows, key_rows, value_rows, key_keep)
    mixed_low = mixed_rows.astype(jnp.bfloat16).reshape(seq_count, slot_count, model_width)
    hidden = inputs + (project(mixed_low, w_out) + widen(bias_out))
    normed_two = layer_norm(hidden, widen(gain_two), widen(shift_two)).astype(jnp.bfloat16)
    raised = project(normed_two, w_up) + widen(bias_up)
    gated_rows = smooth_gate(raised).astype(jnp.bfloat16)
    output = hidden + (project(gated_rows, w_down) + widen(bias_down))
    kept = (
        inputs,
        normed_one,
        query_rows,
        key_rows,
        value_rows,
        log_total,
        mixed_low,
        hidden,
        normed_two,
        raised,
        gated_rows,
    )
    return (output.astype(jnp.bfloat16), kept)


def backward_pass(cotangent_part, key_keep, weights, kept):
    (
        w_qkv,
        w_out,
        w_up,
        w_down,
        gain_one,
        shift_one,
        bias_query,
        bias_value,
        bias_out,
        gain_two,
        shift_two,
        bias_up,
        bias_down,
    ) = weights
    (
        inputs,
        normed_one,
        query_rows,
        key_rows,
        value_rows,
        log_total,
        mixed_low,
        hidden,
        normed_two,
        raised,
        gated_rows,
    ) = kept
    seq_count, slot_count, model_width = inputs.shape
    grad_output = cotangent_part.astype(jnp.float32) * key_keep[:, :, None].astype(jnp.float32)
    grad_low = grad_output.astype(jnp.bfloat16)
    grad_down = outer_sum(gated_rows, grad_low)
    grad_bias_down = jnp.sum(grad_output, (0, 1))
    grad_gated = project_back(grad_low, w_down)
    unused_gate, gate_back = jax.vjp(smooth_gate, raised)
    grad_raised = gate_back(grad_gated)[0].astype(jnp.bfloat16)
    grad_up = outer_sum(normed_two, grad_raised)
    grad_bias_up = jnp.sum(grad_raised, (0, 1), dtype=jnp.float32)
    grad_normed_two = project_back(grad_raised, w_up)
    unused_two, norm_back_two = jax.vjp(layer_norm, hidden, widen(gain_two), widen(shift_two))
    grad_hidden_part, grad_gain_two, grad_shift_two = norm_back_two(grad_normed_two)
    grad_hidden = grad_output + grad_hidden_part
    grad_branch = grad_hidden.astype(jnp.bfloat16)
    grad_out = outer_sum(mixed_low, grad_branch)
    grad_bias_out = jnp.sum(grad_branch, (0, 1), dtype=jnp.float32)
    head_shape = (seq_count, slot_count, HEADS, HEAD_DIM)
    grad_mixed = project_back(grad_branch, w_out).astype(jnp.bfloat16).reshape(head_shape)
    grad_queries, grad_keys, grad_values = attend_backward(
        query_rows, key_rows, value_rows, key_keep, log_total, grad_mixed
    )
    flat_shape = (seq_count, slot_count, model_width)
    grad_triple = jnp.concatenate(
        [
            grad_queries.reshape(flat_shape),
            grad_keys.reshape(flat_shape),
            grad_values.reshape(flat_shape),
        ],
        2,
    ).astype(jnp.bfloat16)
    grad_qkv = outer_sum(normed_one, grad_triple)
    grad_bias_query = jnp.sum(grad_triple[:, :, :model_width], (0, 1), dtype=jnp.float32)
    grad_bias_value = jnp.sum(grad_triple[:, :, 2 * model_width :], (0, 1), dtype=jnp.float32)
    grad_normed_one = project_back(grad_triple, w_qkv)
    unused_one, norm_back_one = jax.vjp(layer_norm, inputs, widen(gain_one), widen(shift_one))
    grad_inputs_part, grad_gain_one, grad_shift_one = norm_back_one(grad_normed_one)
    grad_inputs = (grad_hidden + grad_inputs_part).astype(jnp.bfloat16)
    grads = (
        grad_qkv,
        grad_out,
        grad_up,
        grad_down,
        grad_gain_one,
        grad_shift_one,
        grad_bias_query,
        grad_bias_value,
        grad_bias_out,
        grad_gain_two,
        grad_shift_two,
        grad_bias_up,
        grad_bias_down,
    )
    return (grad_inputs, grads)


def shards(
    tokens,
    lengths,
    source,
    cotangent,
    w_qkv,
    w_out,
    w_up,
    w_down,
    gain_one,
    shift_one,
    bias_query,
    bias_value,
    bias_out,
    gain_two,
    shift_two,
    bias_up,
    bias_down,
):
    per_micro = tokens.shape[0] // MICRO
    slot_count = tokens.shape[1]
    visible = jnp.where(source == 1, lengths, IMG_LEN)
    key_keep = jnp.arange(slot_count, dtype=jnp.int32)[None, :] < visible[:, None]
    shares = None
    outputs = []
    grad_parts = []
    for micro_index in range(MICRO):
        first_row = micro_index * per_micro
        tokens_part = tokens[first_row : first_row + per_micro]
        cotangent_part = cotangent[first_row : first_row + per_micro]
        keep_part = key_keep[first_row : first_row + per_micro]
        forward_set = (
            lax.all_gather(w_qkv, "dp", axis=0, tiled=True),
            lax.all_gather(w_out, "dp", axis=1, tiled=True),
            lax.all_gather(w_up, "dp", axis=0, tiled=True),
            lax.all_gather(w_down, "dp", axis=1, tiled=True),
            lax.all_gather(gain_one, "dp", axis=0, tiled=True),
            lax.all_gather(shift_one, "dp", axis=0, tiled=True),
            lax.all_gather(bias_query, "dp", axis=0, tiled=True),
            lax.all_gather(bias_value, "dp", axis=0, tiled=True),
            lax.all_gather(bias_out, "dp", axis=0, tiled=True),
            lax.all_gather(gain_two, "dp", axis=0, tiled=True),
            lax.all_gather(shift_two, "dp", axis=0, tiled=True),
            lax.all_gather(bias_up, "dp", axis=0, tiled=True),
            lax.all_gather(bias_down, "dp", axis=0, tiled=True),
        )
        output, kept = forward_pass(tokens_part, keep_part, forward_set)
        outputs.append(output)
        backward_set = (
            lax.all_gather(w_qkv, "dp", axis=0, tiled=True),
            lax.all_gather(w_out, "dp", axis=1, tiled=True),
            lax.all_gather(w_up, "dp", axis=0, tiled=True),
            lax.all_gather(w_down, "dp", axis=1, tiled=True),
            lax.all_gather(gain_one, "dp", axis=0, tiled=True),
            lax.all_gather(shift_one, "dp", axis=0, tiled=True),
            lax.all_gather(bias_query, "dp", axis=0, tiled=True),
            lax.all_gather(bias_value, "dp", axis=0, tiled=True),
            lax.all_gather(bias_out, "dp", axis=0, tiled=True),
            lax.all_gather(gain_two, "dp", axis=0, tiled=True),
            lax.all_gather(shift_two, "dp", axis=0, tiled=True),
            lax.all_gather(bias_up, "dp", axis=0, tiled=True),
            lax.all_gather(bias_down, "dp", axis=0, tiled=True),
        )
        grad_inputs, grads = backward_pass(cotangent_part, keep_part, backward_set, kept)
        grad_parts.append(grad_inputs)
        (
            g_qkv,
            g_out,
            g_up,
            g_down,
            g_gain_one,
            g_shift_one,
            g_bias_query,
            g_bias_value,
            g_bias_out,
            g_gain_two,
            g_shift_two,
            g_bias_up,
            g_bias_down,
        ) = grads
        summed = (
            lax.psum_scatter(g_qkv, "dp", scatter_dimension=0, tiled=True),
            lax.psum_scatter(g_out, "dp", scatter_dimension=1, tiled=True),
            lax.psum_scatter(g_up, "dp", scatter_dimension=0, tiled=True),
            lax.psum_scatter(g_down, "dp", scatter_dimension=1, tiled=True),
            lax.psum_scatter(g_gain_one, "dp", scatter_dimension=0, tiled=True),
            lax.psum_scatter(g_shift_one, "dp", scatter_dimension=0, tiled=True),
            lax.psum_scatter(g_bias_query, "dp", scatter_dimension=0, tiled=True),
            lax.psum_scatter(g_bias_value, "dp", scatter_dimension=0, tiled=True),
            lax.psum_scatter(g_bias_out, "dp", scatter_dimension=0, tiled=True),
            lax.psum_scatter(g_gain_two, "dp", scatter_dimension=0, tiled=True),
            lax.psum_scatter(g_shift_two, "dp", scatter_dimension=0, tiled=True),
            lax.psum_scatter(g_bias_up, "dp", scatter_dimension=0, tiled=True),
            lax.psum_scatter(g_bias_down, "dp", scatter_dimension=0, tiled=True),
        )
        shares = (
            summed
            if shares is None
            else tuple((before + after for before, after in zip(shares, summed)))
        )
    mixed = jnp.concatenate(outputs, 0)
    grad_tokens = jnp.concatenate(grad_parts, 0)
    return (
        mixed,
        grad_tokens,
        shares[0],
        shares[1],
        shares[2],
        shares[3],
        shares[4],
        shares[5],
        shares[6],
        shares[7],
        shares[8],
        shares[9],
        shares[10],
        shares[11],
        shares[12],
    )


def solution(mesh):
    in_specs = (
        P("dp", None, None),
        P("dp"),
        P("dp"),
        P("dp", None, None),
        P("dp", None),
        P(None, "dp"),
        P("dp", None),
        P(None, "dp"),
        P("dp"),
        P("dp"),
        P("dp"),
        P("dp"),
        P("dp"),
        P("dp"),
        P("dp"),
        P("dp"),
        P("dp"),
    )
    out_specs = (
        P("dp", None, None),
        P("dp", None, None),
        P("dp", None),
        P(None, "dp"),
        P("dp", None),
        P(None, "dp"),
        P("dp"),
        P("dp"),
        P("dp"),
        P("dp"),
        P("dp"),
        P("dp"),
        P("dp"),
        P("dp"),
        P("dp"),
    )
    return jax.shard_map(shards, mesh=mesh, in_specs=in_specs, out_specs=out_specs, check_vma=False)
```

profile of v0, /device:TPU:0, one launch (start us, length us, event | category | flops | bytes accessed | tf_op | source)
XLA Modules:
  0.0 812.6 jit_solution(11901369471236924716)
XLA Ops:
  19.5 42.8 %all-reduce.19 = (bf16[768]{0:T(1024)(128)(2,1)S(1)}, bf16[768]{0:T(1024)(128)(2,1)S(1)}, bf16[768]{0:T(1024)(128)(2,1)S(1)}, bf16[768]{0:T(1024)(128)(2,1)S(1)}...) all-reduce(bf16[768]{0:T(1024)(128)(2,1)S(1)} %dynamic-update-slice, ...), channel_id=1, replica_groups=mesh['dp'=32] {'dp'}, use_global_device_ids=true, to_apply=%add.3 | all-reduce | flops 9216 | bytes 36864
  63.0 1.4 convert_reduce_fusion.3
  64.5 1.6 fusion.52
  66.7 7.5 all-gather.5.cloned.1.call-done
  74.2 3.6 fusion.18
  78.6 1.1 copy.76
  79.7 3.4 fusion.19
  83.1 1.1 fusion.118
  84.3 1.3 copy.74
  85.6 2.3 copy.73
  87.9 2.1 copy.72
  90.0 2.7 fusion
  92.7 1.4 exponential_reduce_fusion.1
  94.1 1.1 copy-done
  95.2 2.3 convolution_convert_fusion.3
  97.5 32.4 %all-gather.7.cloned.1.call-done = bf16[768,768]{0,1:T(8,128)(2,1)} async-done(((bf16[768,24]{0,1:T(8,128)(2,1)}), bf16[768,768]{0,1:T(8,128)(2,1)}) %all-gather.7.cloned.1.call-update) | async-done | bytes 1179664 | tf_op jit(solution)/shard_map/all_gather | solution.py:248
  129.9 2.2 fusion.121
  132.8 1.7 fusion.1
  134.5 1.8 exponential_reduce_fusion
  136.3 2.3 convolution_convert_fusion.2
  141.6 53.8 %all-gather.9.cloned.1.call-done = bf16[768,3072]{1,0:T(8,128)(2,1)} async-done(((bf16[24,3072]{1,0:T(8,128)(2,1)}), bf16[768,3072]{1,0:T(8,128)(2,1)}) %all-gather.9.cloned.1.call-update) | async-done | bytes 4718608 | tf_op jit(solution)/shard_map/all_gather | solution.py:249
  195.4 6.2 convolution_add_fusion.6
  201.6 3.7 convolution_add_fusion.5
  205.3 55.3 %all-gather.11.cloned.1.call-done = bf16[3072,768]{0,1:T(8,128)(2,1)} async-done(((bf16[3072,24]{0,1:T(8,128)(2,1)}), bf16[3072,768]{0,1:T(8,128)(2,1)}) %all-gather.11.cloned.1.call-update) | async-done | bytes 4718608 | tf_op jit(solution)/shard_map/all_gather | solution.py:250
  260.6 8.2 %convert_reduce_fusion = (f32[3072]{0:T(1024)}, bf16[320,3072]{1,0:T(8,128)(2,1)S(1)}) fusion(f32[320,3072]{1,0:T(8,128)} %convolution_add_fusion.5, bf16[3072,768]{0,1:T(8,128)(2,1)} %all-gather.11.cloned.1.call-done, f32[320]{0:T(512)} %convert_element_type.264, bf16[2,320,768]{2,1,0:T(8,128)(2,1)} %param.20), kind=kOutput, calls=%fused_computation.39 | convolution fusion | flops 1532310528 | bytes 11122688 | tf_op jit(solution)/shard_map/spe,de->spd/dot_general | solution.py:34
  268.8 5.4 fusion.123
  274.3 5.3 convert_reduce_fusion.1
  279.7 2.6 fusion.57
  284.1 1.9 fusion.60
  287.4 1.1 copy.84
  288.5 2.0 fusion.77
  290.5 2.8 convolution_convert_fusion.5
  293.3 2.1 copy.80
  295.4 3.4 convolution_add_fusion.7
  299.0 5.4 multiply_reduce_fusion
  304.5 2.2 multiply_reduce_fusion.1
  307.2 2.1 multiply_convert_fusion
  309.4 1.8 multiply_convert_fusion.1
  312.2 1.3 convert_reduce_fusion.6
  314.6 1.3 convert_reduce_fusion.7
  316.0 2.2 convert_reduce_fusion.5
  318.2 2.3 fusion.65
  320.5 2.2 convert_reduce_fusion.4
  323.5 5.2 convolution_add_fusion
  330.0 5.2 fusion.85
  335.2 5.6 convolution_add_fusion.1
  340.9 1.1 copy-done.8
  342.0 4.5 fusion.107
  346.6 5.6 convolution_add_fusion.2
  353.4 1.9 reduce_sum.387
  355.3 1.3 add.368
  356.6 1.4 reshape.824
  357.9 1.3 add.367
  359.2 1.4 reshape.823
  360.6 5.0 fusion.122
  365.7 3.4 fusion.53
  369.1 1.3 reduce_sum.371
  375.9 2.5 fusion.51
  378.4 40.7 %all-reduce.18 = (f32[768]{0:T(1024)S(1)}, f32[768]{0:T(1024)S(1)}, f32[768]{0:T(1024)S(1)}, f32[768]{0:T(1024)S(1)}, f32[768]{0:T(1024)S(1)}, /*index=5*/f32[76...) all-reduce(f32[768]{0:T(1024)S(1)} %add.358, ...), channel_id=19, replica_groups=mesh['dp'=32] {'dp'}, use_global_device_ids=true, to_apply=%region_31.32.clone | all-reduce | flops 9216 | bytes 73728
  424.4 6.4 fusion.40
  430.9 5.1 fusion.41
  439.6 82.7 %reduce-scatter.5.cloned.1.call-done = f32[24,2304]{1,0:T(8,128)} async-done(((f32[768,2304]{1,0:T(8,128)}), f32[24,2304]{1,0:T(8,128)}) %reduce-scatter.5.cloned.1.call-update) | async-done | bytes 221200 | tf_op jit(solution)/shard_map/reduce_scatter | solution.py:296
  522.2 141.3 %reduce-scatter.11.cloned.1.call-done = f32[3072,24]{0,1:T(8,128)} async-done(((f32[3072,768]{0,1:T(8,128)}), f32[3072,24]{0,1:T(8,128)}) %reduce-scatter.11.cloned.1.call-update) | async-done | bytes 294928 | tf_op jit(solution)/shard_map/reduce_scatter | solution.py:299
  663.6 142.0 %reduce-scatter.9.cloned.1.call-done = f32[24,3072]{1,0:T(8,128)} async-done(((f32[768,3072]{1,0:T(8,128)}), f32[24,3072]{1,0:T(8,128)}) %reduce-scatter.9.cloned.1.call-update) | async-done | bytes 294928 | tf_op jit(solution)/shard_map/reduce_scatter | solution.py:298
  (327 shorter events, 41.2 us)
Async XLA Ops:
  7.2 67.0 %all-gather.5.cloned.1.call-start = ((), (), s32[]{:S(2)}) async-start(), calls=%async_computation.4 | async-start | bytes 3649536 | tf_op jit(solution)/shard_map/all_gather | solution.py:247
  7.9 122.0 %all-gather.7.cloned.1.call-start = ((), (), s32[]{:S(2)}) async-start(), calls=%async_computation.5 | async-start | bytes 1216512 | tf_op jit(solution)/shard_map/all_gather | solution.py:248
  8.7 186.7 %all-gather.9.cloned.1.call-start = ((), (), s32[]{:S(2)}) async-start(), calls=%async_computation.6 | async-start | bytes 4866048 | tf_op jit(solution)/shard_map/all_gather | solution.py:249
  9.4 251.2 %all-gather.11.cloned.1.call-start = ((), (), s32[]{:S(2)}) async-start(), calls=%async_computation.7 | async-start | bytes 4866048 | tf_op jit(solution)/shard_map/all_gather | solution.py:250
  10.0 429.6 %reduce-scatter.7.cloned.1.call-start = ((), (), s32[]{:S(2)}) async-start(), calls=%async_computation.9 | async-start | bytes 2433024 | tf_op jit(solution)/shard_map/reduce_scatter | solution.py:297
  10.8 83.3 %copy-start.80 = (pred[320]{0:T(512)(128)(4,1)}, pred[320]{0:T(512)(128)(4,1)S(1)}, u32[]{:S(2)}) copy-start(pred[320]{0:T(512)(128)(4,1)S(1)} %get-tuple-element.33) | copy-start | bytes 964
  10.8 123.7 %copy-start.77 = (pred[320]{0:T(512)(128)(4,1)}, pred[320]{0:T(512)(128)(4,1)S(1)}, u32[]{:S(2)}) copy-start(pred[320]{0:T(512)(128)(4,1)S(1)} %get-tuple-element.34) | copy-start | bytes 964
  62.4 67.5 %copy-start.99 = (f32[768]{0:T(1024)}, f32[768]{0:T(1024)S(1)}, u32[]{:S(2)}) copy-start(f32[768]{0:T(1024)S(1)} %convert_element_type.236) | copy-start | bytes 9220
  64.4 13.4 %copy-start.61 = (f32[320]{0:T(512)}, f32[320]{0:T(512)S(1)}, u32[]{:S(2)}) copy-start(f32[320]{0:T(512)S(1)} %get-tuple-element.105) | copy-start | bytes 3844
  64.5 15.2 %copy-start.52 = (f32[320]{0:T(512)}, f32[320]{0:T(512)S(1)}, u32[]{:S(2)}) copy-start(f32[320]{0:T(512)S(1)} %get-tuple-element.106) | copy-start | bytes 3844
  66.1 11.7 %copy-start.82 = (f32[320]{0:T(512)}, f32[320]{0:T(512)S(1)}, u32[]{:S(2)}) copy-start(f32[320]{0:T(512)S(1)} %get-tuple-element.30) | copy-start | bytes 3844
  66.7 13.0 %copy-start.49 = (f32[320]{0:T(512)}, f32[320]{0:T(512)S(1)}, u32[]{:S(2)}) copy-start(f32[320]{0:T(512)S(1)} %fusion.91) | copy-start | bytes 3844
  66.7 11.2 %copy-start.58 = (f32[320]{0:T(512)}, f32[320]{0:T(512)S(1)}, u32[]{:S(2)}) copy-start(f32[320]{0:T(512)S(1)} %fusion.93) | copy-start | bytes 3844
  78.3 54.5 %copy-start.17 = (bf16[1,320,768]{1,2,0:T(8,128)(2,1)}, bf16[1,320,768]{1,2,0:T(8,128)(2,1)S(1)}, u32[]{:S(2)}) copy-start(bf16[1,320,768]{1,2,0:T(8,128)(2,1)S(1)} %copy.78) | copy-start | bytes 1474564
  78.6 54.2 %copy-start.19 = (bf16[1,320,768]{1,2,0:T(8,128)(2,1)}, bf16[1,320,768]{1,2,0:T(8,128)(2,1)S(1)}, u32[]{:S(2)}) copy-start(bf16[1,320,768]{1,2,0:T(8,128)(2,1)S(1)} %copy.77) | copy-start | bytes 1474564
  85.6 7.1 copy-start.21
  132.1 150.3 %copy-start.7 = (f32[1,320,768]{2,1,0:T(8,128)}, f32[1,320,768]{2,1,0:T(8,128)S(1)}, u32[]{:S(2)}) copy-start(f32[1,320,768]{2,1,0:T(8,128)S(1)} %get-tuple-element.82) | copy-start | bytes 2949124
  132.4 8.0 copy-start.84
  138.7 62.9 %copy-start.43 = (bf16[12,64,320]{2,1,0:T(8,128)(2,1)}, bf16[12,64,320]{2,1,0:T(8,128)(2,1)S(1)}, u32[]{:S(2)}) copy-start(bf16[12,64,320]{2,1,0:T(8,128)(2,1)S(1)} %convolution_convert_fusion.2) | copy-start | bytes 1474564
  139.5 142.9 %copy-start.3 = (f32[1,320,768]{2,1,0:T(8,128)}, f32[1,320,768]{2,1,0:T(8,128)S(1)}, u32[]{:S(2)}) copy-start(f32[1,320,768]{2,1,0:T(8,128)S(1)} %get-tuple-element.78) | copy-start | bytes 2949124
  195.3 6.2 copy-start.66
  195.3 6.2 copy-start.70
  195.3 6.2 copy-start.97
  195.4 6.2 copy-start.103
  260.6 13.7 %copy-start.107 = (f32[320,3072]{1,0:T(8,128)S(1)}, f32[320,3072]{1,0:T(8,128)}, u32[]{:S(2)}) copy-start(f32[320,3072]{1,0:T(8,128)} %convolution_add_fusion.6) | copy-start | bytes 11796484
  268.8 5.4 copy-start.37
  268.8 5.4 copy-start.14
  268.8 5.4 copy-start.88
  268.8 5.4 copy-start.102
  268.8 10.8 %slice-start.4 = ((s8[4718592]{0:T(1024)(128)(4,1)}), s8[4194304]{0:T(1024)(128)(4,1)S(1)}, s32[]{:S(2)}) async-start(s8[4718592]{0:T(1024)(128)(4,1)} %bitcast.240), calls=%async_computation.16 | async-start | bytes 8388608
  274.3 5.4 copy-start.56
  274.3 5.4 copy-start.67
  274.3 5.4 copy-start.69
  274.3 5.4 copy-start.71
  274.3 5.4 slice-start.5
  283.2 5.3 copy-start.93
  283.2 5.3 copy-start.91
  298.8 5.6 slice-start
  298.9 223.3 %reduce-scatter.5.cloned.1.call-start = ((), (), s32[]{:S(2)}) async-start(), calls=%async_computation.8 | async-start | bytes 7299072 | tf_op jit(solution)/shard_map/reduce_scatter | solution.py:296
  298.9 5.5 slice-start.1
  298.9 5.5 copy-start.29
  299.0 5.5 copy-start.31
  299.0 5.5 copy-start.45
  299.0 5.5 copy-start.81
  312.2 10.5 %copy-start.32 = (bf16[12,64,320]{2,1,0:T(8,128)(2,1)}, bf16[12,64,320]{2,1,0:T(8,128)(2,1)S(1)}, u32[]{:S(2)}) copy-start(bf16[12,64,320]{2,1,0:T(8,128)(2,1)S(1)} %fusion.35) | copy-start | bytes 1474564
  313.6 9.2 %copy-start.35 = (bf16[12,64,320]{2,1,0:T(8,128)(2,1)}, bf16[12,64,320]{2,1,0:T(8,128)(2,1)S(1)}, u32[]{:S(2)}) copy-start(bf16[12,64,320]{2,1,0:T(8,128)(2,1)S(1)} %get-tuple-element.94) | copy-start | bytes 1474564
  328.8 6.4 copy-start.75
  328.8 334.8 %reduce-scatter.11.cloned.1.call-start = ((), (), s32[]{:S(2)}) async-start(), calls=%async_computation.11 | async-start | bytes 9732096 | tf_op jit(solution)/shard_map/reduce_scatter | solution.py:299
  330.0 5.2 copy-start.5
  340.8 5.7 copy-start.4
  340.9 464.7 %reduce-scatter.9.cloned.1.call-start = ((), (), s32[]{:S(2)}) async-start(), calls=%async_computation.10 | async-start | bytes 9732096 | tf_op jit(solution)/shard_map/reduce_scatter | solution.py:298
  352.1 5.8 copy-start.73
  360.6 5.0 copy-start.104
  365.6 10.2 %copy-start.51 = (f32[320]{0:T(512)S(1)}, f32[320]{0:T(512)}, u32[]{:S(2)}) copy-start(f32[320]{0:T(512)} %copy-done.49) | copy-start | bytes 3844
  365.7 10.2 %copy-start.60 = (f32[320]{0:T(512)S(1)}, f32[320]{0:T(512)}, u32[]{:S(2)}) copy-start(f32[320]{0:T(512)} %copy-done.58) | copy-start | bytes 3844
  369.0 9.4 %copy-start.95 = (f32[768]{0:T(1024)S(1)}, f32[768]{0:T(1024)}, u32[]{:S(2)}) copy-start(f32[768]{0:T(1024)} %reshape.824) | copy-start | bytes 9220
  369.0 9.4 %copy-start.96 = (f32[768]{0:T(1024)S(1)}, f32[768]{0:T(1024)}, u32[]{:S(2)}) copy-start(f32[768]{0:T(1024)} %reshape.823) | copy-start | bytes 9220
  369.1 55.4 %copy-start.98 = (f32[768]{0:T(1024)S(1)}, f32[768]{0:T(1024)}, u32[]{:S(2)}) copy-start(f32[768]{0:T(1024)} %convert_element_type.242) | copy-start | bytes 9220
  424.4 6.4 copy-start.6
  430.8 6.3 copy-start.12
  430.9 6.3 copy-start.13
  430.9 6.3 copy-start.16
  430.9 6.3 copy-start.90
  430.9 6.3 copy-start.94
  (58 other events, 142.8 us)
Sparse Core Ops, SparseCore 0:
  10.9 63.2 all-gather.4
  77.1 52.7 all-gather.6
  132.8 62.4 all-gather.8
  198.1 62.4 all-gather.10
  299.0 97.8 reduce-scatter.6
  404.0 118.1 reduce-scatter.4
  528.7 134.8 reduce-scatter.10
  671.0 134.4 reduce-scatter.8
where the time goes:
time: 817 us; the launch traced here: 813 us
  waiting for transfers between devices  518 us (63%)
  matrix products  124 us (15%)
  blocking collectives  83.5 us (10%)
  local copies, waits for them, and re-layouts  36.5 us (4%)
  other arithmetic  34.4 us (4%)
  between operations  15.7 us (2%)
    reduce_scatter x1, waiting for transfers between devices, shards(): lax.psum_scatter(g_up, 'dp', scatter_dimension=0, tiled=True)  142 us
    reduce_scatter x1, waiting for transfers between devices, shards(): lax.psum_scatter(g_down, 'dp', scatter_dimension=1, tiled=True)  141 us
    unnamed x2, blocking collectives  83.5 us
    reduce_scatter x1, waiting for transfers between devices, shards(): lax.psum_scatter(g_qkv, 'dp', scatter_dimension=0, tiled=True)  82.7 us
    all_gather x1, waiting for transfers between devices, shards(): lax.all_gather(w_down, 'dp', axis=1, tiled=True)  55.3 us
    all_gather x1, waiting for transfers between devices, shards(): lax.all_gather(w_up, 'dp', axis=0, tiled=True)  53.8 us
    dot_general x8, matrix products, outer_sum(): jnp.einsum('spd,spe->de', group_rows, grad_rows, preferred_element_type=j...  33.8 us
    dot_general x8, matrix products, project_back(): jnp.einsum('spe,de->spd', grad_rows, matrix, preferred_element_type=jnp.f...  33.3 us
  transfers between devices with their start and end apart: 8, of which 7 were waited for; matrix products, arithmetic and copies ran while one was open for 18% of the time, Pallas kernels for 0%

commit v1 on v0

v1 whole, which is shorter than its diff:
```python
import functools
import jax
import jax.numpy as jnp
from jax import lax
from jax.experimental import pallas as pl
from jax.experimental.pallas import tpu as pltpu
from jax.sharding import PartitionSpec as P

HEADS = 12
HEAD_DIM = 64
IMG_LEN = 196
EPS = 1e-06
D = 768
FF = 3072
HALF = D // 2
WIDE = FF // 2
LOW = jnp.bfloat16
F32 = jnp.float32
STEP = 384
ROWS = 64
SCALE = HEAD_DIM ** (-0.5)
CHUNKS = ((3 * HALF + 128, 640), (HALF + WIDE, 1024))
Z_CODES = (0, 4, 8, 12)
SMEM = pl.BlockSpec(memory_space=pltpu.SMEM)
ANY = pl.BlockSpec(memory_space=pl.ANY)
VMEM = pl.BlockSpec(memory_space=pltpu.VMEM)


def shape(dims, kind=LOW):
    return jax.ShapeDtypeStruct(dims, kind)


def whole(array):
    zeros = (0,) * len(array.shape)
    return pl.BlockSpec(tuple(array.shape), lambda *i: zeros)


def cols(array, width, offset=0):
    return pl.BlockSpec((array.shape[0], width), lambda *i: (0, offset + i[0]))


def fixed(array, width, index=0):
    return pl.BlockSpec((array.shape[0], width), lambda *i: (0, index))


class Chain:
    def __init__(self):
        self.last = None

    def __call__(
        self, body, outs, ins, *, info=None, grid=(1,), in_specs=None, out_specs=None, scratch=(), us=1.0
    ):
        head = [] if info is None else [info]
        ins = list(ins)
        count = len(head) + len(ins)
        in_specs = list(in_specs or [whole(a) for a in ins])
        out_specs = tuple(out_specs or [whole(o) for o in outs])
        if self.last is not None:
            ins.append(self.last)
            in_specs.append(ANY)
        total = len(head) + len(ins)

        def run(*refs):
            body(*refs[:count], *refs[total:])

        size = sum(a.size * a.dtype.itemsize for a in ins)
        size += sum(o.size * jnp.dtype(o.dtype).itemsize for o in outs)
        results = pl.pallas_call(
            run,
            out_shape=tuple(outs),
            grid_spec=pltpu.PrefetchScalarGridSpec(
                num_scalar_prefetch=len(head),
                grid=grid,
                in_specs=in_specs,
                out_specs=out_specs,
                scratch_shapes=list(scratch),
            ),
            compiler_params=pltpu.CompilerParams(
                vmem_limit_bytes=min(48, 12 + 2 * size // 2**20) * 2**20
            ),
            cost_estimate=pl.CostEstimate(
                flops=int(us * 1.1e9), bytes_accessed=size, transcendentals=0
            ),
        )(*head, *ins)
        self.last = min(results, key=lambda r: r.size * r.dtype.itemsize)
        return results


def dot(left, right, left_dim=1, right_dim=0):
    return lax.dot_general(
        left, right, (((left_dim,), (right_dim,)), ((), ())), preferred_element_type=F32
    )


def standardize(values):
    center = values - jnp.mean(values, -1, keepdims=True)
    scale = lax.rsqrt(jnp.mean(center * center, -1, keepdims=True) + EPS)
    return center * scale, scale


def row_loop(rows, body, init=0):
    def step(i, carry):
        return body(pl.ds(pl.multiple_of(i * ROWS, ROWS), ROWS), carry)

    return lax.fori_loop(0, rows // ROWS, step, init)


def swap(value, bit):
    pairs = [(i, i ^ bit) for i in range(32)]
    return lax.ppermute(value, "dp", pairs)


def pack_body(info, small, *refs):
    weights, (mine, other), (rows, *held, sem) = refs[:3], refs[3:5], refs[5:]
    copies = [pltpu.make_async_copy(w, v, sem) for w, v in zip(weights, held)]
    for copy in copies:
        copy.start()
    w_qkv, w_out, w_up = held
    rows[...] = jnp.zeros_like(rows)
    share = w_qkv.shape[0]
    rows[: small.shape[0], :share] = small[...].astype(F32)
    block = rows[...].T[:share, :].astype(LOW)
    for copy in copies:
        copy.wait()
    for flip, out in enumerate((mine, other)):
        h = info[1] ^ flip

        def half(weight, width, start=0):
            return weight[:, pl.ds(pl.multiple_of(start + h * width, 128), width)]

        for i in range(3):
            out[:, i * HALF : (i + 1) * HALF] = half(w_qkv, HALF, i * D)
        out[:, 3 * HALF : 3 * HALF + 128] = block
        at = CHUNKS[0][0]
        out[:, at : at + HALF] = half(w_out, HALF)
        out[:, at + HALF :] = half(w_up, WIDE)


def unit_body(info, mine, other, unit_one, unit_two, unit_a, unit_b):
    a, b = mine[...].astype(F32), other[...].astype(F32)
    unit = jnp.where(
        info[1] == 0, jnp.concatenate([a, b], 0), jnp.concatenate([b, a], 0)
    ).astype(LOW)
    start = at_a = at_b = 0
    for (width, cut), out in zip(CHUNKS, (unit_one, unit_two)):
        part = unit[:, start : start + width]
        out[...] = part
        unit_a[:, at_a : at_a + cut] = part[:, :cut]
        unit_b[:, at_b : at_b + width - cut] = part[:, cut:]
        start, at_a, at_b = start + width, at_a + cut, at_b + width - cut


def own_body(unit_a, far_a, unit_b, far_b, pair_a, pair_b):
    for pair, unit, far in ((pair_a, unit_a, far_a), (pair_b, unit_b, far_b)):
        pair[0] = unit[...]
        pair[1] = far[...]


def stack_body(cut, z_one, z_two, z_three, stack_a, stack_b):
    for i, piece in enumerate((z_one, z_two, z_three)):
        stack_a[i] = piece[:, :cut]
        stack_b[i] = piece[:, cut:]


def join_body(stack_a, far_a, stack_b, far_b, join_a, join_b):
    for join, stack, far in ((join_a, stack_a, far_a), (join_b, stack_b, far_b)):
        join[0:3] = stack[...]
        join[3:6] = far[...]


def place_body(plan, info, *refs):
    pieces, out, sem = refs[:-2], refs[-2], refs[-1]
    copies = []
    for piece, (codes, source, target, width) in zip(pieces, plan):
        for i, code in enumerate(codes):
            row = pl.multiple_of((info[0] ^ code) * 48, 48)
            copies.append(
                pltpu.make_async_copy(
                    piece.at[i, :, pl.ds(source, width)],
                    out.at[pl.ds(row, 48), pl.ds(target, width)],
                    sem,
                )
            )
    for copy in copies:
        copy.start()
    for copy in copies:
        copy.wait()


KEEP_A = tuple(c ^ y for y in (0, 2) for c in Z_CODES)
KEEP_B = tuple(c ^ x for x in (0, 1) for c in Z_CODES)
SEND_A = tuple(c ^ 1 for c in KEEP_A)
SEND_B = tuple(c ^ 2 for c in KEEP_B)


def spread(chip, grad, send, keep, send_codes, keep_codes):
    for out, codes in ((send, send_codes), (keep, keep_codes)):
        for i, code in enumerate(codes):
            row = pl.multiple_of((chip ^ code) * 48, 48)
            out[i] = grad[pl.ds(row, 48), :].astype(LOW)


def add(left, right):
    return (left.astype(F32) + right.astype(F32)).astype(LOW)


def first_sum_body(far_a, keep_a, far_b, keep_b, send_a, own_a, send_b, own_b):
    for far, keep, send, own in ((far_a, keep_a, send_a, own_a), (far_b, keep_b, send_b, own_b)):
        for i in range(4):
            send[i] = add(far[4 + i], keep[4 + i])
            own[i] = add(far[i], keep[i])


def second_sum_body(far_a, keep_a, far_b, keep_b, *outs):
    cut = keep_a.shape[2]
    for i, out in enumerate(outs):
        out[:, :cut] = add(far_a[i], keep_a[i])
        out[:, cut:] = add(far_b[i], keep_b[i])


def last_sum_body(info, own, z_one, z_two, z_three, mine, other, total):
    value = own[...].astype(F32)
    for piece in (z_one, z_two, z_three):
        value = value + piece[...].astype(F32)
    total[...] = value
    rows = mine.shape[0]
    mine[...] = total[pl.ds(pl.multiple_of(info[1] * rows, 8), rows), :]
    other[...] = total[pl.ds(pl.multiple_of((1 - info[1]) * rows, 8), rows), :]


def merge(info, mine, other, start, width, out, count=1):
    for flip, part in enumerate((mine, other)):
        h = info[1] ^ flip
        for i in range(count):
            at = pl.multiple_of((2 * i + h) * width, 128)
            out[:, pl.ds(at, width)] = part[:, start + i * width : start + (i + 1) * width]


def merge_down_body(info, mine, other, out):
    merge(info, mine, other, 0, WIDE, out)


def merge_up_body(info, mine, other, out_up, out_out):
    merge(info, mine, other, 0, WIDE, out_up)
    merge(info, mine, other, WIDE, HALF, out_out)


def merge_qkv_body(info, mine, other, out, vec):
    merge(info, mine, other, 0, HALF, out, 3)
    vec[...] = mine[:, 3 * HALF :] + other[:, 3 * HALF :]


def start_body(slots, visible, cot, dy, total):
    rows = cot.shape[0]
    total[...] = jnp.zeros_like(total)
    for s in range(rows // slots):
        live = lax.broadcasted_iota(jnp.int32, (slots, 1), 0) < visible[s]
        part = jnp.where(live, cot[s * slots : (s + 1) * slots, :].astype(F32), 0.0)
        dy[s * slots : (s + 1) * slots, :] = part.astype(LOW)
        total[0:1, :] += jnp.sum(part, 0, keepdims=True)


def qkv_body(info, tokens, own, par, normed, qkv_own, qkv_par, vecs):
    vecs[...] = own[:, 3 * HALF :].astype(F32).T[:16, :]

    def norm(at, carry):
        z, _ = standardize(tokens[at, :].astype(F32))
        normed[at, :] = (z * vecs[0:1, :] + vecs[1:2, :]).astype(LOW)
        return carry

    row_loop(tokens.shape[0], norm)
    for flip, (weight, out) in enumerate(((own, qkv_own), (par, qkv_par))):
        half = half_of(info, flip, HALF)
        for i in range(3):
            at = slice(i * STEP, (i + 1) * STEP)
            value = dot(normed[...], weight[:, at])
            if i != 1:
                value = value + vecs[6 + i // 2 : 7 + i // 2, half]
            out[:, at] = value.astype(LOW)


def soft_of(query, key, live):
    scores = jnp.where(live, dot(query, key, 1, 1) * SCALE, -1e30)
    power = jnp.exp(scores - jnp.max(scores, -1, keepdims=True))
    return power * (1.0 / jnp.sum(power, -1, keepdims=True))


def attend_body(slots, visible, qkv, out):
    rows = qkv.shape[0]
    lane = lax.broadcasted_iota(jnp.int32, (1, 128), 1)
    for s in range(rows // slots):
        at = slice(s * slots, (s + 1) * slots)
        live = lax.broadcasted_iota(jnp.int32, (1, slots), 1) < visible[s]
        for j in range(HALF // 128):
            query, key, value = (
                qkv[at, i * HALF + j * 128 : i * HALF + (j + 1) * 128] for i in range(3)
            )
            mixed = None
            for e in range(2):
                mine = (lane < HEAD_DIM) if e == 0 else (lane >= HEAD_DIM)
                soft = soft_of(jnp.where(mine, query, 0), key, live).astype(LOW)
                part = dot(soft, jnp.where(mine, value, 0))
                mixed = part if mixed is None else mixed + part
            out[at, j * 128 : (j + 1) * 128] = mixed.astype(LOW)


def hidden_body(tokens, vecs, o_own, o_par, own, par, hidden, normed):
    hidden[...] = dot(o_own[...], own[...], 1, 1) + dot(o_par[...], par[...], 1, 1)

    def norm(at, carry):
        value = tokens[at, :].astype(F32) + (hidden[at, :] + vecs[4:5, :])
        hidden[at, :] = value
        z, _ = standardize(value)
        normed[at, :] = (z * vecs[2:3, :] + vecs[3:4, :]).astype(LOW)
        return carry

    row_loop(tokens.shape[0], norm)


GELU_A = 0.7978845608028654
GELU_B = 0.044715


def raise_body(normed, dy, b_own, b_par, own, par, a_own, s_own, s_par, bundle):
    i = pl.program_id(0)

    @pl.when(i == 0)
    def _():
        bundle[:, :D] = dy[...]

    for bias, weight, slope in ((b_own, own, s_own), (b_par, par, s_par)):
        u = dot(normed[...], weight[...]) + bias[...]
        square = u * u
        t = jnp.tanh(u * (GELU_A + (GELU_A * GELU_B) * square))
        gated = u * (0.5 + 0.5 * t)
        curve = GELU_A + (3.0 * GELU_A * GELU_B) * square
        slope[...] = ((0.5 + 0.5 * t) + (gated * (1.0 - t)) * curve).astype(LOW)
        if weight is own:
            a_own[...] = gated.astype(LOW)
        else:
            at = pl.multiple_of(D + i * STEP, 128)
            bundle[:, pl.ds(at, STEP)] = gated.astype(LOW)


def half_of(info, flip, width):
    return pl.ds(pl.multiple_of((info[1] ^ flip) * width, 128), width)


def mix_body(info, hidden, vecs, a_own, bundle, weight, out):
    value = dot(a_own[...], weight[:, half_of(info, 0, WIDE)], 1, 1)
    value += dot(bundle[:, D:], weight[:, half_of(info, 1, WIDE)], 1, 1)
    out[...] = (hidden[...] + (value + vecs[5:6, :])).astype(LOW)


def raise_back_body(info, dy, normed, s_own, s_par, own, par, d_own, t_own, t_par, bundle):
    i = pl.program_id(0)

    @pl.when(i == 0)
    def _():
        bundle[:, :D] = normed[...]

    for slope, weight, total in ((s_own, own, t_own), (s_par, par, t_par)):
        value = (dot(dy[...], weight[...]) * slope[...].astype(F32)).astype(LOW)
        total[...] = jnp.sum(value.astype(F32), 0, keepdims=True)
        if weight is own:
            d_own[...] = value
        else:
            at = pl.multiple_of(D + i * STEP, 128)
            bundle[:, pl.ds(at, STEP)] = value


def norm_back(part, values, gain):
    z, scale = standardize(values)
    e = part * gain
    mean_e = jnp.mean(e, -1, keepdims=True)
    mean_ez = jnp.mean(e * z, -1, keepdims=True)
    return scale * (e - mean_e - z * mean_ez), z


def hidden_back_body(
    steps, dy, hidden, vecs, o_par, d_own, d_par, own, par, dh, bundle, sums, acc
):
    i = pl.program_id(0)
    part = dot(d_own[...], own[...], 1, 1) + dot(d_par[...], par[...], 1, 1)

    @pl.when(i == 0)
    def _():
        acc[...] = part

    @pl.when(i > 0)
    def _():
        acc[...] += part

    @pl.when(i == steps - 1)
    def _():
        bundle[:, D:] = o_par[...]

        def back(at, carry):
            part = acc[at, :]
            value, z = norm_back(part, hidden[at, :], vecs[2:3, :])
            value = dy[at, :].astype(F32) + value
            dh[at, :] = value
            low = value.astype(LOW)
            bundle[at, :D] = low
            gain, shift, bias = carry
            return (
                gain + jnp.sum(part * z, 0, keepdims=True),
                shift + jnp.sum(part, 0, keepdims=True),
                bias + jnp.sum(low.astype(F32), 0, keepdims=True),
            )

        zero = jnp.zeros((1, D), F32)
        totals = row_loop(acc.shape[0], back, (zero, zero, zero))
        for r in range(3):
            sums[r : r + 1, :] = totals[r]


def attend_back_body(slots, start, visible, normed, qkv, dp, out_weight, dqkv, sums, mixed):
    rows = qkv.shape[0]
    if start:
        dqkv[:, :start] = normed[...]
    mixed[...] = dot(dp[...], out_weight[...]).astype(LOW)
    lane = lax.broadcasted_iota(jnp.int32, (1, 128), 1)
    sums[...] = jnp.zeros_like(sums)
    for s in range(rows // slots):
        at = slice(s * slots, (s + 1) * slots)
        live = lax.broadcasted_iota(jnp.int32, (1, slots), 1) < visible[s]
        for j in range(HALF // 128):
            cols = [slice(i * HALF + j * 128, i * HALF + (j + 1) * 128) for i in range(3)]
            query, key, value = (qkv[at, c] for c in cols)
            grad = mixed[at, j * 128 : (j + 1) * 128]
            totals = [None] * 3
            for e in range(2):
                mine = (lane < HEAD_DIM) if e == 0 else (lane >= HEAD_DIM)
                query_e, key_e, grad_e = (jnp.where(mine, v, 0) for v in (query, key, grad))
                soft = soft_of(query_e, key, live)
                grad_soft = dot(grad_e, value, 1, 1)
                inner = jnp.sum(soft * grad_soft, -1, keepdims=True)
                grad_scores = (soft * (grad_soft - inner)).astype(LOW)
                parts = (
                    dot(grad_scores, key_e),
                    dot(grad_scores, query_e, 0, 0),
                    dot(soft.astype(LOW), grad_e, 0, 0),
                )
                totals = [p if t is None else t + p for t, p in zip(totals, parts)]
            for i, factor in enumerate((SCALE, SCALE, 1.0)):
                low = (totals[i] * factor).astype(LOW)
                dqkv[at, start + cols[i].start : start + cols[i].stop] = low
                if i != 1:
                    sums[i : i + 1, j * 128 : (j + 1) * 128] += jnp.sum(
                        low.astype(F32), 0, keepdims=True
                    )


def token_back_body(
    info, tokens, dh, vecs, sums_two, dy_sum, up_sum, sums_own, sums_par, d_own, d_par, own, par,
    out, block, acc, sums,
):
    acc[...] = dot(d_own[...], own[...], 1, 1) + dot(d_par[:, D:], par[...], 1, 1)

    def back(at, carry):
        part = acc[at, :]
        value, z = norm_back(part, tokens[at, :].astype(F32), vecs[0:1, :])
        out[at, :] = (dh[at, :] + value).astype(LOW)
        gain, shift = carry
        return (
            gain + jnp.sum(part * z, 0, keepdims=True),
            shift + jnp.sum(part, 0, keepdims=True),
        )

    zero = jnp.zeros((1, D), F32)
    totals = row_loop(acc.shape[0], back, (zero, zero))
    sums[...] = jnp.zeros_like(sums)
    for r in range(2):
        sums[r : r + 1, :] = totals[r]
    sums[2:5, :] = sums_two[0:3, :]
    sums[5:6, :] = dy_sum[0:1, :]
    for flip, part in enumerate((sums_own, sums_par)):
        half = half_of(info, flip, HALF)
        sums[6:7, half] = part[0:1, :]
        sums[7:8, half] = part[2:3, :]
    sums[8:12, :] = up_sum[...]
    block[...] = sums[...].T


def outer(left, left_far, right, right_far):
    return dot(left[...], right[...], 0, 0) + dot(left_far[...], right_far[...], 0, 0)


def down_grad_body(
    cut, chip_ref, left, left_far, right, right_far, send_a, keep_a, send_b, keep_b, grad
):
    i = pl.program_id(0)
    chip = chip_ref[0]
    grad[...] = outer(left, left_far, right, right_far)

    @pl.when(i < cut)
    def _():
        spread(chip, grad, send_a, keep_a, SEND_A, KEEP_A)

    @pl.when(i >= cut)
    def _():
        spread(chip, grad, send_b, keep_b, SEND_B, KEEP_B)


def up_grad_body(
    chip_ref, norm, norm_far, du, du_far, dp, dp_far, o, o_far, send_a, keep_a, send_b, keep_b, grad
):
    i = pl.program_id(0)
    chip = chip_ref[0]

    @pl.when(i < 4)
    def _():
        grad[...] = outer(norm, norm_far, du, du_far)

    @pl.when(i == 4)
    def _():
        grad[...] = outer(dp, dp_far, o, o_far)

    @pl.when(i < 2)
    def _():
        spread(chip, grad, send_a, keep_a, SEND_A, KEEP_A)

    @pl.when(i >= 2)
    def _():
        spread(chip, grad, send_b, keep_b, SEND_B, KEEP_B)


def qkv_grad_body(
    chip_ref, norm, dqkv, bundle, vecs, send_a, keep_a, send_b, keep_b, grad
):
    chip = chip_ref[0]
    for i in range(3):
        at = slice(i * STEP, (i + 1) * STEP)
        far = slice(D + i * STEP, D + (i + 1) * STEP)
        grad[...] = outer(norm, bundle.at[:, :D], dqkv.at[:, at], bundle.at[:, far])
        if i < 2:
            spread(chip, grad, send_a.at[:, :, at], keep_a.at[:, :, at], SEND_A, KEEP_A)
        else:
            cols = slice(0, STEP)
            spread(chip, grad, send_b.at[:, :, cols], keep_b.at[:, :, cols], SEND_B, KEEP_B)
    grad[:, 0:128] = vecs[...]
    cols = slice(STEP, STEP + 128)
    spread(
        chip, grad.at[:, 0:128], send_b.at[:, :, cols], keep_b.at[:, :, cols], SEND_B, KEEP_B
    )


def pick(flag, left, right):
    return jnp.where(flag, left, right)


def half_major(matrix):
    rows = matrix.shape[0]
    return matrix.reshape(rows, 3, 2, HALF).transpose(0, 2, 1, 3).reshape(rows, 3 * D)


def third_major(matrix):
    rows = matrix.shape[0]
    return matrix.reshape(rows, 2, 3, HALF).transpose(0, 2, 1, 3).reshape(rows, 3 * D)


class WholeComm:
    def __init__(self, count):
        self.info = jnp.zeros((2,), jnp.int32)

    def order(self, low, high):
        return low, high

    def weights(self, call, small, w_qkv, w_out, w_up, w_down):
        def gather(value):
            return lax.all_gather(value, "dp", axis=0, tiled=True)

        def half(matrix, h):
            width = matrix.shape[1] // 2
            return matrix[:, h * width : (h + 1) * width]

        block = gather(jnp.pad(small.T, ((0, 0), (0, 128 - small.shape[0]))))
        qkv, out, up = (gather(w) for w in (half_major(w_qkv), w_out, w_up))
        self.first = [jnp.concatenate([half(qkv, h), block], 1) for h in range(2)]
        self.second = [jnp.concatenate([half(out, h), half(up, h)], 1) for h in range(2)]
        return gather(w_down)

    def step(self, call):
        pass

    def first_weights(self, call):
        return self.first

    def middle(self, call):
        pass

    def second_weights(self, call):
        return self.second

    def pump(self, call):
        pass

    def reduce(self, value):
        return lax.psum_scatter(value, "dp", scatter_dimension=0, tiled=True)

    def reduce_down(self, call, dy, gated, bundle):
        self.down = self.reduce(dot(dy, jnp.concatenate([gated, bundle[:, D:]], 1), 0, 0))

    def reduce_up(self, call, normed, raised, up_bundle, mixed, out_bundle):
        raised = jnp.concatenate([raised, up_bundle[:, D:]], 1)
        mixed = jnp.concatenate([mixed, out_bundle[:, D:]], 1)
        self.up = (
            self.reduce(dot(normed, raised, 0, 0)),
            self.reduce(dot(out_bundle[:, :D], mixed, 0, 0)),
        )

    def reduce_qkv(self, call, normed, triple, bundle, block):
        triple = jnp.concatenate([triple, bundle[:, D:]], 1)
        self.qkv = third_major(self.reduce(dot(normed, triple, 0, 0))), self.reduce(block)

    def results(self, call):
        return self.down, *self.up, *self.qkv


class GridComm:
    def __init__(self):
        index = lax.axis_index("dp")
        self.info = jnp.stack([index >> 1, index & 1]).astype(jnp.int32)
        self.is_first = (index & 1) == 0
        self.jobs = []

    def order(self, low, high):
        return pick(self.is_first, low, high), pick(self.is_first, high, low)

    def weights(self, call, small, w_qkv, w_out, w_up, w_down):
        down = lax.all_gather(w_down, "dp", axis=0, tiled=True)
        rows = w_qkv.shape[0]
        total = sum(width for width, _ in CHUNKS)
        total_a = sum(cut for _, cut in CHUNKS)
        mine, other = call(
            pack_body,
            [shape((rows, total))] * 2,
            [small, w_qkv, w_out, w_up],
            info=self.info,
            in_specs=[whole(small)] + [ANY] * 3,
            scratch=[pltpu.VMEM((128, 128), F32)]
            + [pltpu.VMEM(w.shape, LOW) for w in (w_qkv, w_out, w_up)]
            + [pltpu.SemaphoreType.DMA],
        )
        *self.units, unit_a, unit_b = call(
            unit_body,
            [shape((48, w)) for w in [*(c[0] for c in CHUNKS), total_a, total - total_a]],
            [mine, swap(other, 1)],
            info=self.info,
        )
        self.own = [unit_a, swap(unit_a, 4), unit_b, swap(unit_b, 2)]
        self.lines = [[swap(self.units[0], bit) for bit in (8, 16, 24)]]
        return down

    def step(self, call):
        outs = [shape((2, *a.shape)) for a in self.own[::2]]
        self.pair_a, self.pair_b = call(own_body, outs, self.own)
        self.far_a, self.far_b = swap(self.pair_a, 2), swap(self.pair_b, 4)

    def stack(self, call, index):
        width, cut = CHUNKS[index]
        a, b = call(
            functools.partial(stack_body, cut),
            [shape((3, 48, cut)), shape((3, 48, width - cut))],
            self.lines[index],
        )
        return a, swap(a, 4), b, swap(b, 2)

    def join(self, call, index, stacked):
        width, cut = CHUNKS[index]
        a, b = call(
            join_body, [shape((6, 48, cut)), shape((6, 48, width - cut))], stacked
        )
        return a, swap(a, 2), b, swap(b, 4)

    def finish(self, call, index, joined):
        width, cut = CHUNKS[index]
        at_a = sum(c for _, c in CHUNKS[:index])
        at_b = sum(w - c for w, c in CHUNKS[:index])
        z = Z_CODES[1:]
        codes_a = z + tuple(c ^ 2 for c in z)
        codes_b = z + tuple(c ^ 1 for c in z)
        plan = [
            (codes_a, 0, 0, cut),
            (tuple(c ^ 1 for c in codes_a), 0, 0, cut),
            (codes_b, 0, cut, width - cut),
            (tuple(c ^ 2 for c in codes_b), 0, cut, width - cut),
            ((0, 2), at_a, 0, cut),
            ((1, 3), at_a, 0, cut),
            ((0, 1), at_b, cut, width - cut),
            ((2, 3), at_b, cut, width - cut),
        ]
        (own,) = call(
            functools.partial(place_body, plan),
            [shape((D, width))],
            [*joined, self.pair_a, self.far_a, self.pair_b, self.far_b],
            info=self.info,
            in_specs=[ANY] * 8,
            scratch=[pltpu.SemaphoreType.DMA],
        )
        return own, swap(own, 1)

    def first_weights(self, call):
        stacked = self.stack(call, 0)
        joined = self.join(call, 0, stacked)
        self.lines.append([swap(self.units[1], bit) for bit in (8, 16, 24)])
        first = self.finish(call, 0, joined)
        self.stacked = self.stack(call, 1)
        return first

    def middle(self, call):
        self.joined = self.join(call, 1, self.stacked)

    def second_weights(self, call):
        return self.finish(call, 1, self.joined)

    def pieces(self, width_a, width_b):
        return [shape((8, 48, w)) for w in (width_a, width_a, width_b, width_b)]

    def job(self, call, parts, body, outs):
        send_a, keep_a, send_b, keep_b = parts
        width_a, width_b = keep_a.shape[2], keep_b.shape[2]
        width = width_a + width_b
        far_a, far_b = swap(send_a, 2), swap(send_b, 4)
        yield
        send_a, keep_a, send_b, keep_b = call(
            first_sum_body,
            [shape((4, 48, w)) for w in (width_a, width_a, width_b, width_b)],
            [far_a, keep_a, far_b, keep_b],
        )
        far_a, far_b = swap(send_a, 4), swap(send_b, 2)
        yield
        own, *lines = call(
            second_sum_body, [shape((48, width))] * 4, [far_a, keep_a, far_b, keep_b]
        )
        lines = [swap(line, bit) for line, bit in zip(lines, (8, 16, 24))]
        yield
        mine, other = call(
            last_sum_body,
            [shape((24, width), F32)] * 2,
            [own, *lines],
            info=self.info,
            scratch=[pltpu.VMEM((48, width), F32)],
        )
        other = swap(other, 1)
        yield
        self.outs.append(
            call(body, outs, [mine, other], info=self.info)
        )

    def begin(self, call, parts, body, outs):
        job = self.job(call, parts, body, outs)
        next(job)
        self.jobs.append(job)

    def pump(self, call):
        self.jobs = [job for job in self.jobs if next(job, self) is not self]

    def results(self, call):
        while self.jobs:
            self.pump(call)
        (down,), (up, out), (qkv, vec) = self.outs
        return down, up, out, qkv, vec

    def reduce_down(self, call, dy, gated, bundle):
        self.outs = []
        far = swap(bundle, 1)
        out_a = pl.BlockSpec((8, 48, STEP), lambda i, _: (0, 0, jnp.minimum(i, 1)))
        out_b = pl.BlockSpec((8, 48, STEP), lambda i, _: (0, 0, jnp.maximum(i - 2, 0)))
        parts = call(
            functools.partial(down_grad_body, 2),
            self.pieces(768, 768),
            [dy, far, gated, far],
            info=self.info,
            grid=(4,),
            in_specs=[whole(dy), fixed(far, D), cols(gated, STEP), cols(far, STEP, 2)],
            out_specs=[out_a, out_a, out_b, out_b],
            scratch=[pltpu.VMEM((D, STEP), F32)],
            us=7,
        )
        self.begin(call, parts, merge_down_body, [shape((24, FF), F32)])

    def reduce_up(self, call, normed, raised, up_bundle, mixed, out_bundle):
        up_far, out_far = swap(up_bundle, 1), swap(out_bundle, 1)

        def part(array, offset=0):
            return pl.BlockSpec(
                (array.shape[0], STEP), lambda i, _: (0, offset + jnp.minimum(i, 3))
            )

        out_a = pl.BlockSpec((8, 48, STEP), lambda i, _: (0, 0, jnp.minimum(i, 1)))
        out_b = pl.BlockSpec((8, 48, STEP), lambda i, _: (0, 0, jnp.maximum(i - 2, 0)))
        parts = call(
            up_grad_body,
            self.pieces(768, 1152),
            [normed, up_far, raised, up_far, out_bundle, out_far, mixed, out_far],
            info=self.info,
            grid=(5,),
            in_specs=[
                whole(normed), fixed(up_far, D), part(raised), part(up_far, 2),
                fixed(out_bundle, D), fixed(out_far, D), whole(mixed), fixed(out_far, HALF, 2),
            ],
            out_specs=[out_a, out_a, out_b, out_b],
            scratch=[pltpu.VMEM((D, STEP), F32)],
            us=10,
        )
        self.begin(
            call, parts, merge_up_body, [shape((24, FF), F32), shape((24, D), F32)]
        )

    def reduce_qkv(self, call, normed, triple, bundle, block):
        parts = call(
            qkv_grad_body,
            self.pieces(768, 512),
            [normed, triple, swap(bundle, 1), block],
            info=self.info,
            scratch=[pltpu.VMEM((D, STEP), F32)],
            us=6.2,
        )
        self.begin(
            call, parts, merge_qkv_body, [shape((24, 3 * D), F32), shape((24, 128), F32)]
        )


def shards(count, tokens, lengths, source, cotangent, w_qkv, w_out, w_up, w_down, *small):
    (
        gain_one, shift_one, bias_query, bias_value, bias_out, gain_two, shift_two,
        bias_up, bias_down,
    ) = small
    seqs, slots = tokens.shape[:2]
    rows = seqs * slots
    share = gain_one.shape[0]
    call = Chain()
    comm = GridComm() if count == 32 else WholeComm(count)
    visible = jnp.where(source == 1, lengths, IMG_LEN)
    tokens = tokens.reshape(rows, D)

    act = shape((rows, D))
    act_f = shape((rows, D), F32)
    half = shape((rows, HALF))
    triple = shape((rows, 3 * HALF))
    wide = shape((rows, WIDE))
    bundle = shape((rows, D + WIDE))

    small = jnp.stack(
        [gain_one, shift_one, gain_two, shift_two, bias_out, bias_down, bias_query, bias_value]
    )
    small = jnp.concatenate([small, bias_up.reshape(4, share)])
    down = comm.weights(call, small, w_qkv, w_out.T, w_up, w_down.T)
    dy, dy_sum = call(
        functools.partial(start_body, slots),
        [act, shape((8, D), F32)],
        [cotangent.reshape(rows, D)],
        info=visible,
    )
    comm.step(call)
    first = comm.first_weights(call)
    normed_one, *qkv, vecs = call(
        qkv_body,
        [act, triple, triple, shape((16, D), F32)],
        [tokens, *first],
        info=comm.info,
        us=6.5,
    )
    comm.middle(call)
    bias_up = vecs[8:12].reshape(4, count, share).transpose(1, 0, 2).reshape(2, 1, WIDE)
    up_own, up_par = comm.order(bias_up[0], bias_up[1])
    o_own, o_par = [
        call(functools.partial(attend_body, slots), [half], [part], info=visible, us=4.3)[0]
        for part in qkv
    ]
    second = comm.second_weights(call)
    out_specs = [fixed(w, HALF) for w in second]
    hidden, normed_two = call(
        hidden_body,
        [act_f, act],
        [tokens, vecs, o_own, o_par, *second],
        in_specs=[whole(a) for a in (tokens, vecs, o_own, o_par)] + out_specs,
        us=4.4,
    )
    steps = WIDE // STEP
    up_specs = [cols(w, STEP, 1) for w in second]
    gate, step = cols(wide, STEP), cols(up_own, STEP)
    gated, *slope, down_bundle = call(
        raise_body,
        [wide] * 3 + [bundle],
        [normed_two, dy, up_own, up_par, *second],
        grid=(steps,),
        in_specs=[whole(act)] * 2 + [step] * 2 + up_specs,
        out_specs=[gate] * 3 + [whole(bundle)],
        us=11.3,
    )
    comm.reduce_down(call, dy, gated, down_bundle)
    down_specs = [
        pl.BlockSpec((D, STEP), lambda i, info: (0, info[1] * steps + i)),
        pl.BlockSpec((D, STEP), lambda i, info: (0, (1 - info[1]) * steps + i)),
    ]
    raised, up_sum_own, up_sum_par, up_bundle = call(
        raise_back_body,
        [wide] + [shape((1, WIDE), F32)] * 2 + [bundle],
        [dy, normed_two, *slope, down, down],
        info=comm.info,
        grid=(steps,),
        in_specs=[whole(act)] * 2 + [gate] * 2 + down_specs,
        out_specs=[gate, step, step, whole(bundle)],
        us=9,
    )
    comm.pump(call)
    out_bundle = shape((rows, D + HALF))
    grad_hidden, out_bundle, sums_two = call(
        functools.partial(hidden_back_body, steps),
        [act_f, out_bundle, shape((8, D), F32)],
        [dy, hidden, vecs, o_par, raised, up_bundle, *second],
        grid=(steps,),
        in_specs=[whole(act)] * 2
        + [whole(vecs), whole(o_par), gate, cols(up_bundle, STEP, 2)]
        + up_specs,
        out_specs=[whole(act), whole(out_bundle), pl.BlockSpec((8, D), lambda i: (0, 0))],
        scratch=[pltpu.VMEM((rows, D), F32)],
        us=10.7,
    )
    comm.pump(call)
    comm.reduce_up(call, normed_two, raised, up_bundle, o_own, out_bundle)
    grads = [None, None]
    for h in (1, 0):
        out = shape((rows, h * D + 3 * HALF))
        grads[h] = call(
            functools.partial(attend_back_body, slots, h * D),
            [out, shape((8, HALF), F32)],
            [normed_one, qkv[h], out_bundle, second[h]],
            info=visible,
            in_specs=[whole(normed_one), whole(triple), fixed(out_bundle, D), out_specs[h]],
            scratch=[pltpu.VMEM((rows, HALF), LOW)],
            us=9.5,
        )
        comm.pump(call)
    grad_own, grad_bundle = grads[0][0], grads[1][0]
    up_sum = jnp.concatenate(comm.order(up_sum_own[0], up_sum_par[0]))
    up_sum = up_sum.reshape(count, 4, share).transpose(1, 0, 2).reshape(4, D)
    grad_tokens, block = call(
        token_back_body,
        [act, shape((D, 128), F32)],
        [
            tokens, grad_hidden, vecs, sums_two, dy_sum, up_sum, grads[0][1], grads[1][1],
            grad_own, grad_bundle, *first,
        ],
        info=comm.info,
        in_specs=[
            whole(a)
            for a in (
                tokens, grad_hidden, vecs, sums_two, dy_sum, up_sum, grads[0][1], grads[1][1],
                grad_own, grad_bundle,
            )
        ]
        + [fixed(w, 3 * HALF) for w in first],
        scratch=[pltpu.VMEM((rows, D), F32), pltpu.VMEM((128, D), F32)],
        us=9.6,
    )
    comm.pump(call)
    comm.reduce_qkv(call, normed_one, grad_own, grad_bundle, block)
    (output,) = call(
        mix_body, [act], [hidden, vecs, gated, down_bundle, down], info=comm.info, us=4.7
    )
    g_down_t, g_up, g_out_t, g_qkv, g_vec = comm.results(call)
    (
        g_gain_one, g_shift_one, g_gain_two, g_shift_two, g_bias_out, g_bias_down, g_query, g_value,
    ) = [g_vec[:, i] for i in range(8)]
    return (
        output.reshape(seqs, slots, D),
        grad_tokens.reshape(seqs, slots, D),
        g_qkv,
        g_out_t.T,
        g_up,
        g_down_t.T,
        g_gain_one, g_shift_one, g_query, g_value, g_bias_out, g_gain_two, g_shift_two,
        g_vec[:, 8:12].T.reshape(4 * share),
        g_bias_down,
    )


def solution(mesh):
    row, tall, wide, vec = P("dp", None, None), P("dp", None), P(None, "dp"), P("dp")
    in_specs = (row, vec, vec, row, tall, wide, tall, wide) + (vec,) * 9
    out_specs = (row, row, tall, wide, tall, wide) + (vec,) * 9
    body = functools.partial(shards, mesh.shape["dp"])
    return jax.shard_map(
        body, mesh=mesh, in_specs=in_specs, out_specs=out_specs, check_vma=False
    )
```

time: 817 us -> 312 us (0.38)
  waiting for transfers between devices: 518 us -> 96.1 us
  matrix products: 124 us -> 0 us
  Pallas kernels: 0 us -> 119 us
  blocking collectives: 83.5 us -> 0 us
  starting transfers between devices: 0.49 us -> 50.4 us
  other arithmetic: 34.4 us -> 0.13 us
  local copies, waits for them, and re-layouts: 36.5 us -> 26.6 us
    reduce_scatter x4 -> x0, waiting for transfers between devices: 366 us -> none  [the longest x1 142 us: shards(): lax.psum_scatter(g_up, 'dp', scatter_dimension=0, tiled=True)]
    all_gather x4 -> x1, waiting for transfers between devices: 149 us -> 0.01 us  [weights(): down = lax.all_gather(w_down, 'dp', axis=0, tiled=True)]
    dot_general x36 -> x0, matrix products: 124 us -> none  [the longest x8 33.8 us: outer_sum(): jnp.einsum('spd,spe->de', group_rows, grad_rows, preferred_element_type=j...]
    pallas_call x0 -> x36, Pallas kernels: none -> 119 us  [__call__(): pl.pallas_call(run, out_shape=tuple(outs), grid_spec=pltpu.PrefetchScalar...]
    ppermute x0 -> x49, waiting for transfers between devices: none -> 96.1 us  [swap(): return lax.ppermute(value, 'dp', pairs)]
    unnamed x2 -> x0, blocking collectives: 83.5 us -> none
    ppermute x0 -> x49, starting transfers between devices: none -> 50.4 us  [swap(): return lax.ppermute(value, 'dp', pairs)]
    reduce_sum x11 -> x0, other arithmetic: 15 us -> none  [the longest x3 5.7 us: layer_norm(): return center * lax.rsqrt(spread + epsilon) * gain_vec + shift_vec]
  transfers between devices with their start and end apart: 8 -> 50, of which waited for: 7 -> 23; matrix products, arithmetic and copies ran while one was open for 18% -> 0% of each run, Pallas kernels for 0% -> 36%
where the time goes in v1:
time: 312 us; the launch traced here: 308 us
  Pallas kernels  119 us (38%)
  waiting for transfers between devices  96.1 us (31%)
  starting transfers between devices  50.4 us (16%)
  local copies, waits for them, and re-layouts  26.6 us (9%)
  between operations  15.3 us (5%)
    pallas_call x36, Pallas kernels, __call__(): pl.pallas_call(run, out_shape=tuple(outs), grid_spec=pltpu.PrefetchScalar...  119 us
    ppermute x49, waiting for transfers between devices, swap(): return lax.ppermute(value, 'dp', pairs)  96.1 us
    ppermute x49, starting transfers between devices, swap(): return lax.ppermute(value, 'dp', pairs)  50.4 us
    unnamed x132, local copies, waits for them, and re-layouts  22.9 us
  transfers between devices with their start and end apart: 50, of which 23 were waited for; matrix products, arithmetic and copies ran while one was open for 0% of the time, Pallas kernels for 36%

profile of v1, /device:TPU:0, one launch (start us, length us, event | category | flops | bytes accessed | tf_op | source)
XLA Modules:
  0.0 307.9 jit_solution(15980541672331877392)
XLA Ops:
  14.6 2.9 collective-permute-start.4
  17.6 1.5 collective-permute-start.5
  19.1 1.6 collective-permute-start.1
  20.7 2.6 collective-permute-start.2
  25.5 7.3 %collective-permute-done.2.refs_1_ = bf16[48,1280]{1,0:T(8,128)(2,1)S(1)} collective-permute-done((bf16[48,1280]{1,0:T(8,128)(2,1)S(1)}, bf16[48,1280]{1,0:T(8,128)(2,1)S(1)}, u32[]{:S(2)}, u32[]{:S(2)}) %collective-permute-start.2) | collective-permute-done | bytes 122912 | tf_op jit(solution)/shard_map/ppermute | solution.py:110
  33.9 5.6 %collective-permute-done.6.refs_1_ = bf16[3,48,640]{2,1,0:T(8,128)(2,1)S(1)} collective-permute-done((bf16[3,48,640]{2,1,0:T(8,128)(2,1)S(1)}, bf16[3,48,640]{2,1,0:T(8,128)(2,1)S(1)}, u32[]{:S(2)}, u32[]{:S(2)}) %collective-permute-start.6) | collective-permute-done | bytes 184352 | tf_op jit(solution)/shard_map/ppermute | solution.py:110
  39.5 1.3 collective-permute-done.7.refs_3_
  41.5 1.5 collective-permute-start.9
  43.0 1.5 collective-permute-start.10
  45.0 7.7 %collective-permute-done.11.refs_8_ = bf16[2,48,1536]{2,1,0:T(8,128)(2,1)S(1)} collective-permute-done((bf16[2,48,1536]{2,1,0:T(8,128)(2,1)S(1)}, bf16[2,48,1536]{2,1,0:T(8,128)(2,1)S(1)}, u32[]{:S(2)}, u32[]{:S(2)}) %collective-permute-start.11) | collective-permute-done | bytes 294944 | tf_op jit(solution)/shard_map/ppermute | solution.py:110
  54.9 1.9 collective-permute-start.13
  57.9 1.4 collective-permute-start.15
  59.4 6.2 %collective-permute-done.13.refs_0_ = bf16[48,1920]{1,0:T(8,128)(2,1)S(1)} collective-permute-done((bf16[48,1920]{1,0:T(8,128)(2,1)S(1)}, bf16[48,1920]{1,0:T(8,128)(2,1)S(1)}, u32[]{:S(2)}, u32[]{:S(2)}) %collective-permute-start.13) | collective-permute-done | bytes 184352 | tf_op jit(solution)/shard_map/ppermute | solution.py:110
  65.6 8.7 %collective-permute-done.14.refs_1_ = bf16[48,1920]{1,0:T(8,128)(2,1)S(1)} collective-permute-done((bf16[48,1920]{1,0:T(8,128)(2,1)S(1)}, bf16[48,1920]{1,0:T(8,128)(2,1)S(1)}, u32[]{:S(2)}, u32[]{:S(2)}) %collective-permute-start.14) | collective-permute-done | bytes 184352 | tf_op jit(solution)/shard_map/ppermute | solution.py:110
  75.9 1.6 collective-permute-start.16
  77.5 1.2 collective-permute-start.17
  78.7 7.9 %shard_map.288 = (bf16[640,768]{1,0:T(8,128)(2,1)S(1)}, bf16[640,1152]{1,0:T(8,128)(2,1)S(1)}, bf16[640,1152]{1,0:T(8,128)(2,1)S(1)}, f32[16,768]{1,0:T(8,128)S(1)}) custom-call(s32[2]{0:T(128)S(1)} %pad_add_fusion.refs_0_, bf16[640,768]{1,0:T(8,128)(2,1)S(1)} %bitcast.26, bf16[768,1280]{1,0:T(8,128)(2,1)S(1)} %shard_map.286.refs_3_.refs_2_.refs_11_, ...), custom_call_target="tpu_custom_call" | custom-call | flops 7150000128 | bytes 9154560 | tf_op jit(solution)/shard_map/pallas_call | solution.py:68
  88.8 4.3 %shard_map.290.refs_2_.refs_7_ = bf16[640,384]{1,0:T(8,128)(2,1)S(1)} custom-call(s32[2]{0:T(128)S(1)} %compare_select_fusion.refs_0_, bf16[640,1152]{1,0:T(8,128)(2,1)S(1)} %get-tuple-element.117.refs_1_.refs_2_, bf16[6,48,896]{2,1,0:T(8,128)(2,1)S(1)} %get-tuple-element.119.refs_2_.refs_3_), custom_call_target="tpu_custom_call" | custom-call | flops 4729999872 | bytes 2482176 | tf_op jit(solution)/shard_map/pallas_call | solution.py:68
  93.2 4.3 %shard_map.291.refs_9_.refs_3_ = bf16[640,384]{1,0:T(8,128)(2,1)S(1)} custom-call(s32[2]{0:T(128)S(1)} %compare_select_fusion.refs_0_, bf16[640,1152]{1,0:T(8,128)(2,1)S(1)} %get-tuple-element.120.refs_1_.refs_2_, bf16[640,384]{1,0:T(8,128)(2,1)S(1)} %shard_map.290.refs_2_.refs_7_), custom_call_target="tpu_custom_call" | custom-call | flops 4729999872 | bytes 2457600 | tf_op jit(solution)/shard_map/pallas_call | solution.py:68
  97.5 3.3 %collective-permute-done.19.refs_4_ = bf16[6,48,896]{2,1,0:T(8,128)(2,1)S(1)} collective-permute-done((bf16[6,48,896]{2,1,0:T(8,128)(2,1)S(1)}, bf16[6,48,896]{2,1,0:T(8,128)(2,1)S(1)}, u32[]{:S(2)}, u32[]{:S(2)}) %collective-permute-start.19) | collective-permute-done | bytes 516128 | tf_op jit(solution)/shard_map/ppermute | solution.py:110
  100.8 3.3 %collective-permute-done.18.refs_2_ = bf16[6,48,1024]{2,1,0:T(8,128)(2,1)S(1)} collective-permute-done((bf16[6,48,1024]{2,1,0:T(8,128)(2,1)S(1)}, bf16[6,48,1024]{2,1,0:T(8,128)(2,1)S(1)}, u32[]{:S(2)}, u32[]{:S(2)}) %collective-permute-start.18) | collective-permute-done | bytes 589856 | tf_op jit(solution)/shard_map/ppermute | solution.py:110
  104.1 1.3 shard_map.292.refs_4_.refs_6_
  106.0 6.5 %collective-permute-done.20.refs_5_.refs_7_.refs_4_ = bf16[768,1920]{1,0:T(8,128)(2,1)} collective-permute-done((bf16[768,1920]{1,0:T(8,128)(2,1)S(1)}, bf16[768,1920]{1,0:T(8,128)(2,1)}, u32[]{:S(2)}, u32[]{:S(2)}) %collective-permute-start.20) | collective-permute-done | bytes 2949152 | tf_op jit(solution)/shard_map/ppermute | solution.py:110
  113.5 1.2 copy-done.19
  115.8 4.5 %shard_map.293 = (f32[640,768]{1,0:T(8,128)S(1)}, bf16[640,768]{1,0:T(8,128)(2,1)S(1)}) custom-call(bf16[640,768]{1,0:T(8,128)(2,1)S(1)} %bitcast.27, f32[16,768]{1,0:T(8,128)S(1)} %get-tuple-element.116.refs_4_.refs_1_.refs_2_.refs_3_, bf16[640,384]{1,0:T(8,128)(2,1)S(1)} %copy-done.48, bf16[640,384]{1,0:T(8,128)(2,1)S(1)} %copy-done.11, ...), custom_call_target="tpu_custom_call" | custom-call | flops 4840000000 | bytes 13811712 | tf_op jit(solution)/shard_map/pallas_call | solution.py:68
  120.3 1.3 copy-done.39
  121.6 11.4 %shard_map.294 = (bf16[640,1536]{1,0:T(8,128)(2,1)S(1)}, bf16[640,1536]{1,0:T(8,128)(2,1)S(1)}, bf16[640,1536]{1,0:T(8,128)(2,1)S(1)}, bf16[640,2304]{1,0:T(8,128)(2,1)}) custom-call(bf16[640,768]{1,0:T(8,128)(2,1)S(1)} %get-tuple-element.123.refs_0_.refs_6_.refs_2_.refs_1_, bf16[640,768]{1,0:T(8,128)(2,1)S(1)} %copy-done.32, ...), custom_call_target="tpu_custom_call" | custom-call | flops 12430000128 | bytes 17707008 | tf_op jit(solution)/shard_map/pallas_call | solution.py:68
  133.2 5.4 %collective-permute-done.21.refs_2_.refs_4_ = bf16[640,2304]{1,0:T(8,128)(2,1)S(1)} collective-permute-done((bf16[640,2304]{1,0:T(8,128)(2,1)}, bf16[640,2304]{1,0:T(8,128)(2,1)S(1)}, u32[]{:S(2)}, u32[]{:S(2)}) %collective-permute-start.21) | collective-permute-done | bytes 2949152 | tf_op jit(solution)/shard_map/ppermute | solution.py:110
  138.6 7.1 %shard_map.295 = (bf16[8,48,768]{2,1,0:T(8,128)(2,1)S(1)}, bf16[8,48,768]{2,1,0:T(8,128)(2,1)S(1)}, bf16[8,48,768]{2,1,0:T(8,128)(2,1)S(1)}, bf16[8,48,768]{2,1,0:T(8,128)(2,1)S(1)}) custom-call(s32[2]{0:T(128)S(1)} %pad_add_fusion.refs_0_, bf16[640,768]{1,0:T(8,128)(2,1)S(1)} %copy-done.32, bf16[640,2304]{1,0:T(8,128)(2,1)S(1)} %collective-permute-done.21.refs_2_.refs_4_, ...), custom_call_target="tpu_custom_call" | custom-call | flops 7699999744 | bytes 13172736 | tf_op jit(solution)/shard_map/pallas_call | solution.py:68
  149.0 9.1 %shard_map.296 = (bf16[640,1536]{1,0:T(8,128)(2,1)S(1)}, f32[1,1536]{1,0:T(1,128)S(1)}, f32[1,1536]{1,0:T(1,128)S(1)}, bf16[640,2304]{1,0:T(8,128)(2,1)}) custom-call(s32[2]{0:T(128)S(1)} %pad_add_fusion.refs_0_, bf16[640,768]{1,0:T(8,128)(2,1)S(1)} %copy-done.33, bf16[640,768]{1,0:T(8,128)(2,1)S(1)} %copy-done.45, bf16[640,1536]{1,0:T(8,128)(2,1)} %copy-done.56, ...), custom_call_target="tpu_custom_call" | custom-call | flops 9900000256 | bytes 20852736 | tf_op jit(solution)/shard_map/pallas_call | solution.py:68
  158.3 3.7 %collective-permute-done.22.refs_0_ = bf16[8,48,768]{2,1,0:T(8,128)(2,1)S(1)} collective-permute-done((bf16[8,48,768]{2,1,0:T(8,128)(2,1)S(1)}, bf16[8,48,768]{2,1,0:T(8,128)(2,1)S(1)}, u32[]{:S(2)}, u32[]{:S(2)}) %collective-permute-start.22) | collective-permute-done | bytes 589856 | tf_op jit(solution)/shard_map/ppermute | solution.py:110
  164.4 10.6 %shard_map.298 = (f32[640,768]{1,0:T(8,128)S(1)}, bf16[640,1152]{1,0:T(8,128)(2,1)S(1)}, f32[8,768]{1,0:T(8,128)S(1)}) custom-call(bf16[640,768]{1,0:T(8,128)(2,1)S(1)} %copy-done.34, f32[640,768]{1,0:T(8,128)S(1)} %copy-done.40, f32[16,768]{1,0:T(8,128)S(1)} %get-tuple-element.116.refs_4_.refs_1_.refs_2_.refs_3_, bf16[640,384]{1,0:T(8,128)(2,1)S(1)} %copy-done.12, ...), custom_call_target="tpu_custom_call" | custom-call | flops 11770000384 | bytes 18063360 | tf_op jit(solution)/shard_map/pallas_call | solution.py:68
  175.0 1.3 copy-done.60
  176.5 1.7 collective-permute-start.27
  178.7 7.4 %collective-permute-done.26.refs_0_ = bf16[4,48,768]{2,1,0:T(8,128)(2,1)} collective-permute-done((bf16[4,48,768]{2,1,0:T(8,128)(2,1)}, bf16[4,48,768]{2,1,0:T(8,128)(2,1)}, u32[]{:S(2)}, u32[]{:S(2)}) %collective-permute-start.26) | collective-permute-done | bytes 294944 | tf_op jit(solution)/shard_map/ppermute | solution.py:110
  187.9 1.3 shard_map.299
  189.3 3.1 collective-permute-start.30
  192.3 1.3 collective-permute-start.31
  193.6 1.4 collective-permute-start.32
  195.1 10.1 %shard_map.300 = (bf16[8,48,768]{2,1,0:T(8,128)(2,1)S(1)}, bf16[8,48,768]{2,1,0:T(8,128)(2,1)S(1)}, bf16[8,48,1152]{2,1,0:T(8,128)(2,1)S(1)}, bf16[8,48,1152]{2,1,0:T(8,128)(2,1)S(1)}) custom-call(s32[2]{0:T(128)S(1)} %pad_add_fusion.refs_0_, bf16[640,768]{1,0:T(8,128)(2,1)S(1)} %copy-done.46, bf16[640,2304]{1,0:T(8,128)(2,1)} %collective-permute-done.24.refs_2_.refs_4_, ...), custom_call_target="tpu_custom_call" | custom-call | flops 11000000512 | bytes 16859136 | tf_op jit(solution)/shard_map/pallas_call | solution.py:68
  205.2 1.4 collective-permute-start.28
  207.3 1.4 copy-done.15
  208.6 9.4 %shard_map.301 = (bf16[640,1920]{1,0:T(8,128)(2,1)S(1)}, f32[8,384]{1,0:T(8,128)S(1)}) custom-call(s32[2]{0:T(128)S(1)} %compare_select_fusion.refs_0_, bf16[640,768]{1,0:T(8,128)(2,1)S(1)} %copy-done.59, bf16[640,1152]{1,0:T(8,128)(2,1)S(1)} %copy-done.53, bf16[640,1152]{1,0:T(8,128)(2,1)S(1)} %copy-done.15, ...), custom_call_target="tpu_custom_call" | custom-call | flops 10449999872 | bytes 9940992 | tf_op jit(solution)/shard_map/pallas_call | solution.py:68
  219.6 7.0 %collective-permute-done.29.refs_2_ = bf16[8,48,1152]{2,1,0:T(8,128)(2,1)S(1)} collective-permute-done((bf16[8,48,1152]{2,1,0:T(8,128)(2,1)S(1)}, bf16[8,48,1152]{2,1,0:T(8,128)(2,1)S(1)}, u32[]{:S(2)}, u32[]{:S(2)}) %collective-permute-start.29) | collective-permute-done | bytes 884768 | tf_op jit(solution)/shard_map/ppermute | solution.py:110
  227.9 1.4 collective-permute-start.35
  229.3 8.5 %shard_map.304 = (bf16[640,1152]{1,0:T(8,128)(2,1)S(1)}, f32[8,384]{1,0:T(8,128)S(1)}) custom-call(s32[2]{0:T(128)S(1)} %compare_select_fusion.refs_0_, bf16[640,768]{1,0:T(8,128)(2,1)S(1)} %copy-done.59, bf16[640,1152]{1,0:T(8,128)(2,1)S(1)} %copy-done.51, bf16[640,1152]{1,0:T(8,128)(2,1)S(1)} %copy-done.16, bf16[768,1920]{1,0:T(8,128)(2,1)S(1)} %copy-done.1, ...), custom_call_target="tpu_custom_call" | custom-call | flops 10449999872 | bytes 8663040 | tf_op jit(solution)/shard_map/pallas_call | solution.py:68
  237.9 1.3 shard_map.305.refs_4_
  240.9 2.4 collective-permute-start.38
  243.4 1.4 collective-permute-start.39
  244.8 8.9 %shard_map.307 = (bf16[640,768]{1,0:T(8,128)(2,1)}, f32[768,128]{1,0:T(8,128)S(1)}) custom-call(s32[2]{0:T(128)S(1)} %pad_add_fusion.refs_0_, bf16[640,768]{1,0:T(8,128)(2,1)S(1)} %bitcast.28, f32[640,768]{1,0:T(8,128)S(1)} %copy-done.61, f32[16,768]{1,0:T(8,128)S(1)} %get-tuple-element.116.refs_4_.refs_1_.refs_2_.refs_3_, ...), custom_call_target="tpu_custom_call" | custom-call | flops 10560000000 | bytes 12509184 | tf_op jit(solution)/shard_map/pallas_call | solution.py:68
  253.6 1.2 collective-permute-done.38.refs_3_
  255.6 4.3 %shard_map.309 = (bf16[8,48,768]{2,1,0:T(8,128)(2,1)S(1)}, bf16[8,48,768]{2,1,0:T(8,128)(2,1)S(1)}, bf16[8,48,512]{2,1,0:T(8,128)(2,1)S(1)}, bf16[8,48,512]{2,1,0:T(8,128)(2,1)S(1)}) custom-call(s32[2]{0:T(128)S(1)} %pad_add_fusion.refs_0_, bf16[640,768]{1,0:T(8,128)(2,1)S(1)} %copy-done.59, bf16[640,1152]{1,0:T(8,128)(2,1)S(1)} %get-tuple-element.154.refs_9_.refs_2_, ...), custom_call_target="tpu_custom_call" | custom-call | flops 6819999744 | bytes 7458816 | tf_op jit(solution)/shard_map/pallas_call | solution.py:68
  262.1 4.8 %shard_map.310.refs_3_ = bf16[640,768]{1,0:T(8,128)(2,1)} custom-call(s32[2]{0:T(128)S(1)} %pad_add_fusion.refs_0_, f32[640,768]{1,0:T(8,128)S(1)} %copy-done.41, f32[16,768]{1,0:T(8,128)S(1)} %get-tuple-element.116.refs_4_.refs_1_.refs_2_.refs_3_, bf16[640,1536]{1,0:T(8,128)(2,1)S(1)} %copy-done.43, bf16[640,2304]{1,0:T(8,128)(2,1)S(1)} %copy-done.13, ...), custom_call_target="tpu_custom_call" | custom-call | flops 5169999872 | bytes 13025280 | tf_op jit(solution)/shard_map/pallas_call | solution.py:68
  266.8 1.2 copy-done.26
  268.0 1.3 shard_map.311
  269.3 3.3 %collective-permute-done.41.refs_2_ = bf16[8,48,512]{2,1,0:T(8,128)(2,1)S(1)} collective-permute-done((bf16[8,48,512]{2,1,0:T(8,128)(2,1)S(1)}, bf16[8,48,512]{2,1,0:T(8,128)(2,1)S(1)}, u32[]{:S(2)}, u32[]{:S(2)}) %collective-permute-start.41) | collective-permute-done | bytes 393248 | tf_op jit(solution)/shard_map/ppermute | solution.py:110
  275.9 5.1 %collective-permute-done.44.refs_2_ = bf16[4,48,512]{2,1,0:T(8,128)(2,1)S(1)} collective-permute-done((bf16[4,48,512]{2,1,0:T(8,128)(2,1)S(1)}, bf16[4,48,512]{2,1,0:T(8,128)(2,1)S(1)}, u32[]{:S(2)}, u32[]{:S(2)}) %collective-permute-start.44) | collective-permute-done | bytes 196640 | tf_op jit(solution)/shard_map/ppermute | solution.py:110
  281.0 1.5 collective-permute-done.43.refs_0_
  282.6 2.6 collective-permute-start.45
  286.4 1.4 collective-permute-start.47
  287.8 1.2 collective-permute-done.45.refs_2_
  289.0 6.8 %collective-permute-done.46.refs_3_ = bf16[48,1280]{1,0:T(8,128)(2,1)S(1)} collective-permute-done((bf16[48,1280]{1,0:T(8,128)(2,1)S(1)}, bf16[48,1280]{1,0:T(8,128)(2,1)S(1)}, u32[]{:S(2)}, u32[]{:S(2)}) %collective-permute-start.46) | collective-permute-done | bytes 122912 | tf_op jit(solution)/shard_map/ppermute | solution.py:110
  296.5 1.3 collective-permute-done.48.refs_2_
  297.8 1.2 shard_map.315
  (228 shorter events, 44.9 us)
Async XLA Ops:
  7.2 139.4 %all-gather.2.cloned.1.call-start = ((), (), s32[]{:S(2)}) async-start(), calls=%async_computation | async-start | bytes 4866048 | tf_op jit(solution)/shard_map/all_gather | solution.py:632
  12.5 1.5 collective-permute-start
  14.6 9.9 %collective-permute-start.4 = (bf16[48,1664]{1,0:T(8,128)(2,1)S(1)}, bf16[48,1664]{1,0:T(8,128)(2,1)S(1)}, u32[]{:S(2)}, u32[]{:S(2)}) collective-permute-start(bf16[48,1664]{1,0:T(8,128)(2,1)S(1)} %get-tuple-element.105.refs_0_), channel_id=1, source_target_pairs={{0,4},{1,5},{2,6},{3,7},{4,0},{5,1},{6,2},{7,3},{8,12},{9,13},{10,... | collective-permute-start | bytes 479240 | tf_op jit(solution)/shard_map/ppermute | solution.py:110
  17.6 6.9 %collective-permute-start.5 = (bf16[48,1536]{1,0:T(8,128)(2,1)S(1)}, bf16[48,1536]{1,0:T(8,128)(2,1)S(1)}, u32[]{:S(2)}, u32[]{:S(2)}) collective-permute-start(bf16[48,1536]{1,0:T(8,128)(2,1)S(1)} %get-tuple-element.106.refs_2_), channel_id=1, source_target_pairs={{0,2},{1,3},{2,0},{3,1},{4,6},{5,7},{6,4},{7,5},{8,10},{9,11},{10,... | collective-permute-start | bytes 442376 | tf_op jit(solution)/shard_map/ppermute | solution.py:110
  19.1 6.4 %collective-permute-start.1 = (bf16[48,1280]{1,0:T(8,128)(2,1)S(1)}, bf16[48,1280]{1,0:T(8,128)(2,1)S(1)}, u32[]{:S(2)}, u32[]{:S(2)}) collective-permute-start(bf16[48,1280]{1,0:T(8,128)(2,1)S(1)} %get-tuple-element.104.refs_2_), channel_id=1, source_target_pairs={{0,8},{1,9},{2,10},{3,11},{4,12},{5,13},{6,14},{7,15},{8,0},{9,1},... | collective-permute-start | bytes 368648 | tf_op jit(solution)/shard_map/ppermute | solution.py:110
  20.7 12.1 %collective-permute-start.2 = (bf16[48,1280]{1,0:T(8,128)(2,1)S(1)}, bf16[48,1280]{1,0:T(8,128)(2,1)S(1)}, u32[]{:S(2)}, u32[]{:S(2)}) collective-permute-start(bf16[48,1280]{1,0:T(8,128)(2,1)S(1)} %get-tuple-element.104.refs_2_), channel_id=1, source_target_pairs={{0,16},{1,17},{2,18},{3,19},{4,20},{5,21},{6,22},{7,23},{8,24},{9,... | collective-permute-start | bytes 368648 | tf_op jit(solution)/shard_map/ppermute | solution.py:110
  23.3 9.5 %collective-permute-start.3 = (bf16[48,1280]{1,0:T(8,128)(2,1)S(1)}, bf16[48,1280]{1,0:T(8,128)(2,1)S(1)}, u32[]{:S(2)}, u32[]{:S(2)}) collective-permute-start(bf16[48,1280]{1,0:T(8,128)(2,1)S(1)} %get-tuple-element.104.refs_2_), channel_id=1, source_target_pairs={{0,24},{1,25},{2,26},{3,27},{4,28},{5,29},{6,30},{7,31},{8,16},{9,... | collective-permute-start | bytes 368648 | tf_op jit(solution)/shard_map/ppermute | solution.py:110
  25.5 28.2 %copy-start.6 = (bf16[2,48,1536]{2,1,0:T(8,128)(2,1)}, bf16[2,48,1536]{2,1,0:T(8,128)(2,1)S(1)}, u32[]{:S(2)}) copy-start(bf16[2,48,1536]{2,1,0:T(8,128)(2,1)S(1)} %get-tuple-element.108.refs_3_.refs_7_) | copy-start | bytes 884740
  32.8 6.7 %collective-permute-start.6 = (bf16[3,48,640]{2,1,0:T(8,128)(2,1)S(1)}, bf16[3,48,640]{2,1,0:T(8,128)(2,1)S(1)}, u32[]{:S(2)}, u32[]{:S(2)}) collective-permute-start(bf16[3,48,640]{2,1,0:T(8,128)(2,1)S(1)} %get-tuple-element.109.refs_0_.refs_4_), channel_id=1, source_target_pairs={{0,4},{1,5},{2,6},{3,7},{4,0},{5,1},{6,2},{7,3},{8,12},{9,13},{10,... | collective-permute-start | bytes 552968 | tf_op jit(solution)/shard_map/ppermute | solution.py:110
  33.4 7.4 %collective-permute-start.7 = (bf16[3,48,640]{2,1,0:T(8,128)(2,1)S(1)}, bf16[3,48,640]{2,1,0:T(8,128)(2,1)S(1)}, u32[]{:S(2)}, u32[]{:S(2)}) collective-permute-start(bf16[3,48,640]{2,1,0:T(8,128)(2,1)S(1)} %get-tuple-element.110.refs_2_), channel_id=1, source_target_pairs={{0,2},{1,3},{2,0},{3,1},{4,6},{5,7},{6,4},{7,5},{8,10},{9,11},{10,... | collective-permute-start | bytes 552968 | tf_op jit(solution)/shard_map/ppermute | solution.py:110
  40.9 12.8 %collective-permute-start.8 = (bf16[6,48,640]{2,1,0:T(8,128)(2,1)S(1)}, bf16[6,48,640]{2,1,0:T(8,128)(2,1)S(1)}, u32[]{:S(2)}, u32[]{:S(2)}) collective-permute-start(bf16[6,48,640]{2,1,0:T(8,128)(2,1)S(1)} %get-tuple-element.111.refs_1_.refs_9_), channel_id=1, source_target_pairs={{0,2},{1,3},{2,0},{3,1},{4,6},{5,7},{6,4},{7,5},{8,10},{9,11},{10,... | collective-permute-start | bytes 1105928 | tf_op jit(solution)/shard_map/ppermute | solution.py:110
  41.5 12.2 %collective-permute-start.9 = (bf16[6,48,640]{2,1,0:T(8,128)(2,1)S(1)}, bf16[6,48,640]{2,1,0:T(8,128)(2,1)S(1)}, u32[]{:S(2)}, u32[]{:S(2)}) collective-permute-start(bf16[6,48,640]{2,1,0:T(8,128)(2,1)S(1)} %get-tuple-element.112.refs_3_), channel_id=1, source_target_pairs={{0,4},{1,5},{2,6},{3,7},{4,0},{5,1},{6,2},{7,3},{8,12},{9,13},{10,... | collective-permute-start | bytes 1105928 | tf_op jit(solution)/shard_map/ppermute | solution.py:110
  43.0 10.7 %collective-permute-start.10 = (bf16[2,48,1664]{2,1,0:T(8,128)(2,1)S(1)}, bf16[2,48,1664]{2,1,0:T(8,128)(2,1)S(1)}, u32[]{:S(2)}, u32[]{:S(2)}) collective-permute-start(bf16[2,48,1664]{2,1,0:T(8,128)(2,1)S(1)} %get-tuple-element.113.refs_5_), channel_id=1, source_target_pairs={{0,2},{1,3},{2,0},{3,1},{4,6},{5,7},{6,4},{7,5},{8,10},{9,11},{10,... | collective-permute-start | bytes 958472 | tf_op jit(solution)/shard_map/ppermute | solution.py:110
  44.5 8.2 %collective-permute-start.11 = (bf16[2,48,1536]{2,1,0:T(8,128)(2,1)S(1)}, bf16[2,48,1536]{2,1,0:T(8,128)(2,1)S(1)}, u32[]{:S(2)}, u32[]{:S(2)}) collective-permute-start(bf16[2,48,1536]{2,1,0:T(8,128)(2,1)S(1)} %get-tuple-element.108.refs_3_.refs_7_), channel_id=1, source_target_pairs={{0,4},{1,5},{2,6},{3,7},{4,0},{5,1},{6,2},{7,3},{8,12},{9,13},{10,... | collective-permute-start | bytes 884744 | tf_op jit(solution)/shard_map/ppermute | solution.py:110
  54.8 23.9 %copy-start.2 = (bf16[768,1280]{1,0:T(8,128)(2,1)}, bf16[768,1280]{1,0:T(8,128)(2,1)S(1)}, u32[]{:S(2)}) copy-start(bf16[768,1280]{1,0:T(8,128)(2,1)S(1)} %shard_map.286.refs_3_.refs_2_.refs_11_) | copy-start | bytes 5898244
  54.8 23.9 %collective-permute-start.12 = (bf16[768,1280]{1,0:T(8,128)(2,1)S(1)}, bf16[768,1280]{1,0:T(8,128)(2,1)}, u32[]{:S(2)}, u32[]{:S(2)}) collective-permute-start(bf16[768,1280]{1,0:T(8,128)(2,1)S(1)} %shard_map.286.refs_3_.refs_2_.refs_11_), channel_id=1, source_target_pairs={{0,1},{1,0},{2,3},{3,2},{4,5},{5,4},{6,7},{7,6},{8,9},{9,8},{10,11... | collective-permute-start | bytes 5898248 | tf_op jit(solution)/shard_map/ppermute | solution.py:110
  54.9 10.7 %collective-permute-start.13 = (bf16[48,1920]{1,0:T(8,128)(2,1)S(1)}, bf16[48,1920]{1,0:T(8,128)(2,1)S(1)}, u32[]{:S(2)}, u32[]{:S(2)}) collective-permute-start(bf16[48,1920]{1,0:T(8,128)(2,1)S(1)} %get-tuple-element.114), channel_id=1, source_target_pairs={{0,8},{1,9},{2,10},{3,11},{4,12},{5,13},{6,14},{7,15},{8,0},{9,1},... | collective-permute-start | bytes 552968 | tf_op jit(solution)/shard_map/ppermute | solution.py:110
  56.8 17.4 %collective-permute-start.14 = (bf16[48,1920]{1,0:T(8,128)(2,1)S(1)}, bf16[48,1920]{1,0:T(8,128)(2,1)S(1)}, u32[]{:S(2)}, u32[]{:S(2)}) collective-permute-start(bf16[48,1920]{1,0:T(8,128)(2,1)S(1)} %get-tuple-element.114), channel_id=1, source_target_pairs={{0,16},{1,17},{2,18},{3,19},{4,20},{5,21},{6,22},{7,23},{8,24},{9,... | collective-permute-start | bytes 552968 | tf_op jit(solution)/shard_map/ppermute | solution.py:110
  57.9 16.3 %collective-permute-start.15 = (bf16[48,1920]{1,0:T(8,128)(2,1)S(1)}, bf16[48,1920]{1,0:T(8,128)(2,1)S(1)}, u32[]{:S(2)}, u32[]{:S(2)}) collective-permute-start(bf16[48,1920]{1,0:T(8,128)(2,1)S(1)} %get-tuple-element.114), channel_id=1, source_target_pairs={{0,24},{1,25},{2,26},{3,27},{4,28},{5,29},{6,30},{7,31},{8,16},{9,... | collective-permute-start | bytes 552968 | tf_op jit(solution)/shard_map/ppermute | solution.py:110
  59.4 19.4 %copy-start.18 = (bf16[2,320,768]{2,1,0:T(8,128)(2,1)S(1)}, bf16[2,320,768]{2,1,0:T(8,128)(2,1)}, u32[]{:S(2)}) copy-start(bf16[2,320,768]{2,1,0:T(8,128)(2,1)} %param.17) | copy-start | bytes 2949124
  75.9 10.8 %collective-permute-start.16 = (bf16[3,48,1024]{2,1,0:T(8,128)(2,1)S(1)}, bf16[3,48,1024]{2,1,0:T(8,128)(2,1)S(1)}, u32[]{:S(2)}, u32[]{:S(2)}) collective-permute-start(bf16[3,48,1024]{2,1,0:T(8,128)(2,1)S(1)} %get-tuple-element.118.refs_0_), channel_id=1, source_target_pairs={{0,4},{1,5},{2,6},{3,7},{4,0},{5,1},{6,2},{7,3},{8,12},{9,13},{10,... | collective-permute-start | bytes 884744 | tf_op jit(solution)/shard_map/ppermute | solution.py:110
  77.5 9.2 %collective-permute-start.17 = (bf16[3,48,896]{2,1,0:T(8,128)(2,1)S(1)}, bf16[3,48,896]{2,1,0:T(8,128)(2,1)S(1)}, u32[]{:S(2)}, u32[]{:S(2)}) collective-permute-start(bf16[3,48,896]{2,1,0:T(8,128)(2,1)S(1)} %get-tuple-element.115.refs_4_.refs_2_), channel_id=1, source_target_pairs={{0,2},{1,3},{2,0},{3,1},{4,6},{5,7},{6,4},{7,5},{8,10},{9,11},{10,... | collective-permute-start | bytes 774152 | tf_op jit(solution)/shard_map/ppermute | solution.py:110
  87.6 16.6 %collective-permute-start.18 = (bf16[6,48,1024]{2,1,0:T(8,128)(2,1)S(1)}, bf16[6,48,1024]{2,1,0:T(8,128)(2,1)S(1)}, u32[]{:S(2)}, u32[]{:S(2)}) collective-permute-start(bf16[6,48,1024]{2,1,0:T(8,128)(2,1)S(1)} %get-tuple-element.121.refs_1_), channel_id=1, source_target_pairs={{0,2},{1,3},{2,0},{3,1},{4,6},{5,7},{6,4},{7,5},{8,10},{9,11},{10,... | collective-permute-start | bytes 1769480 | tf_op jit(solution)/shard_map/ppermute | solution.py:110
  88.4 12.4 %collective-permute-start.19 = (bf16[6,48,896]{2,1,0:T(8,128)(2,1)S(1)}, bf16[6,48,896]{2,1,0:T(8,128)(2,1)S(1)}, u32[]{:S(2)}, u32[]{:S(2)}) collective-permute-start(bf16[6,48,896]{2,1,0:T(8,128)(2,1)S(1)} %get-tuple-element.119.refs_2_.refs_3_), channel_id=1, source_target_pairs={{0,4},{1,5},{2,6},{3,7},{4,0},{5,1},{6,2},{7,3},{8,12},{9,13},{10,... | collective-permute-start | bytes 1548296 | tf_op jit(solution)/shard_map/ppermute | solution.py:110
  105.5 14.8 %copy-start = (bf16[768,1920]{1,0:T(8,128)(2,1)}, bf16[768,1920]{1,0:T(8,128)(2,1)S(1)}, u32[]{:S(2)}) copy-start(bf16[768,1920]{1,0:T(8,128)(2,1)S(1)} %shard_map.292.refs_4_.refs_6_) | copy-start | bytes 8847364
  105.5 7.0 %collective-permute-start.20 = (bf16[768,1920]{1,0:T(8,128)(2,1)S(1)}, bf16[768,1920]{1,0:T(8,128)(2,1)}, u32[]{:S(2)}, u32[]{:S(2)}) collective-permute-start(bf16[768,1920]{1,0:T(8,128)(2,1)S(1)} %shard_map.292.refs_4_.refs_6_), channel_id=1, source_target_pairs={{0,1},{1,0},{2,3},{3,2},{4,5},{5,4},{6,7},{7,6},{8,9},{9,8},{10,11... | collective-permute-start | bytes 8847368 | tf_op jit(solution)/shard_map/ppermute | solution.py:110
  121.6 11.4 %copy-start.44 = (bf16[640,768]{1,0:T(8,128)(2,1)}, bf16[640,768]{1,0:T(8,128)(2,1)S(1)}, u32[]{:S(2)}) copy-start(bf16[640,768]{1,0:T(8,128)(2,1)S(1)} %get-tuple-element.123.refs_0_.refs_6_.refs_2_.refs_1_) | copy-start | bytes 2949124
  133.0 12.8 %copy-start.42 = (bf16[640,1536]{1,0:T(8,128)(2,1)}, bf16[640,1536]{1,0:T(8,128)(2,1)S(1)}, u32[]{:S(2)}) copy-start(bf16[640,1536]{1,0:T(8,128)(2,1)S(1)} %get-tuple-element.125.refs_3_.refs_5_) | copy-start | bytes 5898244
  133.0 12.8 %copy-start.56 = (bf16[640,1536]{1,0:T(8,128)(2,1)}, bf16[640,1536]{1,0:T(8,128)(2,1)S(1)}, u32[]{:S(2)}) copy-start(bf16[640,1536]{1,0:T(8,128)(2,1)S(1)} %get-tuple-element.128.refs_3_) | copy-start | bytes 5898244
  133.0 12.8 %copy-start.57 = (bf16[640,1536]{1,0:T(8,128)(2,1)}, bf16[640,1536]{1,0:T(8,128)(2,1)S(1)}, u32[]{:S(2)}) copy-start(bf16[640,1536]{1,0:T(8,128)(2,1)S(1)} %get-tuple-element.129.refs_4_) | copy-start | bytes 5898244
  133.0 5.7 %collective-permute-start.21 = (bf16[640,2304]{1,0:T(8,128)(2,1)}, bf16[640,2304]{1,0:T(8,128)(2,1)S(1)}, u32[]{:S(2)}, u32[]{:S(2)}) collective-permute-start(bf16[640,2304]{1,0:T(8,128)(2,1)} %get-tuple-element.126.refs_4_), channel_id=1, source_target_pairs={{0,1},{1,0},{2,3},{3,2},{4,5},{5,4},{6,7},{7,6},{8,9},{9,8},{10,11... | collective-permute-start | bytes 8847368 | tf_op jit(solution)/shard_map/ppermute | solution.py:110
  146.6 15.4 %collective-permute-start.22 = (bf16[8,48,768]{2,1,0:T(8,128)(2,1)S(1)}, bf16[8,48,768]{2,1,0:T(8,128)(2,1)S(1)}, u32[]{:S(2)}, u32[]{:S(2)}) collective-permute-start(bf16[8,48,768]{2,1,0:T(8,128)(2,1)S(1)} %get-tuple-element.130.refs_7_), channel_id=1, source_target_pairs={{0,2},{1,3},{2,0},{3,1},{4,6},{5,7},{6,4},{7,5},{8,10},{9,11},{10,... | collective-permute-start | bytes 1769480 | tf_op jit(solution)/shard_map/ppermute | solution.py:110
  146.6 15.4 %collective-permute-start.23 = (bf16[8,48,768]{2,1,0:T(8,128)(2,1)S(1)}, bf16[8,48,768]{2,1,0:T(8,128)(2,1)S(1)}, u32[]{:S(2)}, u32[]{:S(2)}) collective-permute-start(bf16[8,48,768]{2,1,0:T(8,128)(2,1)S(1)} %get-tuple-element.134), channel_id=1, source_target_pairs={{0,4},{1,5},{2,6},{3,7},{4,0},{5,1},{6,2},{7,3},{8,12},{9,13},{10,... | collective-permute-start | bytes 1769480 | tf_op jit(solution)/shard_map/ppermute | solution.py:110
  149.0 13.0 %copy-start.30 = (bf16[8,48,768]{2,1,0:T(8,128)(2,1)S(1)}, bf16[8,48,768]{2,1,0:T(8,128)(2,1)}, u32[]{:S(2)}) copy-start(bf16[8,48,768]{2,1,0:T(8,128)(2,1)} %copy-done.29) | copy-start | bytes 1769476
  158.1 36.9 %collective-permute-start.24 = (bf16[640,2304]{1,0:T(8,128)(2,1)}, bf16[640,2304]{1,0:T(8,128)(2,1)}, u32[]{:S(2)}, u32[]{:S(2)}) collective-permute-start(bf16[640,2304]{1,0:T(8,128)(2,1)} %get-tuple-element.132.refs_5_), channel_id=1, source_target_pairs={{0,1},{1,0},{2,3},{3,2},{4,5},{5,4},{6,7},{7,6},{8,9},{9,8},{10,11... | collective-permute-start | bytes 8847368 | tf_op jit(solution)/shard_map/ppermute | solution.py:110
  176.3 18.8 %copy-start.14 = (bf16[640,1152]{1,0:T(8,128)(2,1)}, bf16[640,1152]{1,0:T(8,128)(2,1)S(1)}, u32[]{:S(2)}) copy-start(bf16[640,1152]{1,0:T(8,128)(2,1)S(1)} %get-tuple-element.138.refs_5_.refs_3_) | copy-start | bytes 4423684
  176.3 18.7 %collective-permute-start.25 = (bf16[640,1152]{1,0:T(8,128)(2,1)S(1)}, bf16[640,1152]{1,0:T(8,128)(2,1)S(1)}, u32[]{:S(2)}, u32[]{:S(2)}) collective-permute-start(bf16[640,1152]{1,0:T(8,128)(2,1)S(1)} %get-tuple-element.138.refs_5_.refs_3_), channel_id=1, source_target_pairs={{0,1},{1,0},{2,3},{3,2},{4,5},{5,4},{6,7},{7,6},{8,9},{9,8},{10,11... | collective-permute-start | bytes 4423688 | tf_op jit(solution)/shard_map/ppermute | solution.py:110
  176.3 9.7 %collective-permute-start.26 = (bf16[4,48,768]{2,1,0:T(8,128)(2,1)}, bf16[4,48,768]{2,1,0:T(8,128)(2,1)}, u32[]{:S(2)}, u32[]{:S(2)}) collective-permute-start(bf16[4,48,768]{2,1,0:T(8,128)(2,1)} %get-tuple-element.137.refs_8_), channel_id=1, source_target_pairs={{0,4},{1,5},{2,6},{3,7},{4,0},{5,1},{6,2},{7,3},{8,12},{9,13},{10,... | collective-permute-start | bytes 884744 | tf_op jit(solution)/shard_map/ppermute | solution.py:110
  176.5 9.5 %collective-permute-start.27 = (bf16[4,48,768]{2,1,0:T(8,128)(2,1)S(1)}, bf16[4,48,768]{2,1,0:T(8,128)(2,1)}, u32[]{:S(2)}, u32[]{:S(2)}) collective-permute-start(bf16[4,48,768]{2,1,0:T(8,128)(2,1)S(1)} %get-tuple-element.140), channel_id=1, source_target_pairs={{0,2},{1,3},{2,0},{3,1},{4,6},{5,7},{6,4},{7,5},{8,10},{9,11},{10,... | collective-permute-start | bytes 884744 | tf_op jit(solution)/shard_map/ppermute | solution.py:110
  189.3 28.8 %collective-permute-start.30 = (bf16[48,1536]{1,0:T(8,128)(2,1)S(1)}, bf16[48,1536]{1,0:T(8,128)(2,1)S(1)}, u32[]{:S(2)}, u32[]{:S(2)}) collective-permute-start(bf16[48,1536]{1,0:T(8,128)(2,1)S(1)} %get-tuple-element.148), channel_id=1, source_target_pairs={{0,8},{1,9},{2,10},{3,11},{4,12},{5,13},{6,14},{7,15},{8,0},{9,1},... | collective-permute-start | bytes 442376 | tf_op jit(solution)/shard_map/ppermute | solution.py:110
  192.3 25.8 %collective-permute-start.31 = (bf16[48,1536]{1,0:T(8,128)(2,1)S(1)}, bf16[48,1536]{1,0:T(8,128)(2,1)S(1)}, u32[]{:S(2)}, u32[]{:S(2)}) collective-permute-start(bf16[48,1536]{1,0:T(8,128)(2,1)S(1)} %get-tuple-element.149), channel_id=1, source_target_pairs={{0,16},{1,17},{2,18},{3,19},{4,20},{5,21},{6,22},{7,23},{8,24},{9,... | collective-permute-start | bytes 442376 | tf_op jit(solution)/shard_map/ppermute | solution.py:110
  193.6 24.5 %collective-permute-start.32 = (bf16[48,1536]{1,0:T(8,128)(2,1)S(1)}, bf16[48,1536]{1,0:T(8,128)(2,1)S(1)}, u32[]{:S(2)}, u32[]{:S(2)}) collective-permute-start(bf16[48,1536]{1,0:T(8,128)(2,1)S(1)} %get-tuple-element.150), channel_id=1, source_target_pairs={{0,24},{1,25},{2,26},{3,27},{4,28},{5,29},{6,30},{7,31},{8,16},{9,... | collective-permute-start | bytes 442376 | tf_op jit(solution)/shard_map/ppermute | solution.py:110
  195.1 12.2 %copy-start.53 = (bf16[640,1152]{1,0:T(8,128)(2,1)S(1)}, bf16[640,1152]{1,0:T(8,128)(2,1)}, u32[]{:S(2)}) copy-start(bf16[640,1152]{1,0:T(8,128)(2,1)} %copy-done.52) | copy-start | bytes 4423684
  195.1 12.2 %copy-start.59 = (bf16[640,768]{1,0:T(8,128)(2,1)S(1)}, bf16[640,768]{1,0:T(8,128)(2,1)}, u32[]{:S(2)}) copy-start(bf16[640,768]{1,0:T(8,128)(2,1)} %copy-done.58) | copy-start | bytes 2949124
  205.2 14.5 %collective-permute-start.28 = (bf16[8,48,768]{2,1,0:T(8,128)(2,1)S(1)}, bf16[8,48,768]{2,1,0:T(8,128)(2,1)S(1)}, u32[]{:S(2)}, u32[]{:S(2)}) collective-permute-start(bf16[8,48,768]{2,1,0:T(8,128)(2,1)S(1)} %get-tuple-element.144.refs_5_), channel_id=1, source_target_pairs={{0,2},{1,3},{2,0},{3,1},{4,6},{5,7},{6,4},{7,5},{8,10},{9,11},{10,... | collective-permute-start | bytes 1769480 | tf_op jit(solution)/shard_map/ppermute | solution.py:110
  206.5 20.1 %collective-permute-start.29 = (bf16[8,48,1152]{2,1,0:T(8,128)(2,1)S(1)}, bf16[8,48,1152]{2,1,0:T(8,128)(2,1)S(1)}, u32[]{:S(2)}, u32[]{:S(2)}) collective-permute-start(bf16[8,48,1152]{2,1,0:T(8,128)(2,1)S(1)} %get-tuple-element.146), channel_id=1, source_target_pairs={{0,4},{1,5},{2,6},{3,7},{4,0},{5,1},{6,2},{7,3},{8,12},{9,13},{10,... | collective-permute-start | bytes 2654216 | tf_op jit(solution)/shard_map/ppermute | solution.py:110
  218.1 37.5 %collective-permute-start.33 = (bf16[640,1920]{1,0:T(8,128)(2,1)S(1)}, bf16[640,1920]{1,0:T(8,128)(2,1)S(1)}, u32[]{:S(2)}, u32[]{:S(2)}) collective-permute-start(bf16[640,1920]{1,0:T(8,128)(2,1)S(1)} %get-tuple-element.155.refs_10_), channel_id=1, source_target_pairs={{0,1},{1,0},{2,3},{3,2},{4,5},{5,4},{6,7},{7,6},{8,9},{9,8},{10,11... | collective-permute-start | bytes 7372808 | tf_op jit(solution)/shard_map/ppermute | solution.py:110
  218.2 11.2 %copy-start.16 = (bf16[640,1152]{1,0:T(8,128)(2,1)S(1)}, bf16[640,1152]{1,0:T(8,128)(2,1)}, u32[]{:S(2)}) copy-start(bf16[640,1152]{1,0:T(8,128)(2,1)} %copy-done.14) | copy-start | bytes 4423684
  218.2 11.2 %copy-start.51 = (bf16[640,1152]{1,0:T(8,128)(2,1)S(1)}, bf16[640,1152]{1,0:T(8,128)(2,1)}, u32[]{:S(2)}) copy-start(bf16[640,1152]{1,0:T(8,128)(2,1)} %copy-done.50) | copy-start | bytes 4423684
  218.8 19.0 %collective-permute-start.36 = (f32[24,1536]{1,0:T(8,128)S(1)}, f32[24,1536]{1,0:T(8,128)S(1)}, u32[]{:S(2)}, u32[]{:S(2)}) collective-permute-start(f32[24,1536]{1,0:T(8,128)S(1)} %get-tuple-element.162), channel_id=1, source_target_pairs={{0,1},{1,0},{2,3},{3,2},{4,5},{5,4},{6,7},{7,6},{8,9},{9,8},{10,11... | collective-permute-start | bytes 442376 | tf_op jit(solution)/shard_map/ppermute | solution.py:110
  227.0 12.1 %collective-permute-start.34 = (bf16[4,48,768]{2,1,0:T(8,128)(2,1)S(1)}, bf16[4,48,768]{2,1,0:T(8,128)(2,1)S(1)}, u32[]{:S(2)}, u32[]{:S(2)}) collective-permute-start(bf16[4,48,768]{2,1,0:T(8,128)(2,1)S(1)} %get-tuple-element.153.refs_5_), channel_id=1, source_target_pairs={{0,4},{1,5},{2,6},{3,7},{4,0},{5,1},{6,2},{7,3},{8,12},{9,13},{10,... | collective-permute-start | bytes 884744 | tf_op jit(solution)/shard_map/ppermute | solution.py:110
  227.9 11.3 %collective-permute-start.35 = (bf16[4,48,1152]{2,1,0:T(8,128)(2,1)S(1)}, bf16[4,48,1152]{2,1,0:T(8,128)(2,1)S(1)}, u32[]{:S(2)}, u32[]{:S(2)}) collective-permute-start(bf16[4,48,1152]{2,1,0:T(8,128)(2,1)S(1)} %get-tuple-element.160), channel_id=1, source_target_pairs={{0,2},{1,3},{2,0},{3,1},{4,6},{5,7},{6,4},{7,5},{8,10},{9,11},{10,... | collective-permute-start | bytes 1327112 | tf_op jit(solution)/shard_map/ppermute | solution.py:110
  240.3 13.3 %collective-permute-start.37 = (bf16[48,1920]{1,0:T(8,128)(2,1)S(1)}, bf16[48,1920]{1,0:T(8,128)(2,1)S(1)}, u32[]{:S(2)}, u32[]{:S(2)}) collective-permute-start(bf16[48,1920]{1,0:T(8,128)(2,1)S(1)} %get-tuple-element.165), channel_id=1, source_target_pairs={{0,8},{1,9},{2,10},{3,11},{4,12},{5,13},{6,14},{7,15},{8,0},{9,1},... | collective-permute-start | bytes 552968 | tf_op jit(solution)/shard_map/ppermute | solution.py:110
  240.9 13.9 %collective-permute-start.38 = (bf16[48,1920]{1,0:T(8,128)(2,1)S(1)}, bf16[48,1920]{1,0:T(8,128)(2,1)S(1)}, u32[]{:S(2)}, u32[]{:S(2)}) collective-permute-start(bf16[48,1920]{1,0:T(8,128)(2,1)S(1)} %get-tuple-element.166), channel_id=1, source_target_pairs={{0,16},{1,17},{2,18},{3,19},{4,20},{5,21},{6,22},{7,23},{8,24},{9,... | collective-permute-start | bytes 552968 | tf_op jit(solution)/shard_map/ppermute | solution.py:110
  243.4 11.5 %collective-permute-start.39 = (bf16[48,1920]{1,0:T(8,128)(2,1)S(1)}, bf16[48,1920]{1,0:T(8,128)(2,1)S(1)}, u32[]{:S(2)}, u32[]{:S(2)}) collective-permute-start(bf16[48,1920]{1,0:T(8,128)(2,1)S(1)} %get-tuple-element.167), channel_id=1, source_target_pairs={{0,24},{1,25},{2,26},{3,27},{4,28},{5,29},{6,30},{7,31},{8,16},{9,... | collective-permute-start | bytes 552968 | tf_op jit(solution)/shard_map/ppermute | solution.py:110
  260.0 12.7 %collective-permute-start.40 = (bf16[8,48,768]{2,1,0:T(8,128)(2,1)S(1)}, bf16[8,48,768]{2,1,0:T(8,128)(2,1)S(1)}, u32[]{:S(2)}, u32[]{:S(2)}) collective-permute-start(bf16[8,48,768]{2,1,0:T(8,128)(2,1)S(1)} %get-tuple-element.171), channel_id=1, source_target_pairs={{0,2},{1,3},{2,0},{3,1},{4,6},{5,7},{6,4},{7,5},{8,10},{9,11},{10,... | collective-permute-start | bytes 1769480 | tf_op jit(solution)/shard_map/ppermute | solution.py:110
  261.1 5.7 %collective-permute-start.42 = (f32[24,1920]{1,0:T(8,128)S(1)}, f32[24,1920]{1,0:T(8,128)S(1)}, u32[]{:S(2)}, u32[]{:S(2)}) collective-permute-start(f32[24,1920]{1,0:T(8,128)S(1)} %get-tuple-element.174), channel_id=1, source_target_pairs={{0,1},{1,0},{2,3},{3,2},{4,5},{5,4},{6,7},{7,6},{8,9},{9,8},{10,11... | collective-permute-start | bytes 552968 | tf_op jit(solution)/shard_map/ppermute | solution.py:110
  261.1 11.5 %collective-permute-start.41 = (bf16[8,48,512]{2,1,0:T(8,128)(2,1)S(1)}, bf16[8,48,512]{2,1,0:T(8,128)(2,1)S(1)}, u32[]{:S(2)}, u32[]{:S(2)}) collective-permute-start(bf16[8,48,512]{2,1,0:T(8,128)(2,1)S(1)} %get-tuple-element.169.refs_6_), channel_id=1, source_target_pairs={{0,4},{1,5},{2,6},{3,7},{4,0},{5,1},{6,2},{7,3},{8,12},{9,13},{10,... | collective-permute-start | bytes 1179656 | tf_op jit(solution)/shard_map/ppermute | solution.py:110
  273.8 8.7 %collective-permute-start.43 = (bf16[4,48,768]{2,1,0:T(8,128)(2,1)S(1)}, bf16[4,48,768]{2,1,0:T(8,128)(2,1)S(1)}, u32[]{:S(2)}, u32[]{:S(2)}) collective-permute-start(bf16[4,48,768]{2,1,0:T(8,128)(2,1)S(1)} %get-tuple-element.176), channel_id=1, source_target_pairs={{0,4},{1,5},{2,6},{3,7},{4,0},{5,1},{6,2},{7,3},{8,12},{9,13},{10,... | collective-permute-start | bytes 884744 | tf_op jit(solution)/shard_map/ppermute | solution.py:110
  274.7 6.3 %collective-permute-start.44 = (bf16[4,48,512]{2,1,0:T(8,128)(2,1)S(1)}, bf16[4,48,512]{2,1,0:T(8,128)(2,1)S(1)}, u32[]{:S(2)}, u32[]{:S(2)}) collective-permute-start(bf16[4,48,512]{2,1,0:T(8,128)(2,1)S(1)} %get-tuple-element.178.refs_4_), channel_id=1, source_target_pairs={{0,2},{1,3},{2,0},{3,1},{4,6},{5,7},{6,4},{7,5},{8,10},{9,11},{10,... | collective-permute-start | bytes 589832 | tf_op jit(solution)/shard_map/ppermute | solution.py:110
  282.6 6.4 %collective-permute-start.45 = (bf16[48,1280]{1,0:T(8,128)(2,1)S(1)}, bf16[48,1280]{1,0:T(8,128)(2,1)S(1)}, u32[]{:S(2)}, u32[]{:S(2)}) collective-permute-start(bf16[48,1280]{1,0:T(8,128)(2,1)S(1)} %get-tuple-element.181), channel_id=1, source_target_pairs={{0,8},{1,9},{2,10},{3,11},{4,12},{5,13},{6,14},{7,15},{8,0},{9,1},... | collective-permute-start | bytes 368648 | tf_op jit(solution)/shard_map/ppermute | solution.py:110
  285.2 10.5 %collective-permute-start.46 = (bf16[48,1280]{1,0:T(8,128)(2,1)S(1)}, bf16[48,1280]{1,0:T(8,128)(2,1)S(1)}, u32[]{:S(2)}, u32[]{:S(2)}) collective-permute-start(bf16[48,1280]{1,0:T(8,128)(2,1)S(1)} %get-tuple-element.182), channel_id=1, source_target_pairs={{0,16},{1,17},{2,18},{3,19},{4,20},{5,21},{6,22},{7,23},{8,24},{9,... | collective-permute-start | bytes 368648 | tf_op jit(solution)/shard_map/ppermute | solution.py:110
  286.4 9.4 %collective-permute-start.47 = (bf16[48,1280]{1,0:T(8,128)(2,1)S(1)}, bf16[48,1280]{1,0:T(8,128)(2,1)S(1)}, u32[]{:S(2)}, u32[]{:S(2)}) collective-permute-start(bf16[48,1280]{1,0:T(8,128)(2,1)S(1)} %get-tuple-element.183), channel_id=1, source_target_pairs={{0,24},{1,25},{2,26},{3,27},{4,28},{5,29},{6,30},{7,31},{8,16},{9,... | collective-permute-start | bytes 368648 | tf_op jit(solution)/shard_map/ppermute | solution.py:110
  296.4 1.4 collective-permute-start.48
  (52 other events, 190.5 us)
Sparse Core Ops, SparseCore 0:
  59.5 66.7 all-gather.1

commit v2 on v1

v2 whole, which is shorter than its diff:
```python
import functools
import jax
import jax.numpy as jnp
import numpy as np
from jax import lax
from jax.experimental import pallas as pl
from jax.experimental.pallas import tpu as pltpu
from jax.sharding import PartitionSpec as P

HEADS = 12
HEAD_DIM = 64
IMG_LEN = 196
EPS = 1e-06
D = 768
FF = 3072
HALF = D // 2
WIDE = FF // 2
LOW = jnp.bfloat16
F32 = jnp.float32
STEP = 384
ROWS = 64
MARGIN = 10
PACE = 4.0
UP_LANE = 32
SCALE = HEAD_DIM ** (-0.5)
CHUNKS = ((4 * HALF + 128, 896), (WIDE, 768), (WIDE, 768))
Z_CODES = (0, 4, 8, 12)
SMEM = pl.BlockSpec(memory_space=pltpu.SMEM)
ANY = pl.BlockSpec(memory_space=pl.ANY)
VMEM = pl.BlockSpec(memory_space=pltpu.VMEM)


def shape(dims, kind=LOW):
    return jax.ShapeDtypeStruct(dims, kind)


class Chain:
    def __init__(self, loose):
        self.last = None
        self.loose = loose

    def near(self, array):
        if any(array is a for a in self.loose):
            return array
        return pltpu.with_memory_space_constraint(array, pltpu.VMEM)

    def __call__(
        self, body, outs, ins, *, info=None, touch=(), in_hbm=(), scratch=(), us=8.0, last=False
    ):
        head = [] if info is None else [info]
        ins = list(ins)
        count = len(head) + len(ins)
        specs = [SMEM] * len(head) + [ANY if i in in_hbm else VMEM for i in range(len(ins))]
        given = [
            pltpu.with_memory_space_constraint(a, pltpu.HBM) if i in in_hbm else self.near(a)
            for i, a in enumerate(ins)
        ]
        extra = list(touch) + ([] if self.last is None else [self.last])
        total = count + len(extra)

        def run(*refs):
            body(*refs[:count], *refs[total:])

        held = sum(
            int(np.prod(k.shape)) * jnp.dtype(k.dtype).itemsize
            for k in scratch
            if getattr(k, "shape", ())
        )
        size = sum(a.size * a.dtype.itemsize for a in [*ins, *outs])
        results = pl.pallas_call(
            run,
            out_shape=tuple(outs if last else [pltpu.VMEM(o.shape, o.dtype) for o in outs]),
            in_specs=specs + [ANY] * len(extra),
            out_specs=(VMEM,) * len(outs),
            scratch_shapes=list(scratch),
            compiler_params=pltpu.CompilerParams(vmem_limit_bytes=held + MARGIN * 2**20),
            cost_estimate=pl.CostEstimate(
                flops=int(us * PACE * 1.1e9), bytes_accessed=size, transcendentals=0
            ),
        )(*head, *given, *extra)
        self.last = min(results, key=lambda r: r.size * r.dtype.itemsize)
        return results


def dot(left, right, left_dim=1, right_dim=0):
    return lax.dot_general(
        left, right, (((left_dim,), (right_dim,)), ((), ())), preferred_element_type=F32
    )


def standardize(values):
    center = values - jnp.mean(values, -1, keepdims=True)
    scale = lax.rsqrt(jnp.mean(center * center, -1, keepdims=True) + EPS)
    return center * scale, scale


def row_loop(rows, body, init=0):
    def step(i, carry):
        return body(pl.ds(pl.multiple_of(i * ROWS, ROWS), ROWS), carry)

    return lax.fori_loop(0, rows // ROWS, step, init)


def swap(value, bit):
    pairs = [(i, i ^ bit) for i in range(32)]
    return lax.ppermute(value, "dp", pairs)


def pack_body(info, small, bias_up, *refs):
    weights, (mine, other), (rows, *held, sem) = refs[:4], refs[4:6], refs[6:]
    copies = [pltpu.make_async_copy(w, v, sem) for w, v in zip(weights, held)]
    for copy in copies:
        copy.start()
    w_qkv, w_out, w_up, w_down = held
    rows[...] = jnp.zeros_like(rows)
    share = w_qkv.shape[0]
    rows[: small.shape[0], :share] = small[...].astype(F32)
    rows[...] = rows[...].T
    rows[0:1, UP_LANE : UP_LANE + 4 * share] = bias_up[...].astype(F32)
    block = rows[:share, :].astype(LOW)
    for copy in copies:
        copy.wait()
    for flip, out in enumerate((mine, other)):
        h = info[1] ^ flip

        def half(weight, width, start=0):
            return weight[:, pl.ds(pl.multiple_of(start + h * width, 128), width)]

        for i in range(3):
            out[:, i * HALF : (i + 1) * HALF] = half(w_qkv, HALF, i * D)
        out[:, 3 * HALF : 4 * HALF] = half(w_out, HALF)
        at = CHUNKS[0][0]
        out[:, 4 * HALF : at] = block
        out[:, at : at + WIDE] = half(w_up, WIDE)
        out[:, at + WIDE :] = half(w_down, WIDE)


def unit_body(info, mine, other, unit_one, unit_two, unit_three, unit_a, unit_b):
    a, b = mine[...].astype(F32), other[...].astype(F32)
    unit = jnp.where(
        info[1] == 0, jnp.concatenate([a, b], 0), jnp.concatenate([b, a], 0)
    ).astype(LOW)
    start = at_a = at_b = 0
    for (width, cut), out in zip(CHUNKS, (unit_one, unit_two, unit_three)):
        part = unit[:, start : start + width]
        out[...] = part
        unit_a[:, at_a : at_a + cut] = part[:, :cut]
        unit_b[:, at_b : at_b + width - cut] = part[:, cut:]
        start, at_a, at_b = start + width, at_a + cut, at_b + width - cut


def own_body(unit_a, far_a, unit_b, far_b, pair_a, pair_b):
    for pair, unit, far in ((pair_a, unit_a, far_a), (pair_b, unit_b, far_b)):
        width = pair.shape[2]
        pair[0] = unit[:, :width]
        pair[1] = far[:, :width]


def pair_body(unit, far, pair):
    pair[0] = unit[...]
    pair[1] = far[...]


def stack_body(cut, *refs):
    pieces, (stack_a, stack_b) = refs[:-2], refs[-2:]
    at = 0
    for piece in pieces:
        for i in range(piece.shape[0] if len(piece.shape) == 3 else 1):
            part = piece.at[i] if len(piece.shape) == 3 else piece
            stack_a[at] = part[:, :cut]
            stack_b[at] = part[:, cut:]
            at += 1


def join_body(start_a, start_b, *refs):
    stacks, own, (join_a, join_b) = refs[:4], refs[4:-2], refs[-2:]
    for side, join, start in ((0, join_a, start_a), (1, join_b, start_b)):
        width = join.shape[2]
        parts = own[2 * side : 2 * side + 2]
        for i, part in enumerate(parts):
            join[i] = part[:, start : start + width]
        at = len(parts)
        join[at : at + 3] = stacks[2 * side][...]
        join[at + 3 : at + 6] = stacks[2 * side + 1][...]


def place_body(plan, info, *refs):
    pieces, out, sem = refs[:-2], refs[-2], refs[-1]
    copies = []
    for piece, (codes, source, target, width) in zip(pieces, plan):
        for i, code in enumerate(codes):
            row = pl.multiple_of((info[0] ^ code) * 48, 48)
            copies.append(
                pltpu.make_async_copy(
                    piece.at[i, :, pl.ds(source, width)],
                    out.at[pl.ds(row, 48), pl.ds(target, width)],
                    sem,
                )
            )
    for copy in copies:
        copy.start()
    for copy in copies:
        copy.wait()


ORDER = (1, 2, 3, 0, 1, 3, 2, 0, 1, 3, 3, 1, 2, 3, 2)
KEEP_A = tuple(c ^ y for y in (0, 2) for c in Z_CODES)
KEEP_B = tuple(c ^ x for x in (0, 1) for c in Z_CODES)
SEND_A = tuple(c ^ 1 for c in KEEP_A)
SEND_B = tuple(c ^ 2 for c in KEEP_B)


def spread(chip, grad, send, keep, send_codes, keep_codes):
    for out, codes in ((send, send_codes), (keep, keep_codes)):
        for i, code in enumerate(codes):
            row = pl.multiple_of((chip ^ code) * 48, 48)
            out[i] = grad[pl.ds(row, 48), :].astype(out.dtype)


def add(left, right):
    return (left.astype(F32) + right.astype(F32)).astype(LOW)


def first_sum_body(far_a, keep_a, far_b, keep_b, send_a, own_a, send_b, own_b):
    for far, keep, send, own in ((far_a, keep_a, send_a, own_a), (far_b, keep_b, send_b, own_b)):
        for i in range(4):
            send[i] = add(far[4 + i], keep[4 + i])
            own[i] = add(far[i], keep[i])


def second_sum_body(far_a, keep_a, far_b, keep_b, *outs):
    cut = keep_a.shape[2]
    for i in range(4):
        out = outs[i] if len(outs) == 4 else outs[i % 2].at[i // 2]
        out[:, :cut] = add(far_a[i], keep_a[i])
        out[:, cut:] = add(far_b[i], keep_b[i])


def last_sum_body(info, own, z_one, z_two, z_three, mine, other, total):
    value = own[...].astype(F32)
    for piece in (z_one, z_two, z_three):
        value = value + piece[...].astype(F32)
    total[...] = value
    split_rows(info, total, mine, other)


def split_rows(info, total, mine, other):
    rows = mine.shape[0]
    mine[...] = total[pl.ds(pl.multiple_of(info[1] * rows, 8), rows), :]
    other[...] = total[pl.ds(pl.multiple_of((1 - info[1]) * rows, 8), rows), :]


def merge(info, mine, other, start, width, out, count=1):
    for flip, part in enumerate((mine, other)):
        h = info[1] ^ flip
        for i in range(count):
            at = pl.multiple_of((2 * i + h) * width, 128)
            out[:, pl.ds(at, width)] = part[:, start + i * width : start + (i + 1) * width]


def merge_one_body(info, mine, other, out):
    merge(info, mine, other, 0, WIDE, out)


def merge_qkv_body(info, mine, other, out_qkv, out_out):
    merge(info, mine, other, 0, HALF, out_qkv, 3)
    merge(info, mine, other, 3 * HALF, HALF, out_out)


def near_sum_body(own, far, keep, send):
    keep[...] = add(own[0], far[0])
    send[...] = add(own[1], far[1])


def last_near_body(info, keep, far, mine, other, total):
    total[...] = keep[...].astype(F32) + far[...].astype(F32)
    split_rows(info, total, mine, other)


def block_body(info, block, send, keep):
    spread(info[0], block, send, keep, SEND_A, KEEP_A)


def block_sum_body(far, keep, send, own):
    count = keep.shape[0] // 2
    own[...] = far[:count] + keep[:count]
    send[...] = far[count:] + keep[count:]


def block_last_body(info, far, keep, mine, other, total):
    total[...] = far[0] + keep[0]
    split_rows(info, total, mine, other)


def block_end_body(mine, other, out):
    out[...] = mine[...] + other[...]


def start_body(slots, visible, cot, dy, total):
    rows = cot.shape[0]
    total[...] = jnp.zeros_like(total)
    for s in range(rows // slots):
        live = lax.broadcasted_iota(jnp.int32, (slots, 1), 0) < visible[s]
        part = jnp.where(live, cot[s * slots : (s + 1) * slots, :].astype(F32), 0.0)
        dy[s * slots : (s + 1) * slots, :] = part.astype(LOW)
        total[0:1, :] += jnp.sum(part, 0, keepdims=True)


def qkv_body(info, tokens, own, normed, qkv, vecs):
    vecs[...] = own[:, 4 * HALF :].astype(F32).T[:16, :]

    def norm(at, carry):
        z, _ = standardize(tokens[at, :].astype(F32))
        normed[at, :] = (z * vecs[0:1, :] + vecs[1:2, :]).astype(LOW)
        return carry

    row_loop(tokens.shape[0], norm)
    project_qkv(info, 0, normed, own, vecs, qkv)


def project_qkv(info, flip, normed, weight, vecs, out):
    half = half_of(info, flip, HALF)
    for i in range(3):
        at = slice(i * STEP, (i + 1) * STEP)
        value = dot(normed[...], weight[:, at])
        if i != 1:
            value = value + vecs[6 + i // 2 : 7 + i // 2, half]
        out[:, at] = value.astype(LOW)


def qkv_far_body(share, info, normed, own, weight, vecs, qkv, bias_up, again):
    again[...] = normed[...]
    project_qkv(info, 1, normed, weight, vecs, qkv)
    for d in range(D // share):
        row = own[d * share // 16 * 16 : d * share // 16 * 16 + 16, 4 * HALF :].astype(F32)
        at = d * share % 16
        bias_up[0:1, 4 * share * d : 4 * share * (d + 1)] = row[
            at : at + 1, UP_LANE : UP_LANE + 4 * share
        ]


def soft_of(query, key, live):
    scores = jnp.where(live, dot(query, key, 1, 1) * SCALE, -1e30)
    power = jnp.exp(scores - jnp.max(scores, -1, keepdims=True))
    return power * (1.0 / jnp.sum(power, -1, keepdims=True))


def attend_body(slots, visible, qkv, out):
    rows = qkv.shape[0]
    lane = lax.broadcasted_iota(jnp.int32, (1, 128), 1)
    for s in range(rows // slots):
        at = slice(s * slots, (s + 1) * slots)
        live = lax.broadcasted_iota(jnp.int32, (1, slots), 1) < visible[s]
        for j in range(HALF // 128):
            query, key, value = (
                qkv[at, i * HALF + j * 128 : i * HALF + (j + 1) * 128] for i in range(3)
            )
            mixed = None
            for e in range(2):
                mine = (lane < HEAD_DIM) if e == 0 else (lane >= HEAD_DIM)
                soft = soft_of(jnp.where(mine, query, 0), key, live).astype(LOW)
                part = dot(soft, jnp.where(mine, value, 0))
                mixed = part if mixed is None else mixed + part
            out[at, j * 128 : (j + 1) * 128] = mixed.astype(LOW)


def hidden_body(tokens, vecs, o_own, o_par, own, par, hidden, normed):
    hidden[...] = dot(o_own[...], own[:, 3 * HALF : 4 * HALF], 1, 1)
    hidden[...] += dot(o_par[...], par[:, 3 * HALF : 4 * HALF], 1, 1)

    def norm(at, carry):
        value = tokens[at, :].astype(F32) + (hidden[at, :] + vecs[4:5, :])
        hidden[at, :] = value
        z, _ = standardize(value)
        normed[at, :] = (z * vecs[2:3, :] + vecs[3:4, :]).astype(LOW)
        return carry

    row_loop(tokens.shape[0], norm)


GELU_A = 0.7978845608028654
GELU_B = 0.044715


def raise_body(flip, info, normed, bias, weight, gate, slope):
    for i in range(WIDE // STEP):
        at = slice(i * STEP, (i + 1) * STEP)
        start = pl.multiple_of((info[1] ^ flip) * WIDE + i * STEP, 128)
        u = dot(normed[...], weight[:, at]) + bias[:, pl.ds(start, STEP)]
        square = u * u
        t = jnp.tanh(u * (GELU_A + (GELU_A * GELU_B) * square))
        lift = 0.5 + 0.5 * t
        gated = u * lift
        curve = GELU_A + (3.0 * GELU_A * GELU_B) * square
        slope[:, at] = (lift + (gated * (1.0 - t)) * curve).astype(LOW)
        gate[:, at] = gated.astype(LOW)


def half_of(info, flip, width):
    return pl.ds(pl.multiple_of((info[1] ^ flip) * width, 128), width)


def mix_body(hidden, vecs, a_own, a_par, own, par, out):
    value = dot(a_own[...], own[...], 1, 1)
    value += dot(a_par[...], par[...], 1, 1)
    out[...] = (hidden[...] + (value + vecs[5:6, :])).astype(LOW)


def raise_back_body(info, dy, s_own, s_par, own, par, d_own, d_par, total):
    for i in range(WIDE // STEP):
        at = slice(i * STEP, (i + 1) * STEP)
        for h, (slope, weight, out) in enumerate(((s_own, own, d_own), (s_par, par, d_par))):
            value = (dot(dy[...], weight[:, at]) * slope[:, at].astype(F32)).astype(LOW)
            start = pl.multiple_of((info[1] ^ h) * WIDE + i * STEP, 128)
            total[:, pl.ds(start, STEP)] = jnp.sum(value.astype(F32), 0, keepdims=True)
            out[:, at] = value


def norm_back(part, values, gain):
    z, scale = standardize(values)
    e = part * gain
    mean_e = jnp.mean(e, -1, keepdims=True)
    mean_ez = jnp.mean(e * z, -1, keepdims=True)
    return scale * (e - mean_e - z * mean_ez), z


def hidden_back_body(dy, hidden, vecs, d_own, d_par, own, par, dh, dp, sums, acc):
    acc[...] = dot(d_own[...], own[...], 1, 1)
    acc[...] += dot(d_par[...], par[...], 1, 1)

    def back(at, carry):
        part = acc[at, :]
        value, z = norm_back(part, hidden[at, :], vecs[2:3, :])
        value = dy[at, :].astype(F32) + value
        dh[at, :] = value
        low = value.astype(LOW)
        dp[at, :] = low
        gain, shift, bias = carry
        return (
            gain + jnp.sum(part * z, 0, keepdims=True),
            shift + jnp.sum(part, 0, keepdims=True),
            bias + jnp.sum(low.astype(F32), 0, keepdims=True),
        )

    zero = jnp.zeros((1, D), F32)
    totals = row_loop(acc.shape[0], back, (zero, zero, zero))
    for r in range(3):
        sums[r : r + 1, :] = totals[r]


def attend_back_body(slots, visible, qkv, dp, out_weight, dqkv, sums, mixed):
    rows = qkv.shape[0]
    mixed[...] = dot(dp[...], out_weight[:, 3 * HALF : 4 * HALF]).astype(LOW)
    lane = lax.broadcasted_iota(jnp.int32, (1, 128), 1)
    sums[...] = jnp.zeros_like(sums)
    for s in range(rows // slots):
        at = slice(s * slots, (s + 1) * slots)
        live = lax.broadcasted_iota(jnp.int32, (1, slots), 1) < visible[s]
        for j in range(HALF // 128):
            cols = [slice(i * HALF + j * 128, i * HALF + (j + 1) * 128) for i in range(3)]
            query, key, value = (qkv[at, c] for c in cols)
            grad = mixed[at, j * 128 : (j + 1) * 128]
            totals = [None] * 3
            for e in range(2):
                mine = (lane < HEAD_DIM) if e == 0 else (lane >= HEAD_DIM)
                query_e, key_e, grad_e = (jnp.where(mine, v, 0) for v in (query, key, grad))
                soft = soft_of(query_e, key, live)
                grad_soft = dot(grad_e, value, 1, 1)
                inner = jnp.sum(soft * grad_soft, -1, keepdims=True)
                grad_scores = (soft * (grad_soft - inner)).astype(LOW)
                parts = (
                    dot(grad_scores, key_e),
                    dot(grad_scores, query_e, 0, 0),
                    dot(soft.astype(LOW), grad_e, 0, 0),
                )
                totals = [p if t is None else t + p for t, p in zip(totals, parts)]
            for i, factor in enumerate((SCALE, SCALE, 1.0)):
                low = (totals[i] * factor).astype(LOW)
                dqkv[at, cols[i]] = low
                if i != 1:
                    sums[i : i + 1, j * 128 : (j + 1) * 128] += jnp.sum(
                        low.astype(F32), 0, keepdims=True
                    )


def token_back_body(
    share, info, tokens, dh, vecs, sums_two, dy_sum, up_sum, sums_own, sums_par, d_own, d_par, own, par,
    out, block, acc, sums,
):
    acc[...] = dot(d_own[...], own[:, : 3 * HALF], 1, 1)
    acc[...] += dot(d_par[...], par[:, : 3 * HALF], 1, 1)

    def back(at, carry):
        part = acc[at, :]
        value, z = norm_back(part, tokens[at, :].astype(F32), vecs[0:1, :])
        out[at, :] = (dh[at, :] + value).astype(LOW)
        gain, shift = carry
        return (
            gain + jnp.sum(part * z, 0, keepdims=True),
            shift + jnp.sum(part, 0, keepdims=True),
        )

    zero = jnp.zeros((1, D), F32)
    totals = row_loop(acc.shape[0], back, (zero, zero))
    sums[...] = jnp.zeros_like(sums)
    for r in range(2):
        sums[r : r + 1, :] = totals[r]
    sums[2:5, :] = sums_two[0:3, :]
    sums[5:6, :] = dy_sum[0:1, :]
    for flip, part in enumerate((sums_own, sums_par)):
        half = half_of(info, flip, HALF)
        sums[6:7, half] = part[0:1, :]
        sums[7:8, half] = part[2:3, :]
    block[...] = sums[...].T
    for d in range(D // share):
        part = up_sum[0:1, 4 * share * d : 4 * share * (d + 1)]
        block[share * d : share * d + 1, UP_LANE : UP_LANE + 4 * share] = part


def outer(left, left_far, right, right_far):
    return dot(left[...], right[...], 0, 0) + dot(left_far[...], right_far[...], 0, 0)


def pair_grads(info, blocks, sends, grad):
    send_a, keep_a, send_b, keep_b = sends
    width = keep_a.shape[2]
    at = 0
    for left, left_far, right, right_far in blocks:
        grad[...] = outer(left, left_far, right, right_far)
        split = min(max(width - at, 0), STEP)
        if split:
            cols = slice(at, at + split)
            part = grad.at[:, :split]
            spread(info[0], part, send_a.at[:, :, cols], keep_a.at[:, :, cols], SEND_A, KEEP_A)
        if split < STEP:
            cols = slice(at + split - width, at + STEP - width)
            part = grad.at[:, split:]
            spread(info[0], part, send_b.at[:, :, cols], keep_b.at[:, :, cols], SEND_B, KEEP_B)
        at += STEP


def steps_of(near, far, count):
    for i in range(count):
        at = slice(i * STEP, (i + 1) * STEP)
        yield near.at[:, at], far.at[:, at]


def wide_grad_body(info, left, left_far, right, right_far, *rest):
    blocks = [(left, left_far, a, b) for a, b in steps_of(right, right_far, 4)]
    pair_grads(info, blocks, rest[:4], rest[4])


def qkv_grad_body(info, norm, norm_far, dqkv, dqkv_far, dp, dp_far, mixed, mixed_far, *rest):
    blocks = [(norm, norm_far, a, b) for a, b in steps_of(dqkv, dqkv_far, 3)]
    blocks += [(dp, dp_far, a, b) for a, b in steps_of(mixed, mixed_far, 1)]
    pair_grads(info, blocks, rest[:4], rest[4])


def pick(flag, left, right):
    return jnp.where(flag, left, right)


def half_major(matrix):
    rows = matrix.shape[0]
    return matrix.reshape(rows, 3, 2, HALF).transpose(0, 2, 1, 3).reshape(rows, 3 * D)


def third_major(matrix):
    rows = matrix.shape[0]
    return matrix.reshape(rows, 2, 3, HALF).transpose(0, 2, 1, 3).reshape(rows, 3 * D)


class WholeComm:
    touch = ()

    def __init__(self, count):
        self.info = jnp.zeros((2,), jnp.int32)

    def order(self, low, high):
        return low, high

    def weights(self, call, small, bias_up, w_qkv, w_out, w_up, w_down):
        def gather(value):
            return lax.all_gather(value, "dp", axis=0, tiled=True)

        def half(matrix, h):
            width = matrix.shape[1] // 2
            return matrix[:, h * width : (h + 1) * width]

        block = jnp.pad(small.T, ((0, 0), (0, 128 - small.shape[0])))
        block = gather(block.at[0, UP_LANE : UP_LANE + bias_up.shape[1]].set(bias_up[0]))
        qkv, out, up = (gather(w) for w in (half_major(w_qkv), w_out, w_up))
        self.first = [jnp.concatenate([half(qkv, h), half(out, h), block], 1) for h in range(2)]
        self.second = [half(up, h) for h in range(2)]
        down = gather(w_down)
        self.third = [half(down, h) for h in range(2)]

    def step(self, call):
        pass

    def advance(self, call):
        pass

    def pump(self, call, index):
        pass

    def reduce(self, value):
        return lax.psum_scatter(value, "dp", scatter_dimension=0, tiled=True)

    def far(self, array):
        return array

    def reduce_down(self, call, dy, dy_far, gated, gated_far):
        self.down = self.reduce(dot(dy, jnp.concatenate([gated, gated_far], 1), 0, 0))

    def reduce_up(self, call, norm, norm_far, du, du_far):
        self.up = self.reduce(dot(norm, jnp.concatenate([du, du_far], 1), 0, 0))

    def reduce_qkv(self, call, norm, norm_far, triple, triple_far, dp, dp_far, mixed, mixed_far):
        triple = jnp.concatenate([triple, triple_far], 1)
        self.qkv = third_major(self.reduce(dot(norm, triple, 0, 0)))
        self.out = self.reduce(dot(dp, jnp.concatenate([mixed, mixed_far], 1), 0, 0))

    def reduce_block(self, call, block):
        self.vec = self.reduce(block)

    def results(self, call):
        return self.down, self.up, self.out, self.qkv, self.vec


class GridComm:
    def __init__(self):
        index = lax.axis_index("dp")
        self.info = jnp.stack([index >> 1, index & 1]).astype(jnp.int32)
        self.is_first = (index & 1) == 0
        self.jobs = []

    def order(self, low, high):
        return pick(self.is_first, low, high), pick(self.is_first, high, low)

    def weights(self, call, small, bias_up, w_qkv, w_out, w_up, w_down):
        rows = w_qkv.shape[0]
        total = sum(width for width, _ in CHUNKS)
        total_a = sum(cut for _, cut in CHUNKS)
        parts = (w_qkv, w_out, w_up, w_down)
        mine, other = call(
            pack_body,
            [shape((rows, total))] * 2,
            [small, bias_up, *parts],
            info=self.info,
            in_hbm=(2, 3, 4, 5),
            scratch=[pltpu.VMEM((128, 128), F32)]
            + [pltpu.VMEM(w.shape, LOW) for w in parts]
            + [pltpu.SemaphoreType.DMA],
        )
        *self.units, unit_a, unit_b = call(
            unit_body,
            [shape((48, w)) for w in [*(c[0] for c in CHUNKS), total_a, total - total_a]],
            [mine, swap(other, 1)],
            info=self.info,
        )
        self.own = [unit_a, swap(unit_a, 4), unit_b, swap(unit_b, 2)]
        self.lines = [swap(self.units[0], bit) for bit in (8, 16, 24)]
        self.plan = self.schedule(call)

    def advance(self, call):
        next(self.plan)

    def pair(self, call, index, far):
        (pair,) = call(pair_body, [shape((2, 48, CHUNKS[index][0]))], [self.units[index], far])
        return [far, swap(pair, 8)]

    def schedule(self, call):
        width, cut = CHUNKS[0]
        pair_a, pair_b = call(
            own_body, [shape((2, 48, cut)), shape((2, 48, width - cut))], self.own
        )
        pairs = [pair_a, swap(pair_a, 2), pair_b, swap(pair_b, 4)]
        stacked = self.stack(call, 0, self.lines)
        far_one = swap(self.units[1], 16)
        joined = self.join(call, 0, stacked, touch=(far_one,))
        line_one = self.pair(call, 1, far_one)
        far_two = swap(self.units[2], 16)
        own = self.finish(call, 0, joined, pairs)
        self.first = [own, swap(own, 1)]
        yield
        line_two = self.pair(call, 2, far_two)
        yield
        stacked = self.stack(call, 1, line_one)
        yield
        joined = self.join(call, 1, stacked)
        stacked = self.stack(call, 2, line_two)
        yield
        joined_two = self.join(call, 2, stacked)
        yield
        own = self.finish(call, 1, joined)
        self.second = [own, swap(own, 1)]
        yield
        own = self.finish(call, 2, joined_two)
        self.third = [own, swap(own, 1)]
        yield

    def starts(self, index):
        return (
            sum(c for _, c in CHUNKS[:index]),
            sum(w - c for w, c in CHUNKS[:index]),
        )

    def stack(self, call, index, line, touch=()):
        width, cut = CHUNKS[index]
        a, b = call(
            functools.partial(stack_body, cut),
            [shape((3, 48, cut)), shape((3, 48, width - cut))],
            line,
            touch=touch,
        )
        return a, swap(a, 4), b, swap(b, 2)

    def join(self, call, index, stacked, touch=()):
        width, cut = CHUNKS[index]
        count = 6 if index == 0 else 8
        a, b = call(
            functools.partial(join_body, *self.starts(index)),
            [shape((count, 48, cut)), shape((count, 48, width - cut))],
            [*stacked] + ([] if index == 0 else self.own),
            touch=touch,
        )
        return a, swap(a, 2), b, swap(b, 4)

    def finish(self, call, index, joined, pairs=()):
        width, cut = CHUNKS[index]
        z = (8, 4, 12) if index else Z_CODES[1:]
        codes_a = z + tuple(c ^ 2 for c in z)
        codes_b = z + tuple(c ^ 1 for c in z)
        if index:
            codes_a, codes_b = (0, 2) + codes_a, (0, 1) + codes_b
        plan = []
        for codes_a, codes_b in [(codes_a, codes_b)] + ([((0, 2), (0, 1))] if pairs else []):
            plan += [
                (codes_a, 0, 0, cut),
                (tuple(c ^ 1 for c in codes_a), 0, 0, cut),
                (codes_b, 0, cut, width - cut),
                (tuple(c ^ 2 for c in codes_b), 0, cut, width - cut),
            ]
        return call(
            functools.partial(place_body, plan),
            [shape((D, width))],
            [*joined, *pairs],
            info=self.info,
            scratch=[pltpu.SemaphoreType.DMA],
        )[0]

    def pieces(self, width_a, width_b):
        return [shape((8, 48, w)) for w in (width_a, width_a, width_b, width_b)]

    def job(self, call, name, parts, body, outs, direct):
        send_a, keep_a, send_b, keep_b = parts
        width_a, width_b = keep_a.shape[2], keep_b.shape[2]
        width = width_a + width_b
        far_a, far_b = swap(send_a, 2), swap(send_b, 4)
        yield
        send_a, keep_a, send_b, keep_b = call(
            first_sum_body,
            [shape((4, 48, w)) for w in (width_a, width_a, width_b, width_b)],
            [far_a, keep_a, far_b, keep_b],
        )
        far_a, far_b = swap(send_a, 4), swap(send_b, 2)
        yield
        if direct:
            own, *lines = call(
                second_sum_body, [shape((48, width))] * 4, [far_a, keep_a, far_b, keep_b]
            )
            lines = [swap(line, bit) for line, bit in zip(lines, (8, 16, 24))]
            yield
            last_body, lines = last_sum_body, [own, *lines]
        else:
            own, send = call(
                second_sum_body, [shape((2, 48, width))] * 2, [far_a, keep_a, far_b, keep_b]
            )
            far = swap(send, 8)
            yield
            own, send = call(near_sum_body, [shape((48, width))] * 2, [own, far])
            far = swap(send, 16)
            yield
            last_body, lines = last_near_body, [own, far]
        mine, other = call(
            last_body,
            [shape((24, width), F32)] * 2,
            lines,
            info=self.info,
            scratch=[pltpu.VMEM((48, width), F32)],
        )
        other = swap(other, 1)
        yield
        self.outs[name] = call(body, outs, [mine, other], info=self.info, last=True)

    def begin(self, job):
        next(job)
        self.jobs.append(job)

    def pump(self, call, index):
        return next(self.jobs[index], self) is not self

    def block_job(self, call, block):
        send, keep = call(
            block_body, [shape((8, 48, 128), F32)] * 2, [block], info=self.info
        )
        far = swap(send, 2)
        yield
        for bit, count in ((4, 4), (16, 2), (8, 1)):
            send, keep = call(
                block_sum_body, [shape((count, 48, 128), F32)] * 2, [far, keep]
            )
            far = swap(send, bit)
            yield
        mine, other = call(
            block_last_body,
            [shape((24, 128), F32)] * 2,
            [far, keep],
            info=self.info,
            scratch=[pltpu.VMEM((48, 128), F32)],
        )
        other = swap(other, 1)
        yield
        self.vec = call(block_end_body, [shape((24, 128), F32)], [mine, other])[0]

    def results(self, call):
        for index in ORDER:
            self.pump(call, index)
        (down,), (up,), (qkv, out) = [self.outs[k] for k in ("down", "up", "qkv")]
        return down, up, out, qkv, self.vec

    def far(self, array):
        return swap(array, 1)

    def reduce_down(self, call, dy, dy_far, gated, gated_far):
        self.outs = {}
        parts = call(
            wide_grad_body,
            self.pieces(768, 768),
            [dy, dy_far, gated, gated_far],
            info=self.info,
            scratch=[pltpu.VMEM((D, STEP), F32)],
            us=6,
        )
        self.begin(self.job(call, "down", parts, merge_one_body, [shape((24, FF), F32)], False))

    def reduce_up(self, call, *args):
        parts = call(
            wide_grad_body,
            self.pieces(768, 768),
            args,
            info=self.info,
            scratch=[pltpu.VMEM((D, STEP), F32)],
            us=6,
        )
        self.begin(self.job(call, "up", parts, merge_one_body, [shape((24, FF), F32)], False))

    def reduce_qkv(self, call, *args):
        parts = call(
            qkv_grad_body,
            self.pieces(768, 768),
            args,
            info=self.info,
            scratch=[pltpu.VMEM((D, STEP), F32)],
            us=6,
        )
        outs = [shape((24, 3 * D), F32), shape((24, D), F32)]
        self.begin(self.job(call, "qkv", parts, merge_qkv_body, outs, True))

    def reduce_block(self, call, block):
        self.begin(self.block_job(call, block))


def shards(count, tokens, lengths, source, cotangent, w_qkv, w_out, w_up, w_down, *small):
    (
        gain_one, shift_one, bias_query, bias_value, bias_out, gain_two, shift_two,
        bias_up, bias_down,
    ) = small
    seqs, slots = tokens.shape[:2]
    rows = seqs * slots
    share = gain_one.shape[0]
    comm = GridComm() if count == 32 else WholeComm(count)
    visible = jnp.where(source == 1, lengths, IMG_LEN)
    tokens = tokens.reshape(rows, D)
    cotangent = cotangent.reshape(rows, D)
    small = jnp.stack(
        [gain_one, shift_one, gain_two, shift_two, bias_out, bias_down, bias_query, bias_value]
    )
    bias_up = bias_up[None]
    call = Chain([tokens, cotangent, small, bias_up])

    act = shape((rows, D))
    act_f = shape((rows, D), F32)
    half = shape((rows, HALF))
    triple = shape((rows, 3 * HALF))
    wide = shape((rows, WIDE))

    def attend(part, *touch):
        return call(
            functools.partial(attend_body, slots), [half], [part], info=visible, us=4.3, touch=touch
        )[0]

    comm.weights(call, small, bias_up, w_qkv, w_out.T, w_up, w_down.T)
    dy, dy_sum = call(
        functools.partial(start_body, slots),
        [act, shape((8, D), F32)],
        [cotangent],
        info=visible,
    )
    dy_far = comm.far(dy)
    comm.advance(call)
    normed_one, qkv_own, vecs = call(
        qkv_body,
        [act, triple, shape((16, D), F32)],
        [tokens, comm.first[0]],
        info=comm.info,
        touch=(dy_far,),
        us=4.3,
    )
    o_own = attend(qkv_own)
    comm.advance(call)
    comm.advance(call)
    qkv_par, bias_up, normed_again = call(
        functools.partial(qkv_far_body, share),
        [triple, shape((1, FF), F32), act],
        [normed_one, comm.first[0], comm.first[1], vecs],
        info=comm.info,
        us=2.5,
    )
    normed_one_far = comm.far(normed_again)
    comm.advance(call)
    o_par = attend(qkv_par)
    o_far = comm.far(o_par)
    comm.advance(call)
    hidden, normed_two = call(
        hidden_body,
        [act_f, act],
        [tokens, vecs, o_own, o_par, *comm.first],
        touch=(o_far, normed_one_far),
        us=3.6,
    )
    normed_two_far = comm.far(normed_two)
    comm.advance(call)
    second = comm.second

    def raise_half(flip, *touch):
        return call(
            functools.partial(raise_body, flip),
            [wide] * 2,
            [normed_two, bias_up, second[flip]],
            info=comm.info,
            touch=touch,
            us=3.7,
        )

    gated, slope = raise_half(0)
    gated_par, slope_par = raise_half(1)
    gated_far = comm.far(gated_par)
    comm.advance(call)
    comm.reduce_down(call, dy, dy_far, gated, gated_far)
    third = comm.third
    raised, raised_par, up_sum = call(
        raise_back_body,
        [wide, wide, shape((1, FF), F32)],
        [dy, slope, slope_par, *third],
        info=comm.info,
        us=4.8,
    )
    raised_far = comm.far(raised_par)
    grad_hidden, branch, sums_two = call(
        hidden_back_body,
        [act_f, act, shape((8, D), F32)],
        [dy, hidden, vecs, raised, raised_par, *second],
        scratch=[pltpu.VMEM((rows, D), F32)],
        us=6.6,
    )
    branch_far = comm.far(branch)

    def attend_back(part, weight, *touch):
        return call(
            functools.partial(attend_back_body, slots),
            [triple, shape((8, HALF), F32)],
            [part, branch, weight],
            info=visible,
            scratch=[pltpu.VMEM((rows, HALF), LOW)],
            touch=touch,
            us=8.2,
        )

    triple_par, sums_par = attend_back(qkv_par, comm.first[1])
    triple_far = comm.far(triple_par)
    comm.pump(call, 0)
    comm.reduce_up(call, normed_two, normed_two_far, raised, raised_far)
    triple_own, sums_own = attend_back(qkv_own, comm.first[0], branch_far)
    comm.pump(call, 0)
    comm.reduce_qkv(
        call, normed_one, normed_one_far, triple_own, triple_far, branch, branch_far, o_own, o_far
    )
    comm.pump(call, 1)
    grad_tokens, block = call(
        functools.partial(token_back_body, share),
        [act, shape((D, 128), F32)],
        [
            tokens, grad_hidden, vecs, sums_two, dy_sum, up_sum, sums_own, sums_par,
            triple_own, triple_par, *comm.first,
        ],
        info=comm.info,
        scratch=[pltpu.VMEM((rows, D), F32), pltpu.VMEM((128, D), F32)],
        us=6.5,
    )
    (output,) = call(
        mix_body, [act], [hidden, vecs, gated, gated_par, *third], us=4.1, last=True
    )
    comm.pump(call, 0)
    comm.reduce_block(call, block)
    g_down_t, g_up, g_out_t, g_qkv, g_vec = comm.results(call)
    (
        g_gain_one, g_shift_one, g_gain_two, g_shift_two, g_bias_out, g_bias_down, g_query, g_value,
    ) = [g_vec[:, i] for i in range(8)]
    return (
        output.reshape(seqs, slots, D),
        grad_tokens.reshape(seqs, slots, D),
        g_qkv,
        g_out_t.T,
        g_up,
        g_down_t.T,
        g_gain_one, g_shift_one, g_query, g_value, g_bias_out, g_gain_two, g_shift_two,
        g_vec[0, UP_LANE : UP_LANE + 4 * share],
        g_bias_down,
    )


def solution(mesh):
    row, tall, wide, vec = P("dp", None, None), P("dp", None), P(None, "dp"), P("dp")
    in_specs = (row, vec, vec, row, tall, wide, tall, wide) + (vec,) * 9
    out_specs = (row, row, tall, wide, tall, wide) + (vec,) * 9
    body = functools.partial(shards, mesh.shape["dp"])
    return jax.shard_map(
        body, mesh=mesh, in_specs=in_specs, out_specs=out_specs, check_vma=False
    )
```

time: 312 us -> 235 us (0.75)
  waiting for transfers between devices: 96.1 us -> 58.6 us
  local copies, waits for them, and re-layouts: 26.6 us -> 10.4 us
  Pallas kernels: 119 us -> 104 us
  between operations: 15.3 us -> 2.03 us
  starting transfers between devices: 50.4 us -> 56 us
    ppermute x49 -> x62, waiting for transfers between devices: 96.1 us -> 58.6 us  [swap(): return lax.ppermute(value, 'dp', pairs)]
    pallas_call x36 -> x51, Pallas kernels: 119 us -> 104 us  [__call__(): pl.pallas_call(run, out_shape=tuple(outs if last else [pltpu.VMEM(o.shape...]
    unnamed x132 -> x125, local copies, waits for them, and re-layouts: 22.9 us -> 8.18 us
    ppermute x49 -> x62, starting transfers between devices: 50.4 us -> 56 us  [swap(): return lax.ppermute(value, 'dp', pairs)]
  transfers between devices with their start and end apart: 50 -> 62, of which waited for: 23 -> 23; matrix products, arithmetic and copies ran while one was open for 0% -> 1% of each run, Pallas kernels for 36% -> 43%
where the time goes in v2:
time: 235 us; the launch traced here: 231 us
  Pallas kernels  104 us (44%)
  waiting for transfers between devices  58.6 us (25%)
  starting transfers between devices  56 us (24%)
  local copies, waits for them, and re-layouts  10.4 us (4%)
    pallas_call x51, Pallas kernels, __call__(): pl.pallas_call(run, out_shape=tuple(outs if last else [pltpu.VMEM(o.shape...  104 us
    ppermute x62, waiting for transfers between devices, swap(): return lax.ppermute(value, 'dp', pairs)  58.6 us
    ppermute x62, starting transfers between devices, swap(): return lax.ppermute(value, 'dp', pairs)  56 us
    unnamed x125, local copies, waits for them, and re-layouts  8.18 us
  transfers between devices with their start and end apart: 62, of which 23 were waited for; matrix products, arithmetic and copies ran while one was open for 1% of the time, Pallas kernels for 43%

profile of v2, /device:TPU:0, one launch (start us, length us, event | category | flops | bytes accessed | tf_op | source)
XLA Modules:
  0.0 230.9 jit_solution(3391032650182258940)
XLA Ops:
  2.2 1.6 shard_map.280
  4.4 1.1 collective-permute-done.refs_2_
  6.1 3.0 %collective-permute-start.1 = (bf16[48,1664]{1,0:T(8,128)(2,1)S(1)}, bf16[48,1664]{1,0:T(8,128)(2,1)S(1)}, u32[]{:S(2)}, u32[]{:S(2)}) collective-permute-start(bf16[48,1664]{1,0:T(8,128)(2,1)S(1)} %get-tuple-element.118), channel_id=1, source_target_pairs={{0,8},{1,9},{2,10},{3,11},{4,12},{5,13},{6,14},{7,15},{8,0},{9,1},... | collective-permute-start | bytes 479240 | tf_op jit(solution)/shard_map/ppermute | solution.py:106
  9.1 2.6 %collective-permute-start.2 = (bf16[48,1664]{1,0:T(8,128)(2,1)S(1)}, bf16[48,1664]{1,0:T(8,128)(2,1)S(1)}, u32[]{:S(2)}, u32[]{:S(2)}) collective-permute-start(bf16[48,1664]{1,0:T(8,128)(2,1)S(1)} %get-tuple-element.118), channel_id=1, source_target_pairs={{0,16},{1,17},{2,18},{3,19},{4,20},{5,21},{6,22},{7,23},{8,24},{9,... | collective-permute-start | bytes 479240 | tf_op jit(solution)/shard_map/ppermute | solution.py:106
  11.7 1.7 collective-permute-start.4
  13.5 1.5 collective-permute-start.5
  16.0 3.9 %collective-permute-done.5.refs_3_.refs_7_ = bf16[48,2304]{1,0:T(8,128)(2,1)S(1)} collective-permute-done((bf16[48,2304]{1,0:T(8,128)(2,1)S(1)}, bf16[48,2304]{1,0:T(8,128)(2,1)S(1)}, u32[]{:S(2)}, u32[]{:S(2)}) %collective-permute-start.5) | collective-permute-done | bytes 221216 | tf_op jit(solution)/shard_map/ppermute | solution.py:106
  20.7 3.2 %collective-permute-done.2.refs_1_ = bf16[48,1664]{1,0:T(8,128)(2,1)S(1)} collective-permute-done((bf16[48,1664]{1,0:T(8,128)(2,1)S(1)}, bf16[48,1664]{1,0:T(8,128)(2,1)S(1)}, u32[]{:S(2)}, u32[]{:S(2)}) %collective-permute-start.2) | collective-permute-done | bytes 159776 | tf_op jit(solution)/shard_map/ppermute | solution.py:106
  23.9 1.6 collective-permute-start.6
  25.5 1.5 collective-permute-start.7
  27.0 3.9 %collective-permute-start.8 = (bf16[48,1536]{1,0:T(8,128)(2,1)S(1)}, bf16[48,1536]{1,0:T(8,128)(2,1)S(1)}, u32[]{:S(2)}, u32[]{:S(2)}) collective-permute-start(bf16[48,1536]{1,0:T(8,128)(2,1)S(1)} %get-tuple-element.121.refs_2_.refs_0_), channel_id=1, source_target_pairs={{0,16},{1,17},{2,18},{3,19},{4,20},{5,21},{6,22},{7,23},{8,24},{9,... | collective-permute-start | bytes 442376 | tf_op jit(solution)/shard_map/ppermute | solution.py:106
  31.4 5.1 %collective-permute-done.8.refs_4_.refs_1_.refs_0_ = bf16[48,1536]{1,0:T(8,128)(2,1)S(1)} collective-permute-done((bf16[48,1536]{1,0:T(8,128)(2,1)S(1)}, bf16[48,1536]{1,0:T(8,128)(2,1)S(1)}, u32[]{:S(2)}, u32[]{:S(2)}) %collective-permute-start.8) | collective-permute-done | bytes 147488 | tf_op jit(solution)/shard_map/ppermute | solution.py:106
  37.2 1.6 collective-permute-start.9
  39.9 4.0 %collective-permute-done.11.refs_6_ = bf16[2,48,896]{2,1,0:T(8,128)(2,1)S(1)} collective-permute-done((bf16[2,48,896]{2,1,0:T(8,128)(2,1)S(1)}, bf16[2,48,896]{2,1,0:T(8,128)(2,1)S(1)}, u32[]{:S(2)}, u32[]{:S(2)}) %collective-permute-start.11) | collective-permute-done | bytes 172064 | tf_op jit(solution)/shard_map/ppermute | solution.py:106
  43.9 3.7 %collective-permute-done.10.refs_4_ = bf16[6,48,768]{2,1,0:T(8,128)(2,1)S(1)} collective-permute-done((bf16[6,48,768]{2,1,0:T(8,128)(2,1)S(1)}, bf16[6,48,768]{2,1,0:T(8,128)(2,1)S(1)}, u32[]{:S(2)}, u32[]{:S(2)}) %collective-permute-start.10) | collective-permute-done | bytes 442400 | tf_op jit(solution)/shard_map/ppermute | solution.py:106
  47.6 3.7 %collective-permute-done.9.refs_2_ = bf16[6,48,896]{2,1,0:T(8,128)(2,1)S(1)} collective-permute-done((bf16[6,48,896]{2,1,0:T(8,128)(2,1)S(1)}, bf16[6,48,896]{2,1,0:T(8,128)(2,1)S(1)}, u32[]{:S(2)}, u32[]{:S(2)}) %collective-permute-start.9) | collective-permute-done | bytes 516128 | tf_op jit(solution)/shard_map/ppermute | solution.py:106
  51.2 1.4 shard_map.287.refs_2_.refs_4_.refs_3_.refs_11_
  52.7 4.4 %shard_map.288 = (bf16[640,768]{1,0:T(8,128)(2,1)S(1)}, bf16[640,1152]{1,0:T(8,128)(2,1)S(1)}, f32[16,768]{1,0:T(8,128)S(1)}) custom-call(s32[2]{0:T(128)S(1)} %pad_add_fusion.refs_0_, bf16[640,768]{1,0:T(8,128)(2,1)S(1)} %bitcast.23, bf16[768,1664]{1,0:T(8,128)(2,1)S(1)} %shard_map.287.refs_2_.refs_4_.refs_3_.refs_11_, ...), custom_call_target="tpu_custom_call" | custom-call | flops 18919999488 | bytes 6045696 | tf_op jit(solution)/shard_map/pallas_call | solution.py:70
  57.1 4.3 %shard_map.289.refs_2_.refs_7_ = bf16[640,384]{1,0:T(8,128)(2,1)S(1)} custom-call(s32[2]{0:T(128)S(1)} %copy-done.36, bf16[640,1152]{1,0:T(8,128)(2,1)S(1)} %get-tuple-element.131.refs_1_, f32[16,768]{1,0:T(8,128)S(1)} %get-tuple-element.130.refs_2_.refs_4_.refs_1_.refs_3_), custom_call_target="tpu_custom_call" | custom-call | flops 18919999488 | bytes 1966080 | tf_op jit(solution)/shard_map/pallas_call | solution.py:70
  63.5 2.3 shard_map.292
  65.8 4.4 %collective-permute-done.18.refs_1_ = bf16[3,48,768]{2,1,0:T(8,128)(2,1)S(1)} collective-permute-done((bf16[3,48,768]{2,1,0:T(8,128)(2,1)S(1)}, bf16[3,48,768]{2,1,0:T(8,128)(2,1)S(1)}, u32[]{:S(2)}, u32[]{:S(2)}) %collective-permute-start.18) | collective-permute-done | bytes 221216 | tf_op jit(solution)/shard_map/ppermute | solution.py:106
  71.7 1.1 collective-permute-start.22
  72.8 1.5 collective-permute-start.23
  74.2 4.3 %shard_map.295.refs_8_.refs_3_ = bf16[640,384]{1,0:T(8,128)(2,1)S(1)} custom-call(s32[2]{0:T(128)S(1)} %copy-done.36, bf16[640,1152]{1,0:T(8,128)(2,1)S(1)} %get-tuple-element.135.refs_1_, bf16[3,48,768]{2,1,0:T(8,128)(2,1)S(1)} %get-tuple-element.139.refs_2_.refs_0_), custom_call_target="tpu_custom_call" | custom-call | flops 18919999488 | bytes 1966080 | tf_op jit(solution)/shard_map/pallas_call | solution.py:70
  79.7 10.3 %collective-permute-done.23.refs_3_ = bf16[3,48,768]{2,1,0:T(8,128)(2,1)S(1)} collective-permute-done((bf16[3,48,768]{2,1,0:T(8,128)(2,1)S(1)}, bf16[3,48,768]{2,1,0:T(8,128)(2,1)S(1)}, u32[]{:S(2)}, u32[]{:S(2)}) %collective-permute-start.23) | collective-permute-done | bytes 221216 | tf_op jit(solution)/shard_map/ppermute | solution.py:106
  90.2 4.2 %shard_map.297 = (f32[640,768]{1,0:T(8,128)S(1)}, bf16[640,768]{1,0:T(8,128)(2,1)}) custom-call(bf16[640,768]{1,0:T(8,128)(2,1)S(1)} %bitcast.24, f32[16,768]{1,0:T(8,128)S(1)} %get-tuple-element.130.refs_2_.refs_4_.refs_1_.refs_3_, bf16[640,384]{1,0:T(8,128)(2,1)S(1)} %copy-done.47, bf16[640,384]{1,0:T(8,128)(2,1)S(1)} %shard_map.295.refs_8_.refs_3_, ...), custom_call_target="tpu_custom_call" | custom-call | flops 15840000000 | bytes 10076160 | tf_op jit(solution)/shard_map/pallas_call | solution.py:70
  94.5 1.6 shard_map.298.refs_3_.refs_4_.refs_5_
  96.8 1.3 collective-permute-start.28
  98.1 4.7 %shard_map.299 = (bf16[640,1536]{1,0:T(8,128)(2,1)S(1)}, bf16[640,1536]{1,0:T(8,128)(2,1)S(1)}) custom-call(s32[2]{0:T(128)S(1)} %pad_add_fusion.refs_0_, bf16[640,768]{1,0:T(8,128)(2,1)} %get-tuple-element.144.refs_5_.refs_1_, f32[1,3072]{1,0:T(1,128)S(1)} %get-tuple-element.137.refs_8_.refs_2_, bf16[768,1536]{1,0:T(8,128)(2,1)S(1)} %shard_map.298.refs_3_.refs_4_.refs_5_, ...), custom_call_target="tpu_custom_call" | custom-call | flops 16280000512 | bytes 7286784 | tf_op jit(solution)/shard_map/pallas_call | solution.py:70
  102.8 5.4 %shard_map.300 = (bf16[640,1536]{1,0:T(8,128)(2,1)S(1)}, bf16[640,1536]{1,0:T(8,128)(2,1)S(1)}) custom-call(s32[2]{0:T(128)S(1)} %pad_add_fusion.refs_0_, bf16[640,768]{1,0:T(8,128)(2,1)} %get-tuple-element.144.refs_5_.refs_1_, f32[1,3072]{1,0:T(1,128)S(1)} %get-tuple-element.137.refs_8_.refs_2_, ...), custom_call_target="tpu_custom_call" | custom-call | flops 16280000512 | bytes 7286784 | tf_op jit(solution)/shard_map/pallas_call | solution.py:70
  108.8 3.1 %collective-permute-done.27.refs_2_ = bf16[8,48,768]{2,1,0:T(8,128)(2,1)S(1)} collective-permute-done((bf16[8,48,768]{2,1,0:T(8,128)(2,1)S(1)}, bf16[8,48,768]{2,1,0:T(8,128)(2,1)S(1)}, u32[]{:S(2)}, u32[]{:S(2)}) %collective-permute-start.27) | collective-permute-done | bytes 589856 | tf_op jit(solution)/shard_map/ppermute | solution.py:106
  112.2 1.2 shard_map.301.refs_5_.refs_4_
  113.5 5.4 %shard_map.302 = (bf16[8,48,768]{2,1,0:T(8,128)(2,1)S(1)}, bf16[8,48,768]{2,1,0:T(8,128)(2,1)S(1)}, bf16[8,48,768]{2,1,0:T(8,128)(2,1)S(1)}, bf16[8,48,768]{2,1,0:T(8,128)(2,1)S(1)}) custom-call(s32[2]{0:T(128)S(1)} %pad_add_fusion.refs_0_, bf16[640,768]{1,0:T(8,128)(2,1)S(1)} %copy-done.16, bf16[640,768]{1,0:T(8,128)(2,1)S(1)} %copy-done.18, ...), custom_call_target="tpu_custom_call" | custom-call | flops 26400000000 | bytes 8257536 | tf_op jit(solution)/shard_map/pallas_call | solution.py:70
  118.9 1.6 collective-permute-start.34
  120.5 1.3 collective-permute-start.35
  121.8 4.8 %shard_map.303 = (bf16[640,1536]{1,0:T(8,128)(2,1)S(1)}, bf16[640,1536]{1,0:T(8,128)(2,1)S(1)}, f32[1,3072]{1,0:T(1,128)S(1)}) custom-call(s32[2]{0:T(128)S(1)} %pad_add_fusion.refs_0_, bf16[640,768]{1,0:T(8,128)(2,1)S(1)} %copy-done.16, bf16[640,1536]{1,0:T(8,128)(2,1)S(1)} %get-tuple-element.149.refs_2_, bf16[640,1536]{1,0:T(8,128)(2,1)S(1)} %get-tuple-element.150.refs_3_, ...), custom_call_target="tpu_custom_call" | custom-call | flops 21120000000 | bytes 13578240 | tf_op jit(solution)/shard_map/pallas_call | solution.py:70
  126.8 6.6 %shard_map.304 = (f32[640,768]{1,0:T(8,128)S(1)}, bf16[640,768]{1,0:T(8,128)(2,1)S(1)}, f32[8,768]{1,0:T(8,128)S(1)}) custom-call(bf16[640,768]{1,0:T(8,128)(2,1)S(1)} %copy-done.16, f32[640,768]{1,0:T(8,128)S(1)} %get-tuple-element.143.refs_1_.refs_0_, f32[16,768]{1,0:T(8,128)S(1)} %copy-done.50, bf16[640,1536]{1,0:T(8,128)(2,1)S(1)} %get-tuple-element.152.refs_3_, ...), custom_call_target="tpu_custom_call" | custom-call | flops 29040001024 | bytes 14622720 | tf_op jit(solution)/shard_map/pallas_call | solution.py:70
  133.9 8.2 %shard_map.305 = (bf16[640,1152]{1,0:T(8,128)(2,1)S(1)}, f32[8,384]{1,0:T(8,128)S(1)}) custom-call(s32[2]{0:T(128)S(1)} %copy-done.37, bf16[640,1152]{1,0:T(8,128)(2,1)S(1)} %copy-done.39, bf16[640,768]{1,0:T(8,128)(2,1)S(1)} %get-tuple-element.157.refs_2_.refs_5_, bf16[768,1664]{1,0:T(8,128)(2,1)S(1)} %copy-done.3, f32[8,768]{1,0:T(8,128)S(1)} %get-tuple-element.156.refs_4_), custom_call_target="tpu_custom_call" | custom-call | flops 36080001024 | bytes 6500352 | tf_op jit(solution)/shard_map/pallas_call | solution.py:70
  144.0 6.8 %shard_map.307 = (bf16[8,48,768]{2,1,0:T(8,128)(2,1)S(1)}, bf16[8,48,768]{2,1,0:T(8,128)(2,1)S(1)}, bf16[8,48,768]{2,1,0:T(8,128)(2,1)S(1)}, bf16[8,48,768]{2,1,0:T(8,128)(2,1)S(1)}) custom-call(s32[2]{0:T(128)S(1)} %pad_add_fusion.refs_0_, bf16[640,768]{1,0:T(8,128)(2,1)} %get-tuple-element.144.refs_5_.refs_1_, ...), custom_call_target="tpu_custom_call" | custom-call | flops 26400000000 | bytes 8257536 | tf_op jit(solution)/shard_map/pallas_call | solution.py:70
  150.8 1.3 collective-permute-start.36
  152.1 1.3 collective-permute-start.37
  153.5 8.2 %shard_map.308 = (bf16[640,1152]{1,0:T(8,128)(2,1)S(1)}, f32[8,384]{1,0:T(8,128)S(1)}) custom-call(s32[2]{0:T(128)S(1)} %copy-done.37, bf16[640,1152]{1,0:T(8,128)(2,1)S(1)} %copy-done.45, bf16[640,768]{1,0:T(8,128)(2,1)S(1)} %get-tuple-element.157.refs_2_.refs_5_, bf16[768,1664]{1,0:T(8,128)(2,1)S(1)} %copy-done.1, ...), custom_call_target="tpu_custom_call" | custom-call | flops 36080001024 | bytes 6500352 | tf_op jit(solution)/shard_map/pallas_call | solution.py:70
  161.9 1.0 copy-done.20
  163.5 6.2 %shard_map.310 = (bf16[8,48,768]{2,1,0:T(8,128)(2,1)}, bf16[8,48,768]{2,1,0:T(8,128)(2,1)S(1)}, bf16[8,48,768]{2,1,0:T(8,128)(2,1)}, bf16[8,48,768]{2,1,0:T(8,128)(2,1)S(1)}) custom-call(s32[2]{0:T(128)S(1)} %pad_add_fusion.refs_0_, bf16[640,768]{1,0:T(8,128)(2,1)S(1)} %copy-done.41, bf16[640,768]{1,0:T(8,128)(2,1)S(1)} %copy-done.20, ...), custom_call_target="tpu_custom_call" | custom-call | flops 26400000000 | bytes 10223616 | tf_op jit(solution)/shard_map/pallas_call | solution.py:70
  171.1 1.7 collective-permute-start.45
  173.3 1.1 collective-permute-start.43
  174.4 1.2 collective-permute-start.44
  175.7 6.6 %shard_map.312 = (bf16[640,768]{1,0:T(8,128)(2,1)S(1)}, f32[768,128]{1,0:T(8,128)S(1)}) custom-call(s32[2]{0:T(128)S(1)} %pad_add_fusion.refs_0_, bf16[640,768]{1,0:T(8,128)(2,1)S(1)} %bitcast.25, f32[640,768]{1,0:T(8,128)S(1)} %get-tuple-element.155.refs_2_, f32[16,768]{1,0:T(8,128)S(1)} %copy-done.51, f32[8,768]{1,0:T(8,128)S(1)} %copy-done.55, ...), custom_call_target="tpu_custom_call" | custom-call | flops 28600000512 | bytes 12521472 | tf_op jit(solution)/shard_map/pallas_call | solution.py:70
  182.3 4.2 %shard_map.313.refs_2_ = bf16[640,768]{1,0:T(8,128)(2,1)} custom-call(f32[640,768]{1,0:T(8,128)S(1)} %get-tuple-element.143.refs_1_.refs_0_, f32[16,768]{1,0:T(8,128)S(1)} %copy-done.51, bf16[640,1536]{1,0:T(8,128)(2,1)S(1)} %copy-done.43, bf16[640,1536]{1,0:T(8,128)(2,1)S(1)} %copy-done.10, bf16[768,1536]{1,0:T(8,128)(2,1)S(1)} %copy-done.6, ...), custom_call_target="tpu_custom_call" | custom-call | flops 18040000512 | bytes 11649024 | tf_op jit(solution)/shard_map/pallas_call | solution.py:70
  186.5 1.2 copy-done.32
  189.2 1.8 collective-permute-done.43.refs_0_
  192.5 1.6 shard_map.317
  195.7 1.1 collective-permute-start.49
  196.8 1.8 collective-permute-start.50
  199.6 4.0 %collective-permute-done.50.refs_1_ = bf16[2,48,1536]{2,1,0:T(8,128)(2,1)S(1)} collective-permute-done((bf16[2,48,1536]{2,1,0:T(8,128)(2,1)S(1)}, bf16[2,48,1536]{2,1,0:T(8,128)(2,1)S(1)}, u32[]{:S(2)}, u32[]{:S(2)}) %collective-permute-start.50) | collective-permute-done | bytes 294944 | tf_op jit(solution)/shard_map/ppermute | solution.py:106
  203.6 3.4 %collective-permute-start.55 = (bf16[48,1536]{1,0:T(8,128)(2,1)S(1)}, bf16[48,1536]{1,0:T(8,128)(2,1)S(1)}, u32[]{:S(2)}, u32[]{:S(2)}) collective-permute-start(bf16[48,1536]{1,0:T(8,128)(2,1)S(1)} %get-tuple-element.204), channel_id=1, source_target_pairs={{0,16},{1,17},{2,18},{3,19},{4,20},{5,21},{6,22},{7,23},{8,24},{9,... | collective-permute-start | bytes 442376 | tf_op jit(solution)/shard_map/ppermute | solution.py:106
  207.2 1.3 shard_map.323.refs_3_
  208.5 3.7 %collective-permute-done.55.refs_2_ = bf16[48,1536]{1,0:T(8,128)(2,1)S(1)} collective-permute-done((bf16[48,1536]{1,0:T(8,128)(2,1)S(1)}, bf16[48,1536]{1,0:T(8,128)(2,1)S(1)}, u32[]{:S(2)}, u32[]{:S(2)}) %collective-permute-start.55) | collective-permute-done | bytes 147488 | tf_op jit(solution)/shard_map/ppermute | solution.py:106
  214.9 1.9 collective-permute-start.52
  216.9 1.5 collective-permute-start.53
  218.4 1.4 collective-permute-start.54
  221.2 1.3 shard_map.327.refs_5_
  223.1 3.1 %collective-permute-done.53.refs_3_ = bf16[48,1536]{1,0:T(8,128)(2,1)S(1)} collective-permute-done((bf16[48,1536]{1,0:T(8,128)(2,1)S(1)}, bf16[48,1536]{1,0:T(8,128)(2,1)S(1)}, u32[]{:S(2)}, u32[]{:S(2)}) %collective-permute-start.53) | collective-permute-done | bytes 147488 | tf_op jit(solution)/shard_map/ppermute | solution.py:106
  229.4 1.3 shard_map.330
  (241 shorter events, 31.8 us)
Async XLA Ops:
  3.8 1.6 collective-permute-start
  6.1 14.5 %collective-permute-start.1 = (bf16[48,1664]{1,0:T(8,128)(2,1)S(1)}, bf16[48,1664]{1,0:T(8,128)(2,1)S(1)}, u32[]{:S(2)}, u32[]{:S(2)}) collective-permute-start(bf16[48,1664]{1,0:T(8,128)(2,1)S(1)} %get-tuple-element.118), channel_id=1, source_target_pairs={{0,8},{1,9},{2,10},{3,11},{4,12},{5,13},{6,14},{7,15},{8,0},{9,1},... | collective-permute-start | bytes 479240 | tf_op jit(solution)/shard_map/ppermute | solution.py:106
  9.1 14.7 %collective-permute-start.2 = (bf16[48,1664]{1,0:T(8,128)(2,1)S(1)}, bf16[48,1664]{1,0:T(8,128)(2,1)S(1)}, u32[]{:S(2)}, u32[]{:S(2)}) collective-permute-start(bf16[48,1664]{1,0:T(8,128)(2,1)S(1)} %get-tuple-element.118), channel_id=1, source_target_pairs={{0,16},{1,17},{2,18},{3,19},{4,20},{5,21},{6,22},{7,23},{8,24},{9,... | collective-permute-start | bytes 479240 | tf_op jit(solution)/shard_map/ppermute | solution.py:106
  11.7 12.2 %collective-permute-start.3 = (bf16[48,1664]{1,0:T(8,128)(2,1)S(1)}, bf16[48,1664]{1,0:T(8,128)(2,1)S(1)}, u32[]{:S(2)}, u32[]{:S(2)}) collective-permute-start(bf16[48,1664]{1,0:T(8,128)(2,1)S(1)} %get-tuple-element.118), channel_id=1, source_target_pairs={{0,24},{1,25},{2,26},{3,27},{4,28},{5,29},{6,30},{7,31},{8,16},{9,... | collective-permute-start | bytes 479240 | tf_op jit(solution)/shard_map/ppermute | solution.py:106
  11.7 8.2 %collective-permute-start.4 = (bf16[48,2432]{1,0:T(8,128)(2,1)S(1)}, bf16[48,2432]{1,0:T(8,128)(2,1)S(1)}, u32[]{:S(2)}, u32[]{:S(2)}) collective-permute-start(bf16[48,2432]{1,0:T(8,128)(2,1)S(1)} %get-tuple-element.119.refs_0_.refs_4_), channel_id=1, source_target_pairs={{0,4},{1,5},{2,6},{3,7},{4,0},{5,1},{6,2},{7,3},{8,12},{9,13},{10,... | collective-permute-start | bytes 700424 | tf_op jit(solution)/shard_map/ppermute | solution.py:106
  13.5 6.4 %collective-permute-start.5 = (bf16[48,2304]{1,0:T(8,128)(2,1)S(1)}, bf16[48,2304]{1,0:T(8,128)(2,1)S(1)}, u32[]{:S(2)}, u32[]{:S(2)}) collective-permute-start(bf16[48,2304]{1,0:T(8,128)(2,1)S(1)} %get-tuple-element.120.refs_2_.refs_6_), channel_id=1, source_target_pairs={{0,2},{1,3},{2,0},{3,1},{4,6},{5,7},{6,4},{7,5},{8,10},{9,11},{10,... | collective-permute-start | bytes 663560 | tf_op jit(solution)/shard_map/ppermute | solution.py:106
  23.9 13.2 %collective-permute-start.6 = (bf16[3,48,896]{2,1,0:T(8,128)(2,1)S(1)}, bf16[3,48,896]{2,1,0:T(8,128)(2,1)S(1)}, u32[]{:S(2)}, u32[]{:S(2)}) collective-permute-start(bf16[3,48,896]{2,1,0:T(8,128)(2,1)S(1)} %get-tuple-element.124.refs_0_), channel_id=1, source_target_pairs={{0,4},{1,5},{2,6},{3,7},{4,0},{5,1},{6,2},{7,3},{8,12},{9,13},{10,... | collective-permute-start | bytes 774152 | tf_op jit(solution)/shard_map/ppermute | solution.py:106
  25.5 11.6 %collective-permute-start.7 = (bf16[3,48,768]{2,1,0:T(8,128)(2,1)S(1)}, bf16[3,48,768]{2,1,0:T(8,128)(2,1)S(1)}, u32[]{:S(2)}, u32[]{:S(2)}) collective-permute-start(bf16[3,48,768]{2,1,0:T(8,128)(2,1)S(1)} %get-tuple-element.125.refs_2_.refs_5_), channel_id=1, source_target_pairs={{0,2},{1,3},{2,0},{3,1},{4,6},{5,7},{6,4},{7,5},{8,10},{9,11},{10,... | collective-permute-start | bytes 663560 | tf_op jit(solution)/shard_map/ppermute | solution.py:106
  27.0 9.6 %collective-permute-start.8 = (bf16[48,1536]{1,0:T(8,128)(2,1)S(1)}, bf16[48,1536]{1,0:T(8,128)(2,1)S(1)}, u32[]{:S(2)}, u32[]{:S(2)}) collective-permute-start(bf16[48,1536]{1,0:T(8,128)(2,1)S(1)} %get-tuple-element.121.refs_2_.refs_0_), channel_id=1, source_target_pairs={{0,16},{1,17},{2,18},{3,19},{4,20},{5,21},{6,22},{7,23},{8,24},{9,... | collective-permute-start | bytes 442376 | tf_op jit(solution)/shard_map/ppermute | solution.py:106
  30.9 21.8 %collective-permute-start.13 = (bf16[640,768]{1,0:T(8,128)(2,1)S(1)}, bf16[640,768]{1,0:T(8,128)(2,1)S(1)}, u32[]{:S(2)}, u32[]{:S(2)}) collective-permute-start(bf16[640,768]{1,0:T(8,128)(2,1)S(1)} %get-tuple-element.129.refs_1_.refs_0_), channel_id=1, source_target_pairs={{0,1},{1,0},{2,3},{3,2},{4,5},{5,4},{6,7},{7,6},{8,9},{9,8},{10,11... | collective-permute-start | bytes 2949128 | tf_op jit(solution)/shard_map/ppermute | solution.py:106
  30.9 8.3 %collective-permute-start.12 = (bf16[2,48,768]{2,1,0:T(8,128)(2,1)S(1)}, bf16[2,48,768]{2,1,0:T(8,128)(2,1)S(1)}, u32[]{:S(2)}, u32[]{:S(2)}) collective-permute-start(bf16[2,48,768]{2,1,0:T(8,128)(2,1)S(1)} %get-tuple-element.123.refs_3_.refs_7_), channel_id=1, source_target_pairs={{0,4},{1,5},{2,6},{3,7},{4,0},{5,1},{6,2},{7,3},{8,12},{9,13},{10,... | collective-permute-start | bytes 442376 | tf_op jit(solution)/shard_map/ppermute | solution.py:106
  36.6 7.3 %collective-permute-start.11 = (bf16[2,48,896]{2,1,0:T(8,128)(2,1)S(1)}, bf16[2,48,896]{2,1,0:T(8,128)(2,1)S(1)}, u32[]{:S(2)}, u32[]{:S(2)}) collective-permute-start(bf16[2,48,896]{2,1,0:T(8,128)(2,1)S(1)} %get-tuple-element.128.refs_5_), channel_id=1, source_target_pairs={{0,2},{1,3},{2,0},{3,1},{4,6},{5,7},{6,4},{7,5},{8,10},{9,11},{10,... | collective-permute-start | bytes 516104 | tf_op jit(solution)/shard_map/ppermute | solution.py:106
  37.2 14.0 %collective-permute-start.9 = (bf16[6,48,896]{2,1,0:T(8,128)(2,1)S(1)}, bf16[6,48,896]{2,1,0:T(8,128)(2,1)S(1)}, u32[]{:S(2)}, u32[]{:S(2)}) collective-permute-start(bf16[6,48,896]{2,1,0:T(8,128)(2,1)S(1)} %get-tuple-element.126.refs_1_), channel_id=1, source_target_pairs={{0,2},{1,3},{2,0},{3,1},{4,6},{5,7},{6,4},{7,5},{8,10},{9,11},{10,... | collective-permute-start | bytes 1548296 | tf_op jit(solution)/shard_map/ppermute | solution.py:106
  38.7 8.8 %collective-permute-start.10 = (bf16[6,48,768]{2,1,0:T(8,128)(2,1)S(1)}, bf16[6,48,768]{2,1,0:T(8,128)(2,1)S(1)}, u32[]{:S(2)}, u32[]{:S(2)}) collective-permute-start(bf16[6,48,768]{2,1,0:T(8,128)(2,1)S(1)} %get-tuple-element.127.refs_2_.refs_3_), channel_id=1, source_target_pairs={{0,4},{1,5},{2,6},{3,7},{4,0},{5,1},{6,2},{7,3},{8,12},{9,13},{10,... | collective-permute-start | bytes 1327112 | tf_op jit(solution)/shard_map/ppermute | solution.py:106
  39.3 22.2 %collective-permute-start.16 = (bf16[48,1536]{1,0:T(8,128)(2,1)S(1)}, bf16[48,1536]{1,0:T(8,128)(2,1)S(1)}, u32[]{:S(2)}, u32[]{:S(2)}) collective-permute-start(bf16[48,1536]{1,0:T(8,128)(2,1)S(1)} %get-tuple-element.133.refs_0_), channel_id=1, source_target_pairs={{0,16},{1,17},{2,18},{3,19},{4,20},{5,21},{6,22},{7,23},{8,24},{9,... | collective-permute-start | bytes 442376 | tf_op jit(solution)/shard_map/ppermute | solution.py:106
  43.9 18.4 %collective-permute-start.15 = (bf16[2,48,1536]{2,1,0:T(8,128)(2,1)S(1)}, bf16[2,48,1536]{2,1,0:T(8,128)(2,1)S(1)}, u32[]{:S(2)}, u32[]{:S(2)}) collective-permute-start(bf16[2,48,1536]{2,1,0:T(8,128)(2,1)S(1)} %shard_map.286.refs_9_), channel_id=1, source_target_pairs={{0,8},{1,9},{2,10},{3,11},{4,12},{5,13},{6,14},{7,15},{8,0},{9,1},... | collective-permute-start | bytes 884744 | tf_op jit(solution)/shard_map/ppermute | solution.py:106
  52.6 37.6 %copy-start = (bf16[768,1664]{1,0:T(8,128)(2,1)}, bf16[768,1664]{1,0:T(8,128)(2,1)S(1)}, u32[]{:S(2)}) copy-start(bf16[768,1664]{1,0:T(8,128)(2,1)S(1)} %shard_map.287.refs_2_.refs_4_.refs_3_.refs_11_) | copy-start | bytes 7667716
  52.6 10.8 %collective-permute-start.14 = (bf16[768,1664]{1,0:T(8,128)(2,1)S(1)}, bf16[768,1664]{1,0:T(8,128)(2,1)S(1)}, u32[]{:S(2)}, u32[]{:S(2)}) collective-permute-start(bf16[768,1664]{1,0:T(8,128)(2,1)S(1)} %shard_map.287.refs_2_.refs_4_.refs_3_.refs_11_), channel_id=1, source_target_pairs={{0,1},{1,0},{2,3},{3,2},{4,5},{5,4},{6,7},{7,6},{8,9},{9,8},{10,11... | collective-permute-start | bytes 7667720 | tf_op jit(solution)/shard_map/ppermute | solution.py:106
  57.1 33.0 %copy-start.49 = (f32[16,768]{1,0:T(8,128)}, f32[16,768]{1,0:T(8,128)S(1)}, u32[]{:S(2)}) copy-start(f32[16,768]{1,0:T(8,128)S(1)} %get-tuple-element.130.refs_2_.refs_4_.refs_1_.refs_3_) | copy-start | bytes 147460
  62.3 9.4 %collective-permute-start.17 = (bf16[2,48,1536]{2,1,0:T(8,128)(2,1)S(1)}, bf16[2,48,1536]{2,1,0:T(8,128)(2,1)S(1)}, u32[]{:S(2)}, u32[]{:S(2)}) collective-permute-start(bf16[2,48,1536]{2,1,0:T(8,128)(2,1)S(1)} %shard_map.290.refs_2_), channel_id=1, source_target_pairs={{0,8},{1,9},{2,10},{3,11},{4,12},{5,13},{6,14},{7,15},{8,0},{9,1},... | collective-permute-start | bytes 884744 | tf_op jit(solution)/shard_map/ppermute | solution.py:106
  62.3 7.9 %collective-permute-start.18 = (bf16[3,48,768]{2,1,0:T(8,128)(2,1)S(1)}, bf16[3,48,768]{2,1,0:T(8,128)(2,1)S(1)}, u32[]{:S(2)}, u32[]{:S(2)}) collective-permute-start(bf16[3,48,768]{2,1,0:T(8,128)(2,1)S(1)} %get-tuple-element.134.refs_5_.refs_0_), channel_id=1, source_target_pairs={{0,4},{1,5},{2,6},{3,7},{4,0},{5,1},{6,2},{7,3},{8,12},{9,13},{10,... | collective-permute-start | bytes 663560 | tf_op jit(solution)/shard_map/ppermute | solution.py:106
  62.9 7.5 %collective-permute-start.19 = (bf16[3,48,768]{2,1,0:T(8,128)(2,1)S(1)}, bf16[3,48,768]{2,1,0:T(8,128)(2,1)S(1)}, u32[]{:S(2)}, u32[]{:S(2)}) collective-permute-start(bf16[3,48,768]{2,1,0:T(8,128)(2,1)S(1)} %get-tuple-element.136.refs_2_), channel_id=1, source_target_pairs={{0,2},{1,3},{2,0},{3,1},{4,6},{5,7},{6,4},{7,5},{8,10},{9,11},{10,... | collective-permute-start | bytes 663560 | tf_op jit(solution)/shard_map/ppermute | solution.py:106
  70.5 23.9 %collective-permute-start.24 = (bf16[8,48,768]{2,1,0:T(8,128)(2,1)S(1)}, bf16[8,48,768]{2,1,0:T(8,128)(2,1)S(1)}, u32[]{:S(2)}, u32[]{:S(2)}) collective-permute-start(bf16[8,48,768]{2,1,0:T(8,128)(2,1)S(1)} %get-tuple-element.138.refs_2_.refs_1_), channel_id=1, source_target_pairs={{0,2},{1,3},{2,0},{3,1},{4,6},{5,7},{6,4},{7,5},{8,10},{9,11},{10,... | collective-permute-start | bytes 1769480 | tf_op jit(solution)/shard_map/ppermute | solution.py:106
  71.7 7.5 %collective-permute-start.22 = (bf16[3,48,768]{2,1,0:T(8,128)(2,1)S(1)}, bf16[3,48,768]{2,1,0:T(8,128)(2,1)S(1)}, u32[]{:S(2)}, u32[]{:S(2)}) collective-permute-start(bf16[3,48,768]{2,1,0:T(8,128)(2,1)S(1)} %get-tuple-element.139.refs_2_.refs_0_), channel_id=1, source_target_pairs={{0,4},{1,5},{2,6},{3,7},{4,0},{5,1},{6,2},{7,3},{8,12},{9,13},{10,... | collective-permute-start | bytes 663560 | tf_op jit(solution)/shard_map/ppermute | solution.py:106
  72.8 17.3 %collective-permute-start.23 = (bf16[3,48,768]{2,1,0:T(8,128)(2,1)S(1)}, bf16[3,48,768]{2,1,0:T(8,128)(2,1)S(1)}, u32[]{:S(2)}, u32[]{:S(2)}) collective-permute-start(bf16[3,48,768]{2,1,0:T(8,128)(2,1)S(1)} %get-tuple-element.141.refs_2_), channel_id=1, source_target_pairs={{0,2},{1,3},{2,0},{3,1},{4,6},{5,7},{6,4},{7,5},{8,10},{9,11},{10,... | collective-permute-start | bytes 663560 | tf_op jit(solution)/shard_map/ppermute | solution.py:106
  78.6 11.5 %collective-permute-start.20 = (bf16[640,384]{1,0:T(8,128)(2,1)S(1)}, bf16[640,384]{1,0:T(8,128)(2,1)S(1)}, u32[]{:S(2)}, u32[]{:S(2)}) collective-permute-start(bf16[640,384]{1,0:T(8,128)(2,1)S(1)} %shard_map.295.refs_8_.refs_3_), channel_id=1, source_target_pairs={{0,1},{1,0},{2,3},{3,2},{4,5},{5,4},{6,7},{7,6},{8,9},{9,8},{10,11... | collective-permute-start | bytes 1474568 | tf_op jit(solution)/shard_map/ppermute | solution.py:106
  78.7 11.5 %collective-permute-start.21 = (bf16[640,768]{1,0:T(8,128)(2,1)S(1)}, bf16[640,768]{1,0:T(8,128)(2,1)S(1)}, u32[]{:S(2)}, u32[]{:S(2)}) collective-permute-start(bf16[640,768]{1,0:T(8,128)(2,1)S(1)} %get-tuple-element.140), channel_id=1, source_target_pairs={{0,1},{1,0},{2,3},{3,2},{4,5},{5,4},{6,7},{7,6},{8,9},{9,8},{10,11... | collective-permute-start | bytes 2949128 | tf_op jit(solution)/shard_map/ppermute | solution.py:106
  79.2 15.4 %collective-permute-start.25 = (bf16[8,48,768]{2,1,0:T(8,128)(2,1)S(1)}, bf16[8,48,768]{2,1,0:T(8,128)(2,1)S(1)}, u32[]{:S(2)}, u32[]{:S(2)}) collective-permute-start(bf16[8,48,768]{2,1,0:T(8,128)(2,1)S(1)} %get-tuple-element.145.refs_3_), channel_id=1, source_target_pairs={{0,4},{1,5},{2,6},{3,7},{4,0},{5,1},{6,2},{7,3},{8,12},{9,13},{10,... | collective-permute-start | bytes 1769480 | tf_op jit(solution)/shard_map/ppermute | solution.py:106
  96.1 6.7 %collective-permute-start.26 = (bf16[768,1536]{1,0:T(8,128)(2,1)S(1)}, bf16[768,1536]{1,0:T(8,128)(2,1)S(1)}, u32[]{:S(2)}, u32[]{:S(2)}) collective-permute-start(bf16[768,1536]{1,0:T(8,128)(2,1)S(1)} %shard_map.298.refs_3_.refs_4_.refs_5_), channel_id=1, source_target_pairs={{0,1},{1,0},{2,3},{3,2},{4,5},{5,4},{6,7},{7,6},{8,9},{9,8},{10,11... | collective-permute-start | bytes 7077896 | tf_op jit(solution)/shard_map/ppermute | solution.py:106
  96.2 15.7 %collective-permute-start.27 = (bf16[8,48,768]{2,1,0:T(8,128)(2,1)S(1)}, bf16[8,48,768]{2,1,0:T(8,128)(2,1)S(1)}, u32[]{:S(2)}, u32[]{:S(2)}) collective-permute-start(bf16[8,48,768]{2,1,0:T(8,128)(2,1)S(1)} %get-tuple-element.142.refs_8_.refs_1_), channel_id=1, source_target_pairs={{0,2},{1,3},{2,0},{3,1},{4,6},{5,7},{6,4},{7,5},{8,10},{9,11},{10,... | collective-permute-start | bytes 1769480 | tf_op jit(solution)/shard_map/ppermute | solution.py:106
  96.8 15.4 %collective-permute-start.28 = (bf16[8,48,768]{2,1,0:T(8,128)(2,1)S(1)}, bf16[8,48,768]{2,1,0:T(8,128)(2,1)S(1)}, u32[]{:S(2)}, u32[]{:S(2)}) collective-permute-start(bf16[8,48,768]{2,1,0:T(8,128)(2,1)S(1)} %get-tuple-element.148.refs_3_), channel_id=1, source_target_pairs={{0,4},{1,5},{2,6},{3,7},{4,0},{5,1},{6,2},{7,3},{8,12},{9,13},{10,... | collective-permute-start | bytes 1769480 | tf_op jit(solution)/shard_map/ppermute | solution.py:106
  98.1 45.3 %collective-permute-start.32 = (bf16[640,768]{1,0:T(8,128)(2,1)}, bf16[640,768]{1,0:T(8,128)(2,1)}, u32[]{:S(2)}, u32[]{:S(2)}) collective-permute-start(bf16[640,768]{1,0:T(8,128)(2,1)} %get-tuple-element.144.refs_5_.refs_1_), channel_id=1, source_target_pairs={{0,1},{1,0},{2,3},{3,2},{4,5},{5,4},{6,7},{7,6},{8,9},{9,8},{10,11... | collective-permute-start | bytes 2949128 | tf_op jit(solution)/shard_map/ppermute | solution.py:106
  108.3 5.2 %collective-permute-start.30 = (bf16[640,1536]{1,0:T(8,128)(2,1)S(1)}, bf16[640,1536]{1,0:T(8,128)(2,1)S(1)}, u32[]{:S(2)}, u32[]{:S(2)}) collective-permute-start(bf16[640,1536]{1,0:T(8,128)(2,1)S(1)} %get-tuple-element.147.refs_5_.refs_3_), channel_id=1, source_target_pairs={{0,1},{1,0},{2,3},{3,2},{4,5},{5,4},{6,7},{7,6},{8,9},{9,8},{10,11... | collective-permute-start | bytes 5898248 | tf_op jit(solution)/shard_map/ppermute | solution.py:106
  113.4 8.4 %collective-permute-start.29 = (bf16[768,1536]{1,0:T(8,128)(2,1)S(1)}, bf16[768,1536]{1,0:T(8,128)(2,1)S(1)}, u32[]{:S(2)}, u32[]{:S(2)}) collective-permute-start(bf16[768,1536]{1,0:T(8,128)(2,1)S(1)} %shard_map.301.refs_5_.refs_4_), channel_id=1, source_target_pairs={{0,1},{1,0},{2,3},{3,2},{4,5},{5,4},{6,7},{7,6},{8,9},{9,8},{10,11... | collective-permute-start | bytes 7077896 | tf_op jit(solution)/shard_map/ppermute | solution.py:106
  118.9 23.3 %collective-permute-start.34 = (bf16[8,48,768]{2,1,0:T(8,128)(2,1)S(1)}, bf16[8,48,768]{2,1,0:T(8,128)(2,1)S(1)}, u32[]{:S(2)}, u32[]{:S(2)}) collective-permute-start(bf16[8,48,768]{2,1,0:T(8,128)(2,1)S(1)} %get-tuple-element.151.refs_6_), channel_id=1, source_target_pairs={{0,2},{1,3},{2,0},{3,1},{4,6},{5,7},{6,4},{7,5},{8,10},{9,11},{10,... | collective-permute-start | bytes 1769480 | tf_op jit(solution)/shard_map/ppermute | solution.py:106
  120.5 21.8 %collective-permute-start.35 = (bf16[8,48,768]{2,1,0:T(8,128)(2,1)S(1)}, bf16[8,48,768]{2,1,0:T(8,128)(2,1)S(1)}, u32[]{:S(2)}, u32[]{:S(2)}) collective-permute-start(bf16[8,48,768]{2,1,0:T(8,128)(2,1)S(1)} %get-tuple-element.159), channel_id=1, source_target_pairs={{0,4},{1,5},{2,6},{3,7},{4,0},{5,1},{6,2},{7,3},{8,12},{9,13},{10,... | collective-permute-start | bytes 1769480 | tf_op jit(solution)/shard_map/ppermute | solution.py:106
  126.6 17.4 %collective-permute-start.33 = (bf16[640,1536]{1,0:T(8,128)(2,1)S(1)}, bf16[640,1536]{1,0:T(8,128)(2,1)S(1)}, u32[]{:S(2)}, u32[]{:S(2)}) collective-permute-start(bf16[640,1536]{1,0:T(8,128)(2,1)S(1)} %get-tuple-element.153.refs_4_), channel_id=1, source_target_pairs={{0,1},{1,0},{2,3},{3,2},{4,5},{5,4},{6,7},{7,6},{8,9},{9,8},{10,11... | collective-permute-start | bytes 5898248 | tf_op jit(solution)/shard_map/ppermute | solution.py:106
  133.4 18.7 %collective-permute-start.31 = (bf16[640,768]{1,0:T(8,128)(2,1)S(1)}, bf16[640,768]{1,0:T(8,128)(2,1)S(1)}, u32[]{:S(2)}, u32[]{:S(2)}) collective-permute-start(bf16[640,768]{1,0:T(8,128)(2,1)S(1)} %get-tuple-element.157.refs_2_.refs_5_), channel_id=1, source_target_pairs={{0,1},{1,0},{2,3},{3,2},{4,5},{5,4},{6,7},{7,6},{8,9},{9,8},{10,11... | collective-permute-start | bytes 2949128 | tf_op jit(solution)/shard_map/ppermute | solution.py:106
  142.2 19.7 %collective-permute-start.38 = (bf16[640,1152]{1,0:T(8,128)(2,1)S(1)}, bf16[640,1152]{1,0:T(8,128)(2,1)S(1)}, u32[]{:S(2)}, u32[]{:S(2)}) collective-permute-start(bf16[640,1152]{1,0:T(8,128)(2,1)S(1)} %get-tuple-element.166.refs_10_), channel_id=1, source_target_pairs={{0,1},{1,0},{2,3},{3,2},{4,5},{5,4},{6,7},{7,6},{8,9},{9,8},{10,11... | collective-permute-start | bytes 4423688 | tf_op jit(solution)/shard_map/ppermute | solution.py:106
  142.8 18.9 %collective-permute-start.39 = (bf16[4,48,768]{2,1,0:T(8,128)(2,1)S(1)}, bf16[4,48,768]{2,1,0:T(8,128)(2,1)S(1)}, u32[]{:S(2)}, u32[]{:S(2)}) collective-permute-start(bf16[4,48,768]{2,1,0:T(8,128)(2,1)S(1)} %get-tuple-element.162.refs_5_), channel_id=1, source_target_pairs={{0,4},{1,5},{2,6},{3,7},{4,0},{5,1},{6,2},{7,3},{8,12},{9,13},{10,... | collective-permute-start | bytes 884744 | tf_op jit(solution)/shard_map/ppermute | solution.py:106
  143.5 18.2 %collective-permute-start.40 = (bf16[4,48,768]{2,1,0:T(8,128)(2,1)S(1)}, bf16[4,48,768]{2,1,0:T(8,128)(2,1)S(1)}, u32[]{:S(2)}, u32[]{:S(2)}) collective-permute-start(bf16[4,48,768]{2,1,0:T(8,128)(2,1)S(1)} %get-tuple-element.171), channel_id=1, source_target_pairs={{0,2},{1,3},{2,0},{3,1},{4,6},{5,7},{6,4},{7,5},{8,10},{9,11},{10,... | collective-permute-start | bytes 884744 | tf_op jit(solution)/shard_map/ppermute | solution.py:106
  150.8 22.1 %collective-permute-start.36 = (bf16[8,48,768]{2,1,0:T(8,128)(2,1)S(1)}, bf16[8,48,768]{2,1,0:T(8,128)(2,1)S(1)}, u32[]{:S(2)}, u32[]{:S(2)}) collective-permute-start(bf16[8,48,768]{2,1,0:T(8,128)(2,1)S(1)} %get-tuple-element.163.refs_5_), channel_id=1, source_target_pairs={{0,2},{1,3},{2,0},{3,1},{4,6},{5,7},{6,4},{7,5},{8,10},{9,11},{10,... | collective-permute-start | bytes 1769480 | tf_op jit(solution)/shard_map/ppermute | solution.py:106
  152.1 20.8 %collective-permute-start.37 = (bf16[8,48,768]{2,1,0:T(8,128)(2,1)S(1)}, bf16[8,48,768]{2,1,0:T(8,128)(2,1)S(1)}, u32[]{:S(2)}, u32[]{:S(2)}) collective-permute-start(bf16[8,48,768]{2,1,0:T(8,128)(2,1)S(1)} %get-tuple-element.168), channel_id=1, source_target_pairs={{0,4},{1,5},{2,6},{3,7},{4,0},{5,1},{6,2},{7,3},{8,12},{9,13},{10,... | collective-permute-start | bytes 1769480 | tf_op jit(solution)/shard_map/ppermute | solution.py:106
  169.7 22.9 %collective-permute-start.41 = (bf16[8,48,768]{2,1,0:T(8,128)(2,1)}, bf16[8,48,768]{2,1,0:T(8,128)(2,1)}, u32[]{:S(2)}, u32[]{:S(2)}) collective-permute-start(bf16[8,48,768]{2,1,0:T(8,128)(2,1)} %get-tuple-element.174.refs_4_), channel_id=1, source_target_pairs={{0,2},{1,3},{2,0},{3,1},{4,6},{5,7},{6,4},{7,5},{8,10},{9,11},{10,... | collective-permute-start | bytes 1769480 | tf_op jit(solution)/shard_map/ppermute | solution.py:106
  170.5 22.1 %collective-permute-start.42 = (bf16[8,48,768]{2,1,0:T(8,128)(2,1)}, bf16[8,48,768]{2,1,0:T(8,128)(2,1)}, u32[]{:S(2)}, u32[]{:S(2)}) collective-permute-start(bf16[8,48,768]{2,1,0:T(8,128)(2,1)} %get-tuple-element.179), channel_id=1, source_target_pairs={{0,4},{1,5},{2,6},{3,7},{4,0},{5,1},{6,2},{7,3},{8,12},{9,13},{10,... | collective-permute-start | bytes 1769480 | tf_op jit(solution)/shard_map/ppermute | solution.py:106
  171.1 15.4 %collective-permute-start.45 = (bf16[2,48,1536]{2,1,0:T(8,128)(2,1)S(1)}, bf16[2,48,1536]{2,1,0:T(8,128)(2,1)S(1)}, u32[]{:S(2)}, u32[]{:S(2)}) collective-permute-start(bf16[2,48,1536]{2,1,0:T(8,128)(2,1)S(1)} %get-tuple-element.184), channel_id=1, source_target_pairs={{0,8},{1,9},{2,10},{3,11},{4,12},{5,13},{6,14},{7,15},{8,0},{9,1},... | collective-permute-start | bytes 884744 | tf_op jit(solution)/shard_map/ppermute | solution.py:106
  173.3 17.8 %collective-permute-start.43 = (bf16[4,48,768]{2,1,0:T(8,128)(2,1)S(1)}, bf16[4,48,768]{2,1,0:T(8,128)(2,1)S(1)}, u32[]{:S(2)}, u32[]{:S(2)}) collective-permute-start(bf16[4,48,768]{2,1,0:T(8,128)(2,1)S(1)} %get-tuple-element.175.refs_13_), channel_id=1, source_target_pairs={{0,4},{1,5},{2,6},{3,7},{4,0},{5,1},{6,2},{7,3},{8,12},{9,13},{10,... | collective-permute-start | bytes 884744 | tf_op jit(solution)/shard_map/ppermute | solution.py:106
  174.4 18.0 %collective-permute-start.44 = (bf16[4,48,768]{2,1,0:T(8,128)(2,1)S(1)}, bf16[4,48,768]{2,1,0:T(8,128)(2,1)S(1)}, u32[]{:S(2)}, u32[]{:S(2)}) collective-permute-start(bf16[4,48,768]{2,1,0:T(8,128)(2,1)S(1)} %get-tuple-element.182), channel_id=1, source_target_pairs={{0,2},{1,3},{2,0},{3,1},{4,6},{5,7},{6,4},{7,5},{8,10},{9,11},{10,... | collective-permute-start | bytes 884744 | tf_op jit(solution)/shard_map/ppermute | solution.py:106
  188.4 7.3 %collective-permute-start.48 = (f32[8,48,128]{2,1,0:T(8,128)S(1)}, f32[8,48,128]{2,1,0:T(8,128)S(1)}, u32[]{:S(2)}, u32[]{:S(2)}) collective-permute-start(f32[8,48,128]{2,1,0:T(8,128)S(1)} %get-tuple-element.186.refs_4_), channel_id=1, source_target_pairs={{0,2},{1,3},{2,0},{3,1},{4,6},{5,7},{6,4},{7,5},{8,10},{9,11},{10,... | collective-permute-start | bytes 589832 | tf_op jit(solution)/shard_map/ppermute | solution.py:106
  191.1 7.8 %collective-permute-start.51 = (bf16[48,1536]{1,0:T(8,128)(2,1)S(1)}, bf16[48,1536]{1,0:T(8,128)(2,1)S(1)}, u32[]{:S(2)}, u32[]{:S(2)}) collective-permute-start(bf16[48,1536]{1,0:T(8,128)(2,1)S(1)} %get-tuple-element.196), channel_id=1, source_target_pairs={{0,16},{1,17},{2,18},{3,19},{4,20},{5,21},{6,22},{7,23},{8,24},{9,... | collective-permute-start | bytes 442376 | tf_op jit(solution)/shard_map/ppermute | solution.py:106
  194.1 13.0 %collective-permute-start.46 = (bf16[4,48,768]{2,1,0:T(8,128)(2,1)S(1)}, bf16[4,48,768]{2,1,0:T(8,128)(2,1)S(1)}, u32[]{:S(2)}, u32[]{:S(2)}) collective-permute-start(bf16[4,48,768]{2,1,0:T(8,128)(2,1)S(1)} %get-tuple-element.188.refs_2_), channel_id=1, source_target_pairs={{0,4},{1,5},{2,6},{3,7},{4,0},{5,1},{6,2},{7,3},{8,12},{9,13},{10,... | collective-permute-start | bytes 884744 | tf_op jit(solution)/shard_map/ppermute | solution.py:106
  194.5 12.6 %collective-permute-start.47 = (bf16[4,48,768]{2,1,0:T(8,128)(2,1)S(1)}, bf16[4,48,768]{2,1,0:T(8,128)(2,1)S(1)}, u32[]{:S(2)}, u32[]{:S(2)}) collective-permute-start(bf16[4,48,768]{2,1,0:T(8,128)(2,1)S(1)} %get-tuple-element.190), channel_id=1, source_target_pairs={{0,2},{1,3},{2,0},{3,1},{4,6},{5,7},{6,4},{7,5},{8,10},{9,11},{10,... | collective-permute-start | bytes 884744 | tf_op jit(solution)/shard_map/ppermute | solution.py:106
  195.7 11.3 %collective-permute-start.49 = (f32[4,48,128]{2,1,0:T(8,128)S(1)}, f32[4,48,128]{2,1,0:T(8,128)S(1)}, u32[]{:S(2)}, u32[]{:S(2)}) collective-permute-start(f32[4,48,128]{2,1,0:T(8,128)S(1)} %get-tuple-element.193.refs_3_), channel_id=1, source_target_pairs={{0,4},{1,5},{2,6},{3,7},{4,0},{5,1},{6,2},{7,3},{8,12},{9,13},{10,... | collective-permute-start | bytes 294920 | tf_op jit(solution)/shard_map/ppermute | solution.py:106
  196.8 6.7 %collective-permute-start.50 = (bf16[2,48,1536]{2,1,0:T(8,128)(2,1)S(1)}, bf16[2,48,1536]{2,1,0:T(8,128)(2,1)S(1)}, u32[]{:S(2)}, u32[]{:S(2)}) collective-permute-start(bf16[2,48,1536]{2,1,0:T(8,128)(2,1)S(1)} %get-tuple-element.195), channel_id=1, source_target_pairs={{0,8},{1,9},{2,10},{3,11},{4,12},{5,13},{6,14},{7,15},{8,0},{9,1},... | collective-permute-start | bytes 884744 | tf_op jit(solution)/shard_map/ppermute | solution.py:106
  199.5 7.8 %collective-permute-start.56 = (f32[24,1536]{1,0:T(8,128)S(1)}, f32[24,1536]{1,0:T(8,128)S(1)}, u32[]{:S(2)}, u32[]{:S(2)}) collective-permute-start(f32[24,1536]{1,0:T(8,128)S(1)} %get-tuple-element.205), channel_id=1, source_target_pairs={{0,1},{1,0},{2,3},{3,2},{4,5},{5,4},{6,7},{7,6},{8,9},{9,8},{10,11... | collective-permute-start | bytes 442376 | tf_op jit(solution)/shard_map/ppermute | solution.py:106
  203.6 8.6 %collective-permute-start.55 = (bf16[48,1536]{1,0:T(8,128)(2,1)S(1)}, bf16[48,1536]{1,0:T(8,128)(2,1)S(1)}, u32[]{:S(2)}, u32[]{:S(2)}) collective-permute-start(bf16[48,1536]{1,0:T(8,128)(2,1)S(1)} %get-tuple-element.204), channel_id=1, source_target_pairs={{0,16},{1,17},{2,18},{3,19},{4,20},{5,21},{6,22},{7,23},{8,24},{9,... | collective-permute-start | bytes 442376 | tf_op jit(solution)/shard_map/ppermute | solution.py:106
  207.0 6.8 %collective-permute-start.58 = (f32[2,48,128]{2,1,0:T(8,128)S(1)}, f32[2,48,128]{2,1,0:T(8,128)S(1)}, u32[]{:S(2)}, u32[]{:S(2)}) collective-permute-start(f32[2,48,128]{2,1,0:T(8,128)S(1)} %get-tuple-element.199.refs_4_), channel_id=1, source_target_pairs={{0,16},{1,17},{2,18},{3,19},{4,20},{5,21},{6,22},{7,23},{8,24},{9,... | collective-permute-start | bytes 147464 | tf_op jit(solution)/shard_map/ppermute | solution.py:106
  213.8 6.0 %collective-permute-start.59 = (f32[1,48,128]{2,1,0:T(8,128)S(1)}, f32[1,48,128]{2,1,0:T(8,128)S(1)}, u32[]{:S(2)}, u32[]{:S(2)}) collective-permute-start(f32[1,48,128]{2,1,0:T(8,128)S(1)} %get-tuple-element.209.refs_3_), channel_id=1, source_target_pairs={{0,8},{1,9},{2,10},{3,11},{4,12},{5,13},{6,14},{7,15},{8,0},{9,1},... | collective-permute-start | bytes 73736 | tf_op jit(solution)/shard_map/ppermute | solution.py:106
  214.9 8.2 %collective-permute-start.52 = (bf16[48,1536]{1,0:T(8,128)(2,1)S(1)}, bf16[48,1536]{1,0:T(8,128)(2,1)S(1)}, u32[]{:S(2)}, u32[]{:S(2)}) collective-permute-start(bf16[48,1536]{1,0:T(8,128)(2,1)S(1)} %get-tuple-element.201), channel_id=1, source_target_pairs={{0,8},{1,9},{2,10},{3,11},{4,12},{5,13},{6,14},{7,15},{8,0},{9,1},... | collective-permute-start | bytes 442376 | tf_op jit(solution)/shard_map/ppermute | solution.py:106
  216.9 9.4 %collective-permute-start.53 = (bf16[48,1536]{1,0:T(8,128)(2,1)S(1)}, bf16[48,1536]{1,0:T(8,128)(2,1)S(1)}, u32[]{:S(2)}, u32[]{:S(2)}) collective-permute-start(bf16[48,1536]{1,0:T(8,128)(2,1)S(1)} %get-tuple-element.202), channel_id=1, source_target_pairs={{0,16},{1,17},{2,18},{3,19},{4,20},{5,21},{6,22},{7,23},{8,24},{9,... | collective-permute-start | bytes 442376 | tf_op jit(solution)/shard_map/ppermute | solution.py:106
  218.4 7.9 %collective-permute-start.54 = (bf16[48,1536]{1,0:T(8,128)(2,1)S(1)}, bf16[48,1536]{1,0:T(8,128)(2,1)S(1)}, u32[]{:S(2)}, u32[]{:S(2)}) collective-permute-start(bf16[48,1536]{1,0:T(8,128)(2,1)S(1)} %get-tuple-element.203), channel_id=1, source_target_pairs={{0,24},{1,25},{2,26},{3,27},{4,28},{5,29},{6,30},{7,31},{8,16},{9,... | collective-permute-start | bytes 442376 | tf_op jit(solution)/shard_map/ppermute | solution.py:106
  219.8 1.4 collective-permute-start.57
  220.4 7.6 %collective-permute-start.61 = (f32[24,128]{1,0:T(8,128)S(1)}, f32[24,128]{1,0:T(8,128)S(1)}, u32[]{:S(2)}, u32[]{:S(2)}) collective-permute-start(f32[24,128]{1,0:T(8,128)S(1)} %get-tuple-element.214), channel_id=1, source_target_pairs={{0,1},{1,0},{2,3},{3,2},{4,5},{5,4},{6,7},{7,6},{8,9},{9,8},{10,11... | collective-permute-start | bytes 36872 | tf_op jit(solution)/shard_map/ppermute | solution.py:106
  227.9 1.5 collective-permute-start.60
  (60 other events, 356.9 us)
